TPU v7x, 32 devices: a whole 2x2x4 slice. The times are simulated.
32 devices in a mesh: groups: 2 (over y), frag: 4 (over z), grid: 2 (over x), sub: 2 (over core).
Axes of the slice: x: 2, y: 2, z: 4, core: 2. Of those that a mesh axis runs over, the one named last changes fastest.
Arguments:
- density: bfloat16 [16, 384, 384], P(('groups', 'frag')), parts along dimension 0, may hold values from -6 to 6
- basis_size: int32 [8], replicated, may hold values from 192 to 384
- coupling: bfloat16 [256, 384, 384], P(('groups', 'frag', 'grid', 'sub')), parts along dimension 0, may hold values from -0.3125 to 0.3125
- pair_first: int32 [128], P(('frag', 'grid', 'sub')), may hold values from 0 to 7, as said below
- pair_second: int32 [128], P(('frag', 'grid', 'sub')), may hold values from 0 to 7, as said below
- dimer_count: int32 [16], P(('frag', 'grid', 'sub')), may hold values from 4 to 8, as said below
- source_coords: float32 [16, 3, 384], P(('groups', 'frag')), parts along dimension 0, may hold values from 0 to 16
- grid_region: int32 [8, 512], P(('grid', 'sub')), may hold values from 0 to 7
Outputs:
- new_density: bfloat16 [16, 384, 384], P(('groups', 'frag'), ('grid', 'sub')), parts along dimension 0
- potential: float32 [16, 512], P(('groups', 'grid', 'sub'), 'frag'), parts along dimension 0
There are 2 independent parts, one for each index of `groups`. A program takes and returns all parts, laid end to end along the dimension named above; an argument that names none is the same for every part. Nothing has to cross between parts.
Inputs may be any that keep to these rules, and one draw needn't show every extreme that they name: `pair_first`: slot s belongs to owner s // 8; its first fragment is one of the 2 fragments t * 2 to t * 2 + 1 with t = (s // 8) // 4. `pair_second`: differs from the slot's first fragment and is one of the fragments of team t or team t + 1, t as for pair_first. Only the first dimer_count[d] slots of owner d are dimers; some owner has 8.
All inputs are finite; a program needn't handle non-finite values.
Results may differ from a plain program's by a relative error of at most 0.0051.
Values may be sent and summed in bfloat16 or wider, within the bound.
No kernel may reach another device: no remote copies, remote signals or barrier semaphores. Data moves between devices by JAX's collectives and lax.ppermute only.
A program may use at most 192 MiB of HBM per device.

v0:
```python
import jax
import jax.numpy as jnp
from jax import lax
from jax.sharding import PartitionSpec as P


def passed_along(value, axis, steps):
    count = lax.axis_size(axis)
    initial, last = (max(0, -steps), min(count, count - steps))
    return lax.ppermute(value, axis, [(source, source + steps) for source in range(initial, last)])


def per_device(
    density, basis_size, coupling, pair_first, pair_second, dimer_count, source_coords, grid_region
):
    frag_dev = density.shape[0]
    nbasis = density.shape[1]
    team_size = lax.axis_size("grid") * lax.axis_size("sub")
    row_share = nbasis // team_size
    team_index = lax.axis_index("frag")
    base = team_index * frag_dev
    member_index = lax.axis_index(("grid", "sub"))
    index_nb = jnp.arange(nbasis, dtype=jnp.int32)
    sizes_own = lax.dynamic_slice_in_dim(basis_size, base, frag_dev)
    live_rows = (index_nb[None, :] < sizes_own[:, None]).astype(jnp.float32)
    mask_own = live_rows[:, :, None] * live_rows[:, None, :]
    masked_own = (density.astype(jnp.float32) * mask_own).astype(jnp.bfloat16)
    row_start = member_index * row_share
    following = passed_along(masked_own, "frag", -1)
    stacked = jnp.concatenate([masked_own, following], axis=0)
    first_local = pair_first - base
    second_local = pair_second - base

    def one_slot(slot, totals):
        factor = coupling[slot]
        first_id = first_local[slot]
        second_id = second_local[slot]
        left_part = jnp.dot(factor, stacked[second_id], preferred_element_type=jnp.float32).astype(
            jnp.bfloat16
        )
        corr_first = jnp.dot(left_part, factor.T, preferred_element_type=jnp.float32)
        right_part = lax.dot_general(
            factor, stacked[first_id], (((0,), (0,)), ((), ())), preferred_element_type=jnp.float32
        ).astype(jnp.bfloat16)
        corr_second = jnp.dot(right_part, factor, preferred_element_type=jnp.float32)
        return totals.at[first_id].add(corr_first).at[second_id].add(corr_second)

    totals = lax.fori_loop(
        0, dimer_count[0], one_slot, jnp.zeros((2 * frag_dev, nbasis, nbasis), jnp.float32)
    )
    summed = lax.psum_scatter(totals, ("grid", "sub"), scatter_dimension=1, tiled=True)
    incoming = passed_along(summed[frag_dev:], "frag", 1)
    correction = summed[:frag_dev] + incoming
    own_rows = lax.dynamic_slice_in_dim(masked_own, row_start, row_share, 1).astype(jnp.float32)
    mask_rows = lax.dynamic_slice_in_dim(mask_own, row_start, row_share, 1)
    new_density = (own_rows + correction * mask_rows).astype(jnp.bfloat16)
    charge = jnp.diagonal(masked_own.astype(jnp.float32), axis1=1, axis2=2)
    pts_rows = grid_region.shape[0]
    total_cols = grid_region.shape[1]
    block_cols = total_cols // 8
    row_ids = member_index * pts_rows + jnp.arange(pts_rows, dtype=jnp.int32)

    def block_partial(block_id):
        cols = block_id * block_cols + jnp.arange(block_cols, dtype=jnp.int32)
        point_x = 0.25 * jnp.broadcast_to(row_ids[:, None], (pts_rows, block_cols)).astype(
            jnp.float32
        )
        point_y = 0.25 * jnp.broadcast_to((cols // 64)[None, :], (pts_rows, block_cols)).astype(
            jnp.float32
        )
        point_z = 0.25 * jnp.broadcast_to((cols % 64)[None, :], (pts_rows, block_cols)).astype(
            jnp.float32
        )
        region = lax.dynamic_slice_in_dim(grid_region, block_id * block_cols, block_cols, 1)
        total = jnp.zeros((pts_rows, block_cols), jnp.float32)
        for member in range(frag_dev):
            where_src = source_coords[member]
            dist_sq = (
                (point_x[..., None] - where_src[0]) ** 2
                + (point_y[..., None] - where_src[1]) ** 2
                + (point_z[..., None] - where_src[2]) ** 2
            )
            contrib = jnp.sum(charge[member] / jnp.sqrt(dist_sq + 1.0), axis=-1)
            total = total + jnp.where(region != base + member, contrib, 0.0)
        return total

    blocks = lax.map(block_partial, jnp.arange(8, dtype=jnp.int32))
    partial_sum = jnp.transpose(blocks, (1, 0, 2)).reshape(pts_rows, total_cols)
    summed_grid = lax.psum_scatter(partial_sum, "frag", scatter_dimension=1, tiled=True)
    scale = 8.0 / jnp.sqrt(jnp.float32(frag_dev * lax.axis_size("frag") * nbasis))
    return (new_density, summed_grid * scale)


def solution(mesh):
    placed = (
        P(("groups", "frag"), None, None),
        P(),
        P(("groups", "frag", "grid", "sub"), None, None),
        P(("frag", "grid", "sub")),
        P(("frag", "grid", "sub")),
        P(("frag", "grid", "sub")),
        P(("groups", "frag"), None, None),
        P(("grid", "sub"), None),
    )
    return jax.shard_map(
        per_device,
        mesh=mesh,
        in_specs=placed,
        out_specs=(
            P(("groups", "frag"), ("grid", "sub"), None),
            P(("groups", "grid", "sub"), "frag"),
        ),
        check_vma=False,
    )
```

profile of v0, /device:TPU:0, one launch (start us, length us, event | category | flops | bytes accessed | tf_op | source)
XLA Modules:
  0.0 214.5 jit_solution(9970458294209246573)
XLA Ops:
  8.9 2.3 %broadcast_multiply_fusion = (f32[2,384,384]{2,1,0:T(8,128)}, bf16[2,384,384]{2,1,0:T(8,128)(2,1)S(1)}) fusion(f32[2,384]{1,0:T(2,128)S(1)} %compare_convert_fusion, bf16[2,384,384]{2,1,0:T(8,128)(2,1)} %param.16), kind=kLoop, calls=%fused_computation.55 | loop fusion | flops 1179648 | bytes 2362368 | tf_op jit(solution)/shard_map/mul | solution.py:26
  11.2 1.3 collective-permute-start
  12.5 16.9 %collective-permute-done = bf16[2,384,384]{2,1,0:T(8,128)(2,1)S(1)} collective-permute-done((bf16[2,384,384]{2,1,0:T(8,128)(2,1)S(1)}, bf16[2,384,384]{2,1,0:T(8,128)(2,1)S(1)}, u32[]{:S(2)}, u32[]{:S(2)}) %collective-permute-start) | collective-permute-done | bytes 589856 | tf_op jit(solution)/shard_map/ppermute | solution.py:10
  29.8 69.4 %while.25 = (s32[]{:T(128)}, f32[4,384,384]{2,1,0:T(8,128)S(1)}, s32[]{:T(128)}, s32[8]{0:T(128)S(1)}, bf16[8,384,384]{2,1,0:T(8,128)(2,1)}, /*index=5*/s32[8]{0...) while((s32[]{:T(128)}, f32[4,384,384]{2,1,0:T(8,128)S(1)}, ...), condition=%wide.region_3.0_spmd, body=%wide.region_0.0_spmd.sunk | while | flops 453869632 | bytes 4134165 | solution.py:48
  35.8 0.8 and_reduce_fusion.3
  36.6 2.2 %fusion.52 = f32[4,384,384]{2,1,0:T(8,128)S(1)} fusion(f32[4,384,384]{2,1,0:T(8,128)S(1)} %get-tuple-element.457, s32[]{:T(128)} %select_n.108, bf16[4,384,384]{2,1,0:T(8,128)(2,1)S(1)} %get-tuple-element.475, s32[]{:T(128)} %select_n.109, pred[]{:T(512)} %get-tuple-element.420, bf16[8,384,384]{2,1,0:T(8,128)(2,1)} %get-tuple-element.473, ...), kind=kOutput, calls=%fused_computation.6.clone.1 | convolution fusion | flops 226934784 | bytes 2066944 | tf_op jit(solution)/shard_map/while/body/dot_general | solution.py:41
  38.8 2.4 %fusion.53 = f32[4,384,384]{2,1,0:T(8,128)S(1)} fusion(f32[4,384,384]{2,1,0:T(8,128)S(1)} %fusion.52, s32[]{:T(128)} %select_n.109, bf16[4,384,384]{2,1,0:T(8,128)(2,1)S(1)} %get-tuple-element.475, s32[]{:T(128)} %select_n.108, pred[]{:T(512)} %get-tuple-element.421, bf16[8,384,384]{2,1,0:T(8,128)(2,1)} %get-tuple-element.473, s32[]{:T(128)S(6)} %select_n.107), kind=kOutput, calls=%fused_computation.9.clone.1 | convolution fusion | flops 226934784 | bytes 2066944 | tf_op jit(solution)/shard_map/while/body/dot_general | solution.py:45
  47.2 0.8 and_reduce_fusion.3
  48.0 2.2 %fusion.52 = f32[4,384,384]{2,1,0:T(8,128)S(1)} fusion(f32[4,384,384]{2,1,0:T(8,128)S(1)} %get-tuple-element.457, s32[]{:T(128)} %select_n.108, bf16[4,384,384]{2,1,0:T(8,128)(2,1)S(1)} %get-tuple-element.475, s32[]{:T(128)} %select_n.109, pred[]{:T(512)} %get-tuple-element.420, bf16[8,384,384]{2,1,0:T(8,128)(2,1)} %get-tuple-element.473, ...), kind=kOutput, calls=%fused_computation.6.clone.1 | convolution fusion | flops 226934784 | bytes 2066944 | tf_op jit(solution)/shard_map/while/body/dot_general | solution.py:41
  50.3 2.4 %fusion.53 = f32[4,384,384]{2,1,0:T(8,128)S(1)} fusion(f32[4,384,384]{2,1,0:T(8,128)S(1)} %fusion.52, s32[]{:T(128)} %select_n.109, bf16[4,384,384]{2,1,0:T(8,128)(2,1)S(1)} %get-tuple-element.475, s32[]{:T(128)} %select_n.108, pred[]{:T(512)} %get-tuple-element.421, bf16[8,384,384]{2,1,0:T(8,128)(2,1)} %get-tuple-element.473, s32[]{:T(128)S(6)} %select_n.107), kind=kOutput, calls=%fused_computation.9.clone.1 | convolution fusion | flops 226934784 | bytes 2066944 | tf_op jit(solution)/shard_map/while/body/dot_general | solution.py:45
  58.7 0.8 and_reduce_fusion.3
  59.4 2.2 %fusion.52 = f32[4,384,384]{2,1,0:T(8,128)S(1)} fusion(f32[4,384,384]{2,1,0:T(8,128)S(1)} %get-tuple-element.457, s32[]{:T(128)} %select_n.108, bf16[4,384,384]{2,1,0:T(8,128)(2,1)S(1)} %get-tuple-element.475, s32[]{:T(128)} %select_n.109, pred[]{:T(512)} %get-tuple-element.420, bf16[8,384,384]{2,1,0:T(8,128)(2,1)} %get-tuple-element.473, ...), kind=kOutput, calls=%fused_computation.6.clone.1 | convolution fusion | flops 226934784 | bytes 2066944 | tf_op jit(solution)/shard_map/while/body/dot_general | solution.py:41
  61.7 2.4 %fusion.53 = f32[4,384,384]{2,1,0:T(8,128)S(1)} fusion(f32[4,384,384]{2,1,0:T(8,128)S(1)} %fusion.52, s32[]{:T(128)} %select_n.109, bf16[4,384,384]{2,1,0:T(8,128)(2,1)S(1)} %get-tuple-element.475, s32[]{:T(128)} %select_n.108, pred[]{:T(512)} %get-tuple-element.421, bf16[8,384,384]{2,1,0:T(8,128)(2,1)} %get-tuple-element.473, s32[]{:T(128)S(6)} %select_n.107), kind=kOutput, calls=%fused_computation.9.clone.1 | convolution fusion | flops 226934784 | bytes 2066944 | tf_op jit(solution)/shard_map/while/body/dot_general | solution.py:45
  70.1 0.8 and_reduce_fusion.3
  70.9 2.2 %fusion.52 = f32[4,384,384]{2,1,0:T(8,128)S(1)} fusion(f32[4,384,384]{2,1,0:T(8,128)S(1)} %get-tuple-element.457, s32[]{:T(128)} %select_n.108, bf16[4,384,384]{2,1,0:T(8,128)(2,1)S(1)} %get-tuple-element.475, s32[]{:T(128)} %select_n.109, pred[]{:T(512)} %get-tuple-element.420, bf16[8,384,384]{2,1,0:T(8,128)(2,1)} %get-tuple-element.473, ...), kind=kOutput, calls=%fused_computation.6.clone.1 | convolution fusion | flops 226934784 | bytes 2066944 | tf_op jit(solution)/shard_map/while/body/dot_general | solution.py:41
  73.1 2.4 %fusion.53 = f32[4,384,384]{2,1,0:T(8,128)S(1)} fusion(f32[4,384,384]{2,1,0:T(8,128)S(1)} %fusion.52, s32[]{:T(128)} %select_n.109, bf16[4,384,384]{2,1,0:T(8,128)(2,1)S(1)} %get-tuple-element.475, s32[]{:T(128)} %select_n.108, pred[]{:T(512)} %get-tuple-element.421, bf16[8,384,384]{2,1,0:T(8,128)(2,1)} %get-tuple-element.473, s32[]{:T(128)S(6)} %select_n.107), kind=kOutput, calls=%fused_computation.9.clone.1 | convolution fusion | flops 226934784 | bytes 2066944 | tf_op jit(solution)/shard_map/while/body/dot_general | solution.py:45
  81.5 0.8 and_reduce_fusion.3
  82.3 2.3 %fusion.52 = f32[4,384,384]{2,1,0:T(8,128)S(1)} fusion(f32[4,384,384]{2,1,0:T(8,128)S(1)} %get-tuple-element.457, s32[]{:T(128)} %select_n.108, bf16[4,384,384]{2,1,0:T(8,128)(2,1)S(1)} %get-tuple-element.475, s32[]{:T(128)} %select_n.109, pred[]{:T(512)} %get-tuple-element.420, bf16[8,384,384]{2,1,0:T(8,128)(2,1)} %get-tuple-element.473, ...), kind=kOutput, calls=%fused_computation.6.clone.1 | convolution fusion | flops 226934784 | bytes 2066944 | tf_op jit(solution)/shard_map/while/body/dot_general | solution.py:41
  84.6 2.4 %fusion.53 = f32[4,384,384]{2,1,0:T(8,128)S(1)} fusion(f32[4,384,384]{2,1,0:T(8,128)S(1)} %fusion.52, s32[]{:T(128)} %select_n.109, bf16[4,384,384]{2,1,0:T(8,128)(2,1)S(1)} %get-tuple-element.475, s32[]{:T(128)} %select_n.108, pred[]{:T(512)} %get-tuple-element.421, bf16[8,384,384]{2,1,0:T(8,128)(2,1)} %get-tuple-element.473, s32[]{:T(128)S(6)} %select_n.107), kind=kOutput, calls=%fused_computation.9.clone.1 | convolution fusion | flops 226934784 | bytes 2066944 | tf_op jit(solution)/shard_map/while/body/dot_general | solution.py:45
  93.8 2.3 %fusion.52 = f32[4,384,384]{2,1,0:T(8,128)S(1)} fusion(f32[4,384,384]{2,1,0:T(8,128)S(1)} %get-tuple-element.457, s32[]{:T(128)} %select_n.108, bf16[4,384,384]{2,1,0:T(8,128)(2,1)S(1)} %get-tuple-element.475, s32[]{:T(128)} %select_n.109, pred[]{:T(512)} %get-tuple-element.420, bf16[8,384,384]{2,1,0:T(8,128)(2,1)} %get-tuple-element.473, ...), kind=kOutput, calls=%fused_computation.6.clone.1 | convolution fusion | flops 226934784 | bytes 2066944 | tf_op jit(solution)/shard_map/while/body/dot_general | solution.py:41
  96.1 2.4 %fusion.53 = f32[4,384,384]{2,1,0:T(8,128)S(1)} fusion(f32[4,384,384]{2,1,0:T(8,128)S(1)} %fusion.52, s32[]{:T(128)} %select_n.109, bf16[4,384,384]{2,1,0:T(8,128)(2,1)S(1)} %get-tuple-element.475, s32[]{:T(128)} %select_n.108, pred[]{:T(512)} %get-tuple-element.421, bf16[8,384,384]{2,1,0:T(8,128)(2,1)} %get-tuple-element.473, s32[]{:T(128)S(6)} %select_n.107), kind=kOutput, calls=%fused_computation.9.clone.1 | convolution fusion | flops 226934784 | bytes 2066944 | tf_op jit(solution)/shard_map/while/body/dot_general | solution.py:45
  99.2 1.4 copy-done
  100.7 30.7 %copy.44 = f32[2,384,384]{0,2,1:T(8,128)} copy(bf16[2,384,384]{2,1,0:T(8,128)(2,1)S(1)} %copy-done.2) | data formatting | bytes 1769472 | tf_op jit(solution)/shard_map/convert_element_type | solution.py:57
  131.4 8.4 %gather_fusion = f32[384,2]{1,0:T(8,128)S(1)} fusion(f32[2,384,384]{0,2,1:T(8,128)} %copy.44, s32[384]{0:T(512)S(1)} %or_reduce_fusion), kind=kCustom, calls=%fused_computation | custom fusion | bytes 9216 | tf_op jit(solution)/shard_map/jit(diagonal)/gather | solution.py:57
  139.8 15.9 %reduce-scatter.5.cloned.1.call-done = f32[4,96,384]{2,1,0:T(8,128)} async-done(((f32[4,384,384]{2,1,0:T(8,128)}), f32[4,96,384]{2,1,0:T(8,128)}) %reduce-scatter.5.cloned.1.call-update) | async-done | bytes 589840 | tf_op jit(solution)/shard_map/reduce_scatter | solution.py:51
  155.7 1.1 slice.119
  156.7 10.7 %collective-permute-start.1 = (f32[2,96,384]{2,1,0:T(8,128)S(1)}, f32[2,96,384]{2,1,0:T(8,128)S(1)}, u32[]{:S(2)}, u32[]{:S(2)}) collective-permute-start(f32[2,96,384]{2,1,0:T(8,128)S(1)} %slice.119), channel_id=1, source_target_pairs={{0,4},{4,8},{8,12},{1,5},{5,9},{9,13},{2,6},{6,10},{10,14},{3,7},{... | collective-permute-start | bytes 884744 | tf_op jit(solution)/shard_map/ppermute | solution.py:10
  167.4 18.3 %while.26 = (s32[]{:T(128)}, f32[8,2,64]{2,1,0:T(2,128)S(1)}, s32[8]{0:T(128)S(1)}, s32[2,512]{1,0:T(2,128)}, s32[]{:T(128)}, /*index=5*/f32[2,384]{1,0:T(2,128)...) while((s32[]{:T(128)}, f32[8,2,64]{2,1,0:T(2,128)S(1)}, ...), condition=%wide.region_8.9_spmd.clone, body=%wide.region_5.8_spmd.clone.sunk | while | flops 1083276 | bytes 42719 | solution.py:87
  185.8 0.9 copy.49
  186.6 17.3 %reduce-scatter.7.cloned.1.call-done = f32[128,2]{1,0:T(8,128)} async-done(((f32[512,2]{1,0:T(8,128)}), f32[128,2]{1,0:T(8,128)}) %reduce-scatter.7.cloned.1.call-update) | async-done | bytes 1040
  203.9 0.9 copy.48
  205.4 1.7 fusion.35
  (99 shorter events, 24.2 us)
Async XLA Ops:
  8.0 4.5 %copy-start.7 = (s32[8]{0:T(128)S(1)}, s32[8]{0:T(128)}, u32[]{:S(2)}) copy-start(s32[8]{0:T(128)} %param.19) | copy-start | bytes 100
  8.0 4.5 %copy-start.6 = (s32[8]{0:T(128)S(1)}, s32[8]{0:T(128)}, u32[]{:S(2)}) copy-start(s32[8]{0:T(128)} %param.20) | copy-start | bytes 100
  8.0 147.7 %reduce-scatter.5.cloned.1.call-start = ((), (), s32[]{:S(2)}) async-start(), calls=%async_computation.2 | async-start | bytes 2949120 | tf_op jit(solution)/shard_map/reduce_scatter | solution.py:51
  11.2 18.4 %copy-start.1 = (bf16[2,384,384]{2,1,0:T(8,128)(2,1)}, bf16[2,384,384]{2,1,0:T(8,128)(2,1)S(1)}, u32[]{:S(2)}) copy-start(bf16[2,384,384]{2,1,0:T(8,128)(2,1)S(1)} %get-tuple-element.313) | copy-start | bytes 1769476
  11.2 18.2 %collective-permute-start = (bf16[2,384,384]{2,1,0:T(8,128)(2,1)S(1)}, bf16[2,384,384]{2,1,0:T(8,128)(2,1)S(1)}, u32[]{:S(2)}, u32[]{:S(2)}) collective-permute-start(bf16[2,384,384]{2,1,0:T(8,128)(2,1)S(1)} %get-tuple-element.313), channel_id=1, source_target_pairs={{4,0},{8,4},{12,8},{5,1},{9,5},{13,9},{6,2},{10,6},{14,10},{7,3},{... | collective-permute-start | bytes 1769480 | tf_op jit(solution)/shard_map/ppermute | solution.py:10
  12.5 17.2 %copy-start.5 = (s32[3]{0:T(128)S(1)}, s32[3]{0:T(128)}, u32[]{:S(2)}) copy-start(s32[3]{0:T(128)} %constant.137.clone.1) | copy-start | bytes 40
  99.1 1.4 copy-start
  99.2 1.5 copy-start.2
  100.6 103.3 %reduce-scatter.7.cloned.1.call-start = ((), (), s32[]{:S(2)}) async-start(), calls=%async_computation.3 | async-start | bytes 327680
  100.7 66.8 %copy-start.4 = (f32[2,3,384]{2,0,1:T(2,128)S(1)}, f32[2,3,384]{2,0,1:T(2,128)}, u32[]{:S(2)}) copy-start(f32[2,3,384]{2,0,1:T(2,128)} %param.22) | copy-start | bytes 27652
  155.7 49.7 %copy-start.3 = (f32[4,96,384]{2,1,0:T(8,128)S(1)}, f32[4,96,384]{2,1,0:T(8,128)}, u32[]{:S(2)}) copy-start(f32[4,96,384]{2,1,0:T(8,128)} %reduce-scatter.5.cloned.1.call-done) | copy-start | bytes 1769476
  156.7 48.7 %collective-permute-start.1 = (f32[2,96,384]{2,1,0:T(8,128)S(1)}, f32[2,96,384]{2,1,0:T(8,128)S(1)}, u32[]{:S(2)}, u32[]{:S(2)}) collective-permute-start(f32[2,96,384]{2,1,0:T(8,128)S(1)} %slice.119), channel_id=1, source_target_pairs={{0,4},{4,8},{8,12},{1,5},{5,9},{9,13},{2,6},{6,10},{10,14},{3,7},{... | collective-permute-start | bytes 884744 | tf_op jit(solution)/shard_map/ppermute | solution.py:10
Sparse Core Ops, SparseCore 0:
  100.7 54.9 reduce-scatter.4
Sparse Core Ops, SparseCore 1:
  186.7 17.1 reduce-scatter.6
where the time goes:
time: 216 us; the launch traced here: 215 us
  local copies, waits for them, and re-layouts  57.2 us (26%)
  waiting for transfers between devices  50.1 us (23%)
  loops' own time  33.9 us (16%)
  matrix products  27.8 us (13%)
  other arithmetic  18 us (8%)
  between operations  15.6 us (7%)
  starting transfers between devices  12 us (6%)
    convert_element_type x1, local copies, waits for them, and re-layouts, per_device(): charge = jnp.diagonal(masked_own.astype(jnp.float32), axis1=1, axis2=2)  30.7 us
    another operation x1, loops' own time, per_device(): lax.fori_loop(0, dimer_count[0], one_slot, jnp.zeros((2 * frag_dev, nbasi...  29.1 us
    unnamed x3, waiting for transfers between devices  17.3 us
    ppermute x2, waiting for transfers between devices, passed_along(): lax.ppermute(value, axis, [(source, source + steps) for source in range(i...  16.9 us
    reduce_scatter x1, waiting for transfers between devices, per_device(): lax.psum_scatter(totals, ('grid', 'sub'), scatter_dimension=1, tiled=True)  15.9 us
    dot_general x6, matrix products, one_slot(): jnp.dot(right_part, factor, preferred_element_type=jnp.float32)  14.3 us
    dot_general x6, matrix products, one_slot(): jnp.dot(left_part, factor.T, preferred_element_type=jnp.float32)  13.5 us
    ppermute x2, starting transfers between devices, passed_along(): lax.ppermute(value, axis, [(source, source + steps) for source in range(i...  11.9 us
  transfers between devices with their start and end apart: 4, of which 3 were waited for; matrix products, arithmetic and copies ran while one was open for 26% of the time, Pallas kernels for 0%

commit v1 on v0

v1 whole, which is shorter than its diff:
```python
import functools

import jax
import jax.numpy as jnp
from jax import lax
from jax.experimental import pallas as pl
from jax.experimental.pallas import tpu as pltpu
from jax.sharding import PartitionSpec as P

VMEM_LIMIT = 24 * 1024 * 1024


def live_square(values, size):
    rows = lax.broadcasted_iota(jnp.int32, values.shape, 0)
    cols = lax.broadcasted_iota(jnp.int32, values.shape, 1)
    return jnp.where((rows < size) & (cols < size), values, jnp.zeros_like(values))


def slot_ids(first_ref, second_ref, count_ref, slot, base, frag_dev):
    first = jnp.clip(first_ref[slot] - base, 0, frag_dev - 1)
    second = jnp.clip(second_ref[slot] - base, 0, 2 * frag_dev - 1)
    return first, second, slot < count_ref[0]


def right_kernel(
    size_ref, first_ref, second_ref, count_ref, density_ref, coupling_ref, coords_ref, region_ref,
    keep_ref, send_ref, own_ref, pot_ref,
    factor_ref, masked_ref, total_ref, sems,
):
    frag_dev, nbasis = density_ref.shape[0], density_ref.shape[1]
    slots = coupling_ref.shape[0]
    copies = [
        pltpu.make_async_copy(coupling_ref.at[s], factor_ref.at[s], sems.at[s]) for s in range(slots)
    ]
    for copy in copies:
        copy.start()
    team = lax.axis_index("frag")
    base = team * frag_dev
    for f in range(frag_dev):
        masked_ref[f] = live_square(density_ref[f].astype(jnp.float32), size_ref[base + f]).astype(
            jnp.bfloat16
        )
    total_ref[...] = jnp.zeros_like(total_ref)

    pts_rows = region_ref.shape[0]
    blocks, block_cols = pot_ref.shape[0], pot_ref.shape[2]
    member = lax.axis_index("grid") * lax.axis_size("sub") + lax.axis_index("sub")
    columns = []
    for f in range(frag_dev):
        diag = live_square(density_ref[f].astype(jnp.float32), size_ref[base + f])
        rows = lax.broadcasted_iota(jnp.int32, diag.shape, 0)
        cols = lax.broadcasted_iota(jnp.int32, diag.shape, 1)
        charge = jnp.sum(jnp.where(rows == cols, diag, 0.0), axis=1, keepdims=True)
        place = jnp.transpose(jnp.concatenate([coords_ref[f], jnp.zeros((5, nbasis), jnp.float32)]))
        columns.append((charge, place[:, 0:1], place[:, 1:2], place[:, 2:3]))
    lane = lax.broadcasted_iota(jnp.int32, (1, block_cols), 1)

    def one_block(step, carry):
        block = lax.rem(team + step, blocks)
        col = block * block_cols + lane
        point_y = 0.25 * (col // 64).astype(jnp.float32)
        point_z = 0.25 * (col % 64).astype(jnp.float32)
        start = pl.multiple_of(block * block_cols, block_cols)
        for r in range(pts_rows):
            point_x = 0.25 * (member * pts_rows + r).astype(jnp.float32)
            region = region_ref[r : r + 1, pl.ds(start, block_cols)]
            total = jnp.zeros((1, block_cols), jnp.float32)
            for f in range(frag_dev):
                charge, src_x, src_y, src_z = columns[f]
                dist_sq = (
                    (point_x - src_x) ** 2 + (point_y - src_y) ** 2 + (point_z - src_z) ** 2
                )
                value = jnp.sum(charge * lax.rsqrt(dist_sq + 1.0), axis=0, keepdims=True)
                total = total + jnp.where(region != base + f, value, 0.0)
            pot_ref[step, r : r + 1, :] = total
        return carry

    lax.fori_loop(0, blocks, one_block, 0)

    for s in range(slots):
        copies[s].wait()
        first, second, live = slot_ids(first_ref, second_ref, count_ref, s, base, frag_dev)
        factor = factor_ref[s]
        right = jnp.dot(factor.T, masked_ref[first], preferred_element_type=jnp.float32)
        corr = jnp.dot(right.astype(jnp.bfloat16), factor, preferred_element_type=jnp.float32)
        target = jnp.where(live, second, 2 * frag_dev)
        total_ref[target] = total_ref[target] + corr

    own_ref[...] = total_ref[:frag_dev]
    split_rows(total_ref, frag_dev, keep_ref, send_ref)


def split_rows(total_ref, start, keep_ref, send_ref):
    frag_dev, grid_size, share, _ = keep_ref.shape
    sub_size = lax.axis_size("sub")
    me = lax.axis_index("sub")
    for f in range(frag_dev):
        for g in range(grid_size):
            mine = pl.multiple_of((g * sub_size + me) * share, share)
            other = pl.multiple_of((g * sub_size + 1 - me) * share, share)
            keep_ref[f, g] = total_ref[start + f, pl.ds(mine, share), :].astype(keep_ref.dtype)
            send_ref[f, g] = total_ref[start + f, pl.ds(other, share), :].astype(send_ref.dtype)


def left_kernel(
    size_ref, first_ref, second_ref, count_ref, density_ref, mine_ref, other_ref, own_ref, coupling_ref,
    keep_ref, send_ref,
    factor_ref, masked_ref, total_ref, sems,
):
    frag_dev = density_ref.shape[0]
    slots = coupling_ref.shape[0]
    half = mine_ref.shape[0]
    copies = [
        pltpu.make_async_copy(coupling_ref.at[s], factor_ref.at[s], sems.at[s]) for s in range(slots)
    ]
    for copy in copies:
        copy.start()
    base = lax.axis_index("frag") * frag_dev
    me = lax.axis_index("sub")
    last = size_ref.shape[0] - 1

    def put(place, values):
        size = size_ref[jnp.minimum(base + place, last)]
        masked_ref[place] = live_square(values.astype(jnp.float32), size).astype(jnp.bfloat16)

    for f in range(frag_dev):
        put(f, density_ref[f])
    for f in range(half):
        put(frag_dev + me * half + f, mine_ref[f])
        put(frag_dev + (1 - me) * half + f, other_ref[f])
    total_ref[:frag_dev] = own_ref[...]
    total_ref[frag_dev] = jnp.zeros_like(total_ref[frag_dev])
    for s in range(slots):
        copies[s].wait()
        first, second, live = slot_ids(first_ref, second_ref, count_ref, s, base, frag_dev)
        factor = factor_ref[s]
        left = jnp.dot(factor, masked_ref[second], preferred_element_type=jnp.float32)
        corr = lax.dot_general(
            left.astype(jnp.bfloat16), factor, (((1,), (1,)), ((), ())), preferred_element_type=jnp.float32
        )
        target = jnp.where(live, first, frag_dev)
        total_ref[target] = total_ref[target] + corr
    split_rows(total_ref, 0, keep_ref, send_ref)


def shifted(value, axis, steps):
    count = lax.axis_size(axis)
    pairs = [(s, s + steps) for s in range(count) if 0 <= s + steps < count]
    return lax.ppermute(value, axis, pairs)


def turned(value, axis, steps):
    count = lax.axis_size(axis)
    return lax.ppermute(value, axis, [(s, (s + steps) % count) for s in range(count)])


def per_device(
    density, basis_size, coupling, pair_first, pair_second, dimer_count, source_coords, grid_region
):
    frag_dev, nbasis, _ = density.shape
    slots = coupling.shape[0]
    teams, grid_size, sub_size = (lax.axis_size(a) for a in ("frag", "grid", "sub"))
    assert sub_size == 2 and frag_dev % sub_size == 0 and teams & (teams - 1) == 0
    share = nbasis // (grid_size * sub_size)
    half = frag_dev // sub_size
    pts_rows, total_cols = grid_region.shape
    team, grid_at, sub_at = (lax.axis_index(a) for a in ("frag", "grid", "sub"))

    smem = pl.BlockSpec(memory_space=pltpu.SMEM)
    vmem = pl.BlockSpec(memory_space=pltpu.VMEM)
    anywhere = pl.BlockSpec(memory_space=pl.ANY)
    params = pltpu.CompilerParams(vmem_limit_bytes=VMEM_LIMIT)
    cost = pl.CostEstimate(
        flops=4 * slots * nbasis**3, bytes_accessed=2 * slots * nbasis * nbasis, transcendentals=0
    )

    def scratch(masks, totals):
        return [
            pltpu.VMEM((slots, nbasis, nbasis), jnp.bfloat16),
            pltpu.VMEM((masks, nbasis, nbasis), jnp.bfloat16),
            pltpu.VMEM((totals, nbasis, nbasis), jnp.float32),
            pltpu.SemaphoreType.DMA((slots,)),
        ]

    halves = (frag_dev, grid_size, share, nbasis)
    mine = shifted(lax.dynamic_slice_in_dim(density, sub_at * half, half), "frag", -1)
    next_keep, next_send, own_part, pot = pl.pallas_call(
        right_kernel,
        out_shape=(
            jax.ShapeDtypeStruct(halves, jnp.bfloat16),
            jax.ShapeDtypeStruct(halves, jnp.bfloat16),
            jax.ShapeDtypeStruct((frag_dev, nbasis, nbasis), jnp.float32),
            jax.ShapeDtypeStruct((teams, pts_rows, total_cols // teams), jnp.float32),
        ),
        in_specs=[smem] * 4 + [vmem, anywhere, vmem, vmem],
        out_specs=(vmem,) * 4,
        scratch_shapes=scratch(frag_dev, 2 * frag_dev + 1),
        compiler_params=params,
        cost_estimate=cost,
        name="right",
    )(basis_size, pair_first, pair_second, dimer_count, density, coupling, source_coords, grid_region)

    next_sum = (
        next_keep.astype(jnp.float32) + turned(next_send, "sub", 1).astype(jnp.float32)
    ).astype(jnp.bfloat16)
    from_before = shifted(next_sum, "frag", 1)

    other = turned(mine, "sub", 1)
    own_keep, own_send = pl.pallas_call(
        left_kernel,
        out_shape=(
            jax.ShapeDtypeStruct(halves, jnp.float32),
            jax.ShapeDtypeStruct(halves, jnp.bfloat16),
        ),
        in_specs=[smem] * 4 + [vmem] * 4 + [anywhere],
        out_specs=(vmem,) * 2,
        scratch_shapes=scratch(2 * frag_dev, frag_dev + 1),
        compiler_params=params,
        cost_estimate=cost,
        name="left",
    )(basis_size, pair_first, pair_second, dimer_count, density, mine, other, own_part, coupling)
    own_sum = own_keep + turned(own_send, "sub", 1).astype(jnp.float32) + from_before.astype(jnp.float32)

    correction = lax.dynamic_index_in_dim(own_sum, grid_at, 1, keepdims=False)
    for step in range(1, grid_size):
        part = lax.dynamic_index_in_dim(own_sum, (grid_at + step) % grid_size, 1, keepdims=False)
        correction = correction + turned(part.astype(jnp.bfloat16), "grid", step).astype(jnp.float32)

    row_start = (grid_at * sub_size + sub_at) * share
    sizes = lax.dynamic_slice_in_dim(basis_size, team * frag_dev, frag_dev)[:, None, None]
    own_rows = lax.dynamic_slice_in_dim(density, row_start, share, 1).astype(jnp.float32)
    live = (row_start + jnp.arange(share, dtype=jnp.int32)[None, :, None] < sizes) & (
        jnp.arange(nbasis, dtype=jnp.int32)[None, None, :] < sizes
    )
    new_density = jnp.where(live, own_rows + correction, 0.0).astype(jnp.bfloat16)

    while pot.shape[0] > 1:
        rest = pot.shape[0] // 2
        pot = pot[:rest] + turned(pot[rest:], "frag", rest)
    scale = 8.0 / jnp.sqrt(jnp.float32(frag_dev * teams * nbasis))
    return (new_density, pot[0] * scale)


def solution(mesh):
    placed = (
        P(("groups", "frag"), None, None),
        P(),
        P(("groups", "frag", "grid", "sub"), None, None),
        P(("frag", "grid", "sub")),
        P(("frag", "grid", "sub")),
        P(("frag", "grid", "sub")),
        P(("groups", "frag"), None, None),
        P(("grid", "sub"), None),
    )
    return jax.shard_map(
        per_device,
        mesh=mesh,
        in_specs=placed,
        out_specs=(
            P(("groups", "frag"), ("grid", "sub"), None),
            P(("groups", "grid", "sub"), "frag"),
        ),
        check_vma=False,
    )
```

time: 216 us -> 55.4 us (0.26)
  waiting for transfers between devices: 50.1 us -> 4.85 us
  local copies, waits for them, and re-layouts: 57.2 us -> 12.3 us
  loops' own time: 33.9 us -> 0 us
  matrix products: 27.8 us -> 0 us
  Pallas kernels: 0 us -> 17 us
  between operations: 15.6 us -> 1.4 us
  other arithmetic: 18 us -> 6.92 us
    another operation x2 -> x0, loops' own time: 33.9 us -> none  [the longest x1 29.1 us: per_device(): lax.fori_loop(0, dimer_count[0], one_slot, jnp.zeros((2 * frag_dev, nbasi...]
    convert_element_type x1, local copies, waits for them, and re-layouts: 30.7 us -> 0.03 us  [per_device(): part.astype(jnp.bfloat16)]
    dot_general x12 -> x0, matrix products: 27.8 us -> none  [the longest x6 14.3 us: one_slot(): jnp.dot(right_part, factor, preferred_element_type=jnp.float32)]
    unnamed x3 -> x0, waiting for transfers between devices: 17.3 us -> none
    pallas_call x0 -> x2, Pallas kernels: none -> 17 us  [the longest x1 9.68 us: per_device(): pl.pallas_call(right_kernel, out_shape=(jax.ShapeDtypeStruct(halves, jnp....]
    reduce_scatter x1 -> x0, waiting for transfers between devices: 15.9 us -> none  [per_device(): lax.psum_scatter(totals, ('grid', 'sub'), scatter_dimension=1, tiled=True)]
    ppermute x2 -> x8, waiting for transfers between devices: 16.9 us -> 4.85 us  [the longest x6 4.85 us: turned(): lax.ppermute(value, axis, [(s, (s + steps) % count) for s in range(count)])]
    dynamic_slice x21 -> x2, local copies, waits for them, and re-layouts: 13.2 us -> 2.28 us  [the longest x1 1.7 us: per_device(): lax.dynamic_slice_in_dim(density, sub_at * half, half)]
  transfers between devices with their start and end apart: 4 -> 8, of which waited for: 3 -> 3; matrix products, arithmetic and copies ran while one was open for 26% -> 13% of each run, Pallas kernels for 0% -> 31%
where the time goes in v1:
time: 55.4 us; the launch traced here: 54.8 us
  Pallas kernels  17 us (31%)
  starting transfers between devices  12.4 us (22%)
  local copies, waits for them, and re-layouts  12.3 us (22%)
  other arithmetic  6.92 us (12%)
  waiting for transfers between devices  4.85 us (9%)
  between operations  1.4 us (3%)
    pallas_call x1, Pallas kernels, per_device(): pl.pallas_call(right_kernel, out_shape=(jax.ShapeDtypeStruct(halves, jnp....  9.68 us
    unnamed x33, local copies, waits for them, and re-layouts  9.37 us
    pallas_call x1, Pallas kernels, per_device(): pl.pallas_call(left_kernel, out_shape=(jax.ShapeDtypeStruct(halves, jnp.f...  7.27 us
    ppermute x6, starting transfers between devices, turned(): lax.ppermute(value, axis, [(s, (s + steps) % count) for s in range(count)])  6.97 us
    ppermute x2, starting transfers between devices, shifted(): return lax.ppermute(value, axis, pairs)  5.48 us
    ppermute x6, waiting for transfers between devices, turned(): lax.ppermute(value, axis, [(s, (s + steps) % count) for s in range(count)])  4.85 us
    convert_element_type x1, other arithmetic, per_device(): next_sum = (next_keep.astype(jnp.float32) + turned(next_send, 'sub', 1).a...  1.77 us
    dynamic_slice x1, local copies, waits for them, and re-layouts, per_device(): lax.dynamic_slice_in_dim(density, sub_at * half, half)  1.7 us
  transfers between devices with their start and end apart: 8, of which 3 were waited for; matrix products, arithmetic and copies ran while one was open for 13% of the time, Pallas kernels for 31%

profile of v1, /device:TPU:0, one launch (start us, length us, event | category | flops | bytes accessed | tf_op | source)
XLA Modules:
  0.0 54.8 jit_solution(17154874248931550255)
XLA Ops:
  0.6 1.7 %constant_dynamic-slice_fusion = bf16[1,384,384]{2,1,0:T(8,128)(2,1)} fusion(bf16[2,384,384]{2,1,0:T(8,128)(2,1)} %density_ref.3, s32[]{:T(128)S(6)} %select_n.29), kind=kLoop, calls=%fused_computation.13 | loop fusion | bytes 589828 | tf_op jit(solution)/shard_map/dynamic_slice | solution.py:186
  2.3 1.3 %collective-permute-start = (bf16[1,384,384]{2,1,0:T(8,128)(2,1)}, bf16[1,384,384]{2,1,0:T(8,128)(2,1)S(1)}, u32[]{:S(2)}, u32[]{:S(2)}) collective-permute-start(bf16[1,384,384]{2,1,0:T(8,128)(2,1)} %constant_dynamic-slice_fusion), channel_id=1, source_target_pairs={{4,0},{8,4},{12,8},{5,1},{9,5},{13,9},{6,2},{10,6},{14,10},{7,3},{... | collective-permute-start | bytes 884744 | tf_op jit(solution)/shard_map/ppermute | solution.py:149
  4.3 0.7 %copy.10.coords_ref = f32[2,3,384]{2,1,0:T(4,128)S(1)} copy(f32[2,3,384]{2,0,1:T(2,128)} %param.14) | data formatting | bytes 18432 | tf_op args[6]
  5.0 1.1 %copy-done = bf16[2,384,384]{2,1,0:T(8,128)(2,1)S(1)} copy-done((bf16[2,384,384]{2,1,0:T(8,128)(2,1)S(1)}, bf16[2,384,384]{2,1,0:T(8,128)(2,1)}, u32[]{:S(2)}) %copy-start) | copy-done | bytes 589848
  6.0 1.7 %copy-done.2 = bf16[8,384,384]{2,1,0:T(8,128)(2,1)S(1)} copy-done((bf16[8,384,384]{2,1,0:T(8,128)(2,1)S(1)}, bf16[8,384,384]{2,1,0:T(8,128)(2,1)}, u32[]{:S(2)}) %copy-start.2) | copy-done | bytes 2359320
  7.7 0.7 %copy-done.6 = s32[2,512]{1,0:T(2,128)S(1)} copy-done((s32[2,512]{1,0:T(2,128)S(1)}, s32[2,512]{1,0:T(2,128)}, u32[]{:S(2)}) %copy-start.6) | copy-done | bytes 4120
  8.4 0.7 %copy-done.7 = s32[8]{0:T(128)S(1)} copy-done((s32[8]{0:T(128)S(1)}, s32[8]{0:T(128)}, u32[]{:S(2)}) %copy-start.7) | copy-done | bytes 56
  9.1 0.7 %copy-done.9 = s32[8]{0:T(128)S(1)} copy-done((s32[8]{0:T(128)S(1)}, s32[8]{0:T(128)}, u32[]{:S(2)}) %copy-start.9) | copy-done | bytes 56
  9.7 0.7 %copy-done.11 = s32[8]{0:T(128)S(1)} copy-done((s32[8]{0:T(128)S(1)}, s32[8]{0:T(128)}, u32[]{:S(2)}) %copy-start.11) | copy-done | bytes 56
  10.4 9.7 %right.1 = (bf16[2,2,96,384]{3,2,1,0:T(8,128)(2,1)S(1)}, bf16[2,2,96,384]{3,2,1,0:T(8,128)(2,1)}, f32[2,384,384]{2,1,0:T(8,128)S(1)}, f32[4,2,128]{2,1,0:T(2,128)S(1)}) custom-call(s32[8]{0:T(128)S(1)} %copy-done.7, s32[8]{0:T(128)S(1)} %copy-done.9, s32[8]{0:T(128)S(1)} %copy-done.11, s32[1]{0:T(128)S(6)} %copy.11.count_ref, ...), custom_call_target="tpu_custom_call" | custom-call | flops 1811939328 | bytes 2359296 | tf_op jit(solution)/shard_map/right/pallas_call | solution.py:187
  20.1 1.0 %copy-done.13 = f32[2,384,384]{2,1,0:T(8,128)} copy-done((f32[2,384,384]{2,1,0:T(8,128)}, f32[2,384,384]{2,1,0:T(8,128)S(1)}, u32[]{:S(2)}) %copy-start.13) | copy-done | bytes 1179672
  21.1 0.5 collective-permute-start.3
  21.6 0.6 %slice.13 = f32[2,2,128]{2,1,0:T(2,128)} slice(f32[4,2,128]{2,1,0:T(2,128)S(1)} %get-tuple-element.13), slice={[2:4], [0:2], [0:128]} | slice | bytes 4096 | tf_op jit(solution)/shard_map/slice | solution.py:239
  22.2 4.7 %collective-permute-start.6 = (f32[2,2,128]{2,1,0:T(2,128)}, f32[2,2,128]{2,1,0:T(2,128)}, u32[]{:S(2)}, u32[]{:S(2)}) collective-permute-start(f32[2,2,128]{2,1,0:T(2,128)} %slice.13), channel_id=1, source_target_pairs={{0,8},{4,12},{8,0},{12,4},{1,9},{5,13},{9,1},{13,5},{2,10},{6,14},... | collective-permute-start | bytes 6152 | tf_op jit(solution)/shard_map/ppermute | solution.py:154
  26.8 0.6 %dynamic_slice.16 = s32[2]{0:T(128)} dynamic-slice(s32[8]{0:T(128)S(1)} %copy-done.8, s32[]{:T(128)S(6)} %select_n.27), dynamic_slice_sizes={2} | dynamic-slice | bytes 20 | tf_op jit(solution)/shard_map/dynamic_slice | solution.py:230
  27.4 1.3 %iota_compare_fusion = pred[2,384]{1,0:T(4,128)(4,1)} fusion(s32[2]{0:T(128)} %dynamic_slice.16), kind=kLoop, calls=%fused_computation.8 | loop fusion | flops 768 | bytes 776 | tf_op jit(solution)/shard_map/lt | solution.py:233
  28.7 0.2 collective-permute-start.1
  28.9 1.8 %add_convert_fusion = bf16[2,2,96,384]{3,2,1,0:T(8,128)(2,1)} fusion(bf16[2,2,96,384]{3,2,1,0:T(8,128)(2,1)} %collective-permute-done.3, bf16[2,2,96,384]{3,2,1,0:T(8,128)(2,1)S(1)} %get-tuple-element.11), kind=kLoop, calls=%fused_computation.1 | loop fusion | flops 589824 | bytes 884736 | tf_op jit(solution)/shard_map/convert_element_type | solution.py:205
  30.7 4.2 %collective-permute-start.4 = (bf16[2,2,96,384]{3,2,1,0:T(8,128)(2,1)}, bf16[2,2,96,384]{3,2,1,0:T(8,128)(2,1)}, u32[]{:S(2)}, u32[]{:S(2)}) collective-permute-start(bf16[2,2,96,384]{3,2,1,0:T(8,128)(2,1)} %add_convert_fusion), channel_id=1, source_target_pairs={{0,4},{4,8},{8,12},{1,5},{5,9},{9,13},{2,6},{6,10},{10,14},{3,7},{... | collective-permute-start | bytes 884744 | tf_op jit(solution)/shard_map/ppermute | solution.py:149
  35.0 1.0 %copy-done.5 = bf16[1,384,384]{2,1,0:T(8,128)(2,1)S(1)} copy-done((bf16[1,384,384]{2,1,0:T(8,128)(2,1)S(1)}, bf16[1,384,384]{2,1,0:T(8,128)(2,1)}, u32[]{:S(2)}) %copy-start.5) | copy-done | bytes 294936
  35.9 1.3 %copy-done.14 = f32[2,384,384]{2,1,0:T(8,128)S(1)} copy-done((f32[2,384,384]{2,1,0:T(8,128)S(1)}, f32[2,384,384]{2,1,0:T(8,128)}, u32[]{:S(2)}) %copy-start.14) | copy-done | bytes 1179672
  37.2 7.3 %left.1 = (f32[2,2,96,384]{3,2,1,0:T(8,128)S(1)}, bf16[2,2,96,384]{3,2,1,0:T(8,128)(2,1)}) custom-call(s32[8]{0:T(128)S(1)} %copy-done.8, s32[8]{0:T(128)S(1)} %copy-done.10, s32[8]{0:T(128)S(1)} %copy-done.12, s32[1]{0:T(128)S(6)} %copy.11.count_ref, bf16[2,384,384]{2,1,0:T(8,128)(2,1)S(1)} %copy-done.1, bf16[1,384,384]{2,1,0:T(8,128)(2,1)S(1)} %copy-done.5, ...), custom_call_target="tpu_custom_call" | custom-call | flops 1811939328 | bytes 2359296 | tf_op jit(solution)/shard_map/left/pallas_call | solution.py:209
  44.5 0.1 collective-permute-start.2
  44.6 0.1 broadcast_compare_fusion
  44.6 0.7 %slice_add_fusion = f32[2,2,128]{2,1,0:T(2,128)S(1)} fusion(f32[2,2,128]{2,1,0:T(2,128)} %collective-permute-done.6, f32[4,2,128]{2,1,0:T(2,128)S(1)} %get-tuple-element.13), kind=kLoop, calls=%fused_computation.9 | loop fusion | flops 512 | bytes 6144 | tf_op jit(solution)/shard_map/add | solution.py:239
  45.3 1.0 %collective-permute-done.2 = bf16[2,2,96,384]{3,2,1,0:T(8,128)(2,1)S(1)} collective-permute-done((bf16[2,2,96,384]{3,2,1,0:T(8,128)(2,1)}, bf16[2,2,96,384]{3,2,1,0:T(8,128)(2,1)S(1)}, u32[]{:S(2)}, u32[]{:S(2)}) %collective-permute-start.2) | collective-permute-done | bytes 294944 | tf_op jit(solution)/shard_map/ppermute | solution.py:154
  46.3 1.1 %convert_add_fusion = f32[2,2,96,384]{3,2,1,0:T(8,128)S(1)} fusion(bf16[2,2,96,384]{3,2,1,0:T(8,128)(2,1)} %collective-permute-done.4, f32[2,2,96,384]{3,2,1,0:T(8,128)S(1)} %get-tuple-element.9, bf16[2,2,96,384]{3,2,1,0:T(8,128)(2,1)S(1)} %collective-permute-done.2), kind=kLoop, calls=%fused_computation | loop fusion | flops 589824 | bytes 1769472 | tf_op jit(solution)/shard_map/add | solution.py:222
  47.4 1.6 %collective-permute-start.5 = (bf16[2,96,384]{2,1,0:T(8,128)(2,1)S(1)}, bf16[2,96,384]{2,1,0:T(8,128)(2,1)S(1)}, u32[]{:S(2)}, u32[]{:S(2)}) collective-permute-start(bf16[2,96,384]{2,1,0:T(8,128)(2,1)S(1)} %fusion.3), channel_id=1, source_target_pairs={{0,2},{2,0},{1,3},{3,1},{4,6},{6,4},{5,7},{7,5},{8,10},{10,8},{9,1... | collective-permute-start | bytes 442376 | tf_op jit(solution)/shard_map/ppermute | solution.py:154
  49.0 1.7 %collective-permute-done.7 = f32[1,2,128]{2,1,0:T(2,128)S(1)} collective-permute-done((f32[1,2,128]{2,1,0:T(2,128)S(1)}, f32[1,2,128]{2,1,0:T(2,128)S(1)}, u32[]{:S(2)}, u32[]{:S(2)}) %collective-permute-start.7) | collective-permute-done | bytes 1056 | tf_op jit(solution)/shard_map/ppermute | solution.py:154
  50.7 0.6 %fusion.5 = f32[2,128]{1,0:T(2,128)} fusion(f32[1,2,128]{2,1,0:T(2,128)S(1)} %collective-permute-done.7, f32[2,2,128]{2,1,0:T(2,128)S(1)} %slice_add_fusion), kind=kLoop, calls=%fused_computation.12 | loop fusion | flops 512 | bytes 3072 | tf_op jit(solution)/shard_map/mul | solution.py:241
  51.2 2.1 %collective-permute-done.5 = bf16[2,96,384]{2,1,0:T(8,128)(2,1)S(1)} collective-permute-done((bf16[2,96,384]{2,1,0:T(8,128)(2,1)S(1)}, bf16[2,96,384]{2,1,0:T(8,128)(2,1)S(1)}, u32[]{:S(2)}, u32[]{:S(2)}) %collective-permute-start.5) | collective-permute-done | bytes 147488 | tf_op jit(solution)/shard_map/ppermute | solution.py:154
  53.4 1.5 %fusion.2 = bf16[2,96,384]{2,1,0:T(8,128)(2,1)} fusion(bf16[2,96,384]{2,1,0:T(8,128)(2,1)S(1)} %collective-permute-done.5, f32[2,2,96,384]{3,2,1,0:T(8,128)S(1)} %convert_add_fusion, s32[]{:T(128)S(6)} %select_n.30, bf16[2,384,384]{2,1,0:T(8,128)(2,1)S(1)} %copy-done.1, s32[]{:T(128)S(6)} %select_n.28, pred[2,384]{1,0:T(4,128)(4,1)} %iota_compare_fusion, ...), kind=kLoop, calls=%fused_computation.5 | loop fusion | flops 516096 | bytes 738248 | tf_op jit(solution)/shard_map/convert_element_type | solution.py:235
  (32 shorter events, 0.1 us)
Async XLA Ops:
  2.3 26.4 %collective-permute-start = (bf16[1,384,384]{2,1,0:T(8,128)(2,1)}, bf16[1,384,384]{2,1,0:T(8,128)(2,1)S(1)}, u32[]{:S(2)}, u32[]{:S(2)}) collective-permute-start(bf16[1,384,384]{2,1,0:T(8,128)(2,1)} %constant_dynamic-slice_fusion), channel_id=1, source_target_pairs={{4,0},{8,4},{12,8},{5,1},{9,5},{13,9},{6,2},{10,6},{14,10},{7,3},{... | collective-permute-start | bytes 884744 | tf_op jit(solution)/shard_map/ppermute | solution.py:149
  5.0 1.1 %copy-start = (bf16[2,384,384]{2,1,0:T(8,128)(2,1)S(1)}, bf16[2,384,384]{2,1,0:T(8,128)(2,1)}, u32[]{:S(2)}) copy-start(bf16[2,384,384]{2,1,0:T(8,128)(2,1)} %density_ref.3) | copy-start | bytes 1769476
  6.0 1.7 %copy-start.2 = (bf16[8,384,384]{2,1,0:T(8,128)(2,1)S(1)}, bf16[8,384,384]{2,1,0:T(8,128)(2,1)}, u32[]{:S(2)}) copy-start(bf16[8,384,384]{2,1,0:T(8,128)(2,1)} %coupling_ref.3) | copy-start | bytes 7077892
  7.7 0.7 %copy-start.6 = (s32[2,512]{1,0:T(2,128)S(1)}, s32[2,512]{1,0:T(2,128)}, u32[]{:S(2)}) copy-start(s32[2,512]{1,0:T(2,128)} %region_ref.1) | copy-start | bytes 12292
  8.4 0.7 %copy-start.7 = (s32[8]{0:T(128)S(1)}, s32[8]{0:T(128)}, u32[]{:S(2)}) copy-start(s32[8]{0:T(128)} %size_ref.3) | copy-start | bytes 100
  9.1 0.7 %copy-start.9 = (s32[8]{0:T(128)S(1)}, s32[8]{0:T(128)}, u32[]{:S(2)}) copy-start(s32[8]{0:T(128)} %first_ref.3) | copy-start | bytes 100
  9.7 0.7 %copy-start.11 = (s32[8]{0:T(128)S(1)}, s32[8]{0:T(128)}, u32[]{:S(2)}) copy-start(s32[8]{0:T(128)} %second_ref.3) | copy-start | bytes 100
  10.4 16.4 %copy-start.8 = (s32[8]{0:T(128)S(1)}, s32[8]{0:T(128)}, u32[]{:S(2)}) copy-start(s32[8]{0:T(128)} %size_ref.3) | copy-start | bytes 100
  10.4 24.6 %copy-start.1 = (bf16[2,384,384]{2,1,0:T(8,128)(2,1)S(1)}, bf16[2,384,384]{2,1,0:T(8,128)(2,1)}, u32[]{:S(2)}) copy-start(bf16[2,384,384]{2,1,0:T(8,128)(2,1)} %density_ref.3) | copy-start | bytes 1769476
  10.4 24.6 %copy-start.3 = (bf16[8,384,384]{2,1,0:T(8,128)(2,1)S(1)}, bf16[8,384,384]{2,1,0:T(8,128)(2,1)}, u32[]{:S(2)}) copy-start(bf16[8,384,384]{2,1,0:T(8,128)(2,1)} %coupling_ref.3) | copy-start | bytes 7077892
  10.4 24.6 %copy-start.10 = (s32[8]{0:T(128)S(1)}, s32[8]{0:T(128)}, u32[]{:S(2)}) copy-start(s32[8]{0:T(128)} %first_ref.3) | copy-start | bytes 100
  10.4 24.6 %copy-start.12 = (s32[8]{0:T(128)S(1)}, s32[8]{0:T(128)}, u32[]{:S(2)}) copy-start(s32[8]{0:T(128)} %second_ref.3) | copy-start | bytes 100
  20.1 1.0 %copy-start.13 = (f32[2,384,384]{2,1,0:T(8,128)}, f32[2,384,384]{2,1,0:T(8,128)S(1)}, u32[]{:S(2)}) copy-start(f32[2,384,384]{2,1,0:T(8,128)S(1)} %get-tuple-element.8.own_ref) | copy-start | bytes 3538948
  21.1 7.8 %collective-permute-start.3 = (bf16[2,2,96,384]{3,2,1,0:T(8,128)(2,1)}, bf16[2,2,96,384]{3,2,1,0:T(8,128)(2,1)}, u32[]{:S(2)}, u32[]{:S(2)}) collective-permute-start(bf16[2,2,96,384]{3,2,1,0:T(8,128)(2,1)} %get-tuple-element.12), channel_id=1, source_target_pairs={{0,1},{1,0},{2,3},{3,2},{4,5},{5,4},{6,7},{7,6},{8,9},{9,8},{10,11... | collective-permute-start | bytes 884744 | tf_op jit(solution)/shard_map/ppermute | solution.py:154
  22.2 22.5 %collective-permute-start.6 = (f32[2,2,128]{2,1,0:T(2,128)}, f32[2,2,128]{2,1,0:T(2,128)}, u32[]{:S(2)}, u32[]{:S(2)}) collective-permute-start(f32[2,2,128]{2,1,0:T(2,128)} %slice.13), channel_id=1, source_target_pairs={{0,8},{4,12},{8,0},{12,4},{1,9},{5,13},{9,1},{13,5},{2,10},{6,14},... | collective-permute-start | bytes 6152 | tf_op jit(solution)/shard_map/ppermute | solution.py:154
  28.7 6.2 %copy-start.4 = (bf16[1,384,384]{2,1,0:T(8,128)(2,1)}, bf16[1,384,384]{2,1,0:T(8,128)(2,1)S(1)}, u32[]{:S(2)}) copy-start(bf16[1,384,384]{2,1,0:T(8,128)(2,1)S(1)} %collective-permute-done.mine_ref) | copy-start | bytes 884740
  28.7 6.2 %collective-permute-start.1 = (bf16[1,384,384]{2,1,0:T(8,128)(2,1)S(1)}, bf16[1,384,384]{2,1,0:T(8,128)(2,1)S(1)}, u32[]{:S(2)}, u32[]{:S(2)}) collective-permute-start(bf16[1,384,384]{2,1,0:T(8,128)(2,1)S(1)} %collective-permute-done.mine_ref), channel_id=1, source_target_pairs={{0,1},{1,0},{2,3},{3,2},{4,5},{5,4},{6,7},{7,6},{8,9},{9,8},{10,11... | collective-permute-start | bytes 884744 | tf_op jit(solution)/shard_map/ppermute | solution.py:154
  30.7 14.6 %collective-permute-start.4 = (bf16[2,2,96,384]{3,2,1,0:T(8,128)(2,1)}, bf16[2,2,96,384]{3,2,1,0:T(8,128)(2,1)}, u32[]{:S(2)}, u32[]{:S(2)}) collective-permute-start(bf16[2,2,96,384]{3,2,1,0:T(8,128)(2,1)} %add_convert_fusion), channel_id=1, source_target_pairs={{0,4},{4,8},{8,12},{1,5},{5,9},{9,13},{2,6},{6,10},{10,14},{3,7},{... | collective-permute-start | bytes 884744 | tf_op jit(solution)/shard_map/ppermute | solution.py:149
  35.0 1.0 %copy-start.5 = (bf16[1,384,384]{2,1,0:T(8,128)(2,1)S(1)}, bf16[1,384,384]{2,1,0:T(8,128)(2,1)}, u32[]{:S(2)}) copy-start(bf16[1,384,384]{2,1,0:T(8,128)(2,1)} %copy-done.4) | copy-start | bytes 884740
  35.9 1.3 %copy-start.14 = (f32[2,384,384]{2,1,0:T(8,128)S(1)}, f32[2,384,384]{2,1,0:T(8,128)}, u32[]{:S(2)}) copy-start(f32[2,384,384]{2,1,0:T(8,128)} %copy-done.13) | copy-start | bytes 3538948
  37.2 7.4 %copy-start.15 = (s32[2]{0:T(128)S(1)}, s32[2]{0:T(128)}, u32[]{:S(2)}) copy-start(s32[2]{0:T(128)} %dynamic_slice.16) | copy-start | bytes 28
  44.5 1.9 %collective-permute-start.2 = (bf16[2,2,96,384]{3,2,1,0:T(8,128)(2,1)}, bf16[2,2,96,384]{3,2,1,0:T(8,128)(2,1)S(1)}, u32[]{:S(2)}, u32[]{:S(2)}) collective-permute-start(bf16[2,2,96,384]{3,2,1,0:T(8,128)(2,1)} %get-tuple-element.10), channel_id=1, source_target_pairs={{0,1},{1,0},{2,3},{3,2},{4,5},{5,4},{6,7},{7,6},{8,9},{9,8},{10,11... | collective-permute-start | bytes 884744 | tf_op jit(solution)/shard_map/ppermute | solution.py:154
  45.3 5.4 %collective-permute-start.7 = (f32[1,2,128]{2,1,0:T(2,128)S(1)}, f32[1,2,128]{2,1,0:T(2,128)S(1)}, u32[]{:S(2)}, u32[]{:S(2)}) collective-permute-start(f32[1,2,128]{2,1,0:T(2,128)S(1)} %slice.17), channel_id=1, source_target_pairs={{0,4},{4,8},{8,12},{12,0},{1,5},{5,9},{9,13},{13,1},{2,6},{6,10},{... | collective-permute-start | bytes 3080 | tf_op jit(solution)/shard_map/ppermute | solution.py:154
  47.4 6.0 %collective-permute-start.5 = (bf16[2,96,384]{2,1,0:T(8,128)(2,1)S(1)}, bf16[2,96,384]{2,1,0:T(8,128)(2,1)S(1)}, u32[]{:S(2)}, u32[]{:S(2)}) collective-permute-start(bf16[2,96,384]{2,1,0:T(8,128)(2,1)S(1)} %fusion.3), channel_id=1, source_target_pairs={{0,2},{2,0},{1,3},{3,1},{4,6},{6,4},{5,7},{7,5},{8,10},{10,8},{9,1... | collective-permute-start | bytes 442376 | tf_op jit(solution)/shard_map/ppermute | solution.py:154

commit v2 on v0

v2 whole, which is shorter than its diff:
```python
import functools
import math

import jax
import jax.numpy as jnp
from jax import lax
from jax.experimental import pallas as pl
from jax.experimental.pallas import tpu as pltpu
from jax.sharding import PartitionSpec as P

VMEM_LIMIT = 24 * 1024 * 1024
BF16, F32, I32 = jnp.bfloat16, jnp.float32, jnp.int32


def live_square(values, size):
    rows = lax.broadcasted_iota(I32, values.shape, 0)
    cols = lax.broadcasted_iota(I32, values.shape, 1)
    return jnp.where((rows < size) & (cols < size), values.astype(F32), 0.0).astype(BF16)


def charges(masked_ref, f):
    nbasis, tile = masked_ref.shape[1], 128
    parts = []
    for at in range(0, nbasis, tile):
        block = masked_ref[f, at : at + tile, at : at + tile].astype(F32)
        rows = lax.broadcasted_iota(I32, block.shape, 0)
        cols = lax.broadcasted_iota(I32, block.shape, 1)
        parts.append(jnp.sum(jnp.where(rows == cols, block, 0.0), axis=1, keepdims=True))
    return jnp.concatenate(parts, axis=0)


def split_rows(read, keep_ref, send_ref):
    frag_dev, grid_size, share, _ = keep_ref.shape
    sub_size, me = lax.axis_size("sub"), lax.axis_index("sub")
    for f in range(frag_dev):
        for g in range(grid_size):
            mine = pl.multiple_of((g * sub_size + me) * share, share)
            other = pl.multiple_of((g * sub_size + 1 - me) * share, share)
            keep_ref[f, g] = read(f, pl.ds(mine, share)).astype(keep_ref.dtype)
            send_ref[f, g] = read(f, pl.ds(other, share)).astype(send_ref.dtype)


def pipelined(slots, first_dot, second_dot, add):
    held = None
    for slot in range(slots + 1):
        now = first_dot(slot).astype(BF16) if slot < slots else None
        if held is not None:
            add(slot - 1, second_dot(slot - 1, held))
        held = now


def dot(a, b):
    return jnp.dot(a, b, preferred_element_type=F32)


def dot_t(a, b):
    return lax.dot_general(a, b, (((1,), (1,)), ((), ())), preferred_element_type=F32)


def right_kernel(
    size_hbm, first_hbm, second_hbm, count_hbm, density_ref, coupling_hbm, coords_hbm, region_hbm,
    keep_ref, send_ref, own_ref, factor_ref, masked_ref, far_ref, near_ref, ids_ref,
    size_ref, first_ref, second_ref, count_ref, coords_ref, region_ref, total_ref, sems,
):
    frag_dev, nbasis = density_ref.shape[0], density_ref.shape[1]
    slots = factor_ref.shape[0]
    copies = [
        pltpu.make_async_copy(source, target, sems.at[i])
        for i, (source, target) in enumerate(
            [
                (size_hbm, size_ref), (first_hbm, first_ref), (second_hbm, second_ref),
                (count_hbm, count_ref), (coords_hbm, coords_ref), (region_hbm, region_ref),
            ]
            + [(coupling_hbm.at[s], factor_ref.at[s]) for s in range(slots)]
        )
    ]
    for copy in copies:
        copy.start()
    total_ref[...] = jnp.zeros_like(total_ref)
    for copy in copies[:6]:
        copy.wait()
    team = lax.axis_index("frag")
    base = team * frag_dev
    trash = 2 * frag_dev
    for s in range(slots):
        live = s < count_ref[0]
        first = jnp.clip(first_ref[s] - base, 0, frag_dev - 1)
        second = jnp.clip(second_ref[s] - base, 0, trash - 1)
        ids_ref[s] = first
        ids_ref[slots + s] = second
        ids_ref[2 * slots + s] = jnp.where(live, first, frag_dev)
        ids_ref[3 * slots + s] = jnp.where(live, second, trash)
    for f in range(2 * frag_dev):
        ids_ref[4 * slots + f] = size_ref[jnp.minimum(base + f, size_ref.shape[0] - 1)]
    for f in range(frag_dev):
        masked_ref[f] = live_square(density_ref[f], size_ref[base + f])

    pts_rows = region_ref.shape[0]
    near, block_cols = near_ref.shape[0], near_ref.shape[2]
    teams = near + far_ref.shape[0]
    member = lax.axis_index("grid") * lax.axis_size("sub") + lax.axis_index("sub")
    columns = []
    for f in range(frag_dev):
        place = [coords_ref[d, f : f + 1, :] for d in range(3)]
        place = jnp.transpose(jnp.concatenate(place + [jnp.zeros((5, nbasis), F32)]))
        columns.append((charges(masked_ref, f), place[:, 0:1], place[:, 1:2], place[:, 2:3]))
    lane = lax.broadcasted_iota(I32, (1, block_cols), 1)

    def one_block(step, slab_ref, at):
        block = lax.rem(team + step, teams)
        col = block * block_cols + lane
        point_y = 0.25 * (col // 64).astype(F32)
        point_z = 0.25 * (col % 64).astype(F32)
        start = pl.multiple_of(block * block_cols, block_cols)
        totals = [jnp.zeros((1, block_cols), F32) for _ in range(pts_rows)]
        for f in range(frag_dev):
            charge, src_x, src_y, src_z = columns[f]
            in_plane = (point_y - src_y) ** 2 + (point_z - src_z) ** 2 + 1.0
            for r in range(pts_rows):
                point_x = 0.25 * (member * pts_rows + r).astype(F32)
                value = charge * lax.rsqrt((point_x - src_x) ** 2 + in_plane)
                value = jnp.sum(value, axis=0, keepdims=True)
                region = region_ref[r : r + 1, pl.ds(start, block_cols)]
                totals[r] = totals[r] + jnp.where(region != base + f, value, 0.0)
        for r in range(pts_rows):
            slab_ref[at, r : r + 1, :] = totals[r]

    @pl.loop(0, near)
    def _(step):
        one_block(step, near_ref, step)
        one_block(near + step, far_ref, step)

    for copy in copies[6:]:
        copy.wait()

    def add(s, corr):
        target = ids_ref[3 * slots + s]
        total_ref[target] = total_ref[target] + corr

    pipelined(
        slots,
        lambda s: dot(factor_ref[s].T, masked_ref[ids_ref[s]]),
        lambda s, right: dot(right, factor_ref[s]),
        add,
    )
    own_ref[...] = total_ref[:frag_dev]
    split_rows(lambda f, rows: total_ref[frag_dev + f, rows, :], keep_ref, send_ref)


def left_kernel(
    ids_ref, masked_ref, mine_ref, other_ref, own_ref, factor_ref,
    keep_ref, send_ref,
    all_ref, total_ref,
):
    frag_dev, slots, half = masked_ref.shape[0], factor_ref.shape[0], mine_ref.shape[0]
    me = lax.axis_index("sub")
    for f in range(frag_dev):
        all_ref[f] = masked_ref[f]
        total_ref[f] = own_ref[f]
    total_ref[frag_dev] = jnp.zeros_like(total_ref[frag_dev])
    for f in range(half):
        at = frag_dev + me * half + f
        all_ref[at] = live_square(mine_ref[f], ids_ref[4 * slots + at])
        at = frag_dev + (1 - me) * half + f
        all_ref[at] = live_square(other_ref[f], ids_ref[4 * slots + at])

    def add(s, corr):
        target = ids_ref[2 * slots + s]
        total_ref[target] = total_ref[target] + corr

    pipelined(
        slots,
        lambda s: dot(factor_ref[s], all_ref[ids_ref[slots + s]]),
        lambda s, left: dot_t(left, factor_ref[s]),
        add,
    )
    split_rows(lambda f, rows: total_ref[f, rows, :], keep_ref, send_ref)


def next_kernel(keep_ref, recv_ref, out_ref):
    out_ref[...] = (keep_ref[...].astype(F32) + recv_ref[...].astype(F32)).astype(BF16)


def sum_kernel(keep_ref, recv_ref, before_ref, near_ref, far_ref, own_ref, pot_ref, pass_ref, *part_refs):
    grid_size = keep_ref.shape[1]
    me = lax.axis_index("grid")

    def total(g):
        return keep_ref[:, g] + recv_ref[:, g].astype(F32) + before_ref[:, g].astype(F32)

    own_ref[...] = total(me)
    for step, part_ref in enumerate(part_refs, 1):
        part_ref[...] = total(lax.rem(me + step, grid_size)).astype(BF16)
    pot_ref[...] = near_ref[0:1] + far_ref[0:1]
    pass_ref[...] = near_ref[1:2] + far_ref[1:2]


def last_kernel(scale, slots, ids_ref, masked_ref, own_ref, pot_ref, passed_ref, *rest):
    part_refs, (out_ref, potential_ref) = rest[:-2], rest[-2:]
    frag_dev, share, nbasis = out_ref.shape
    member = lax.axis_index("grid") * lax.axis_size("sub") + lax.axis_index("sub")
    row_start = pl.multiple_of(member * share, share)
    rows = row_start + lax.broadcasted_iota(I32, (share, nbasis), 0)
    cols = lax.broadcasted_iota(I32, (share, nbasis), 1)
    for f in range(frag_dev):
        size = ids_ref[4 * slots + f]
        correction = own_ref[f]
        for part_ref in part_refs:
            correction = correction + part_ref[f].astype(F32)
        correction = jnp.where((rows < size) & (cols < size), correction, 0.0)
        out_ref[f] = (masked_ref[f, pl.ds(row_start, share), :].astype(F32) + correction).astype(BF16)
    potential_ref[...] = (pot_ref[0] + passed_ref[0]) * scale


def shifted(value, axis, steps):
    count = lax.axis_size(axis)
    return lax.ppermute(value, axis, [(s, s + steps) for s in range(count) if 0 <= s + steps < count])


def turned(value, axis, steps):
    count = lax.axis_size(axis)
    return lax.ppermute(value, axis, [(s, (s + steps) % count) for s in range(count)])


def in_hbm(value):
    return pltpu.with_memory_space_constraint(value, pltpu.HBM)


def shape(dims, dtype):
    return jax.ShapeDtypeStruct(dims, dtype)


def per_device(
    density, basis_size, coupling, pair_first, pair_second, dimer_count, source_coords, grid_region
):
    frag_dev, nbasis, _ = density.shape
    slots = coupling.shape[0]
    teams, grid_size, sub_size = (lax.axis_size(a) for a in ("frag", "grid", "sub"))
    assert sub_size == 2 and frag_dev % sub_size == 0
    assert teams >= 4 and teams & (teams - 1) == 0
    share = nbasis // (grid_size * sub_size)
    half = frag_dev // sub_size
    pts_rows, total_cols = grid_region.shape
    block_cols = total_cols // teams

    smem = pl.BlockSpec(memory_space=pltpu.SMEM)
    vmem = pl.BlockSpec(memory_space=pltpu.VMEM)
    hbm = pl.BlockSpec(memory_space=pltpu.HBM)
    halves = (frag_dev, grid_size, share, nbasis)
    square = (nbasis, nbasis)

    def call(kernel, name, ins, outs, out_specs, scratch=(), flops=0):
        return pl.pallas_call(
            kernel,
            out_shape=outs,
            in_specs=ins,
            out_specs=out_specs,
            scratch_shapes=scratch,
            compiler_params=pltpu.CompilerParams(vmem_limit_bytes=VMEM_LIMIT),
            cost_estimate=pl.CostEstimate(flops=flops, bytes_accessed=1 << 20, transcendentals=0),
            name=name,
        )

    work = 4 * slots * nbasis**3
    mine = shifted(lax.dynamic_slice_in_dim(density, lax.axis_index("sub") * half, half), "frag", -1)
    slabs = shape((teams // 2, pts_rows, block_cols), F32)
    next_keep, next_send, own_part, factors, masked, far, near, ids = call(
        right_kernel,
        "right",
        [hbm] * 4 + [vmem] + [hbm] * 3,
        (
            shape(halves, BF16), shape(halves, BF16), shape((frag_dev,) + square, F32),
            shape((slots,) + square, BF16), shape((frag_dev,) + square, BF16), slabs, slabs,
            shape((4 * slots + 2 * frag_dev,), I32),
        ),
        (vmem,) * 7 + (smem,),
        [
            pltpu.SMEM(basis_size.shape, I32), pltpu.SMEM((slots,), I32), pltpu.SMEM((slots,), I32),
            pltpu.SMEM((1,), I32), pltpu.VMEM((3, frag_dev, nbasis), F32), pltpu.VMEM(grid_region.shape, I32),
            pltpu.VMEM((2 * frag_dev + 1,) + square, F32), pltpu.SemaphoreType.DMA((6 + slots,)),
        ],
        work,
    )(
        in_hbm(basis_size), in_hbm(pair_first), in_hbm(pair_second), dimer_count, density, in_hbm(coupling),
        in_hbm(jnp.transpose(source_coords, (1, 0, 2))), in_hbm(grid_region),
    )

    next_sum = call(next_kernel, "next_sum", [vmem] * 2, shape(halves, BF16), vmem)(
        next_keep, turned(next_send, "sub", 1)
    )
    before = shifted(next_sum, "frag", 1)

    far = turned(far, "frag", teams // 2)
    while near.shape[0] > 2:
        near, rest = near + far, near.shape[0] // 2
        near, far = near[:rest], turned(near[rest:], "frag", rest)

    other = turned(mine, "sub", 1)
    own_keep, own_send = call(
        left_kernel,
        "left",
        [smem] + [vmem] * 5,
        (shape(halves, F32), shape(halves, BF16)),
        (vmem,) * 2,
        [pltpu.VMEM((2 * frag_dev,) + square, BF16), pltpu.VMEM((frag_dev + 1,) + square, F32)],
        work,
    )(ids, masked, mine, other, own_part, factors)

    slab = shape((1, pts_rows, block_cols), F32)
    own, pot, passed, *parts = call(
        sum_kernel,
        "own_sum",
        [vmem] * 5,
        (shape((frag_dev, share, nbasis), F32), slab, slab)
        + (shape((frag_dev, share, nbasis), BF16),) * (grid_size - 1),
        (vmem,) * (2 + grid_size),
    )(own_keep, turned(own_send, "sub", 1), before, near, far)
    parts = [turned(part, "grid", step) for step, part in enumerate(parts, 1)]
    passed = turned(passed, "frag", 1)

    scale = 8.0 / math.sqrt(frag_dev * teams * nbasis)
    return call(
        functools.partial(last_kernel, scale, slots),
        "last",
        [smem] + [vmem] * (4 + len(parts)),
        (shape((frag_dev, share, nbasis), BF16), shape((pts_rows, block_cols), F32)),
        (vmem,) * 2,
    )(ids, masked, own, pot, passed, *parts)


def solution(mesh):
    placed = (
        P(("groups", "frag"), None, None),
        P(),
        P(("groups", "frag", "grid", "sub"), None, None),
        P(("frag", "grid", "sub")),
        P(("frag", "grid", "sub")),
        P(("frag", "grid", "sub")),
        P(("groups", "frag"), None, None),
        P(("grid", "sub"), None),
    )
    return jax.shard_map(
        per_device,
        mesh=mesh,
        in_specs=placed,
        out_specs=(
            P(("groups", "frag"), ("grid", "sub"), None),
            P(("groups", "grid", "sub"), "frag"),
        ),
        check_vma=False,
    )
```

time: 216 us -> 35.4 us (0.16)
  local copies, waits for them, and re-layouts: 57.2 us -> 2.06 us
  waiting for transfers between devices: 50.1 us -> 7.99 us
  loops' own time: 33.9 us -> 0 us
  matrix products: 27.8 us -> 0 us
  other arithmetic: 18 us -> 0 us
  between operations: 15.6 us -> 1.35 us
  Pallas kernels: 0 us -> 11.3 us
    another operation x2 -> x0, loops' own time: 33.9 us -> none  [the longest x1 29.1 us: per_device(): lax.fori_loop(0, dimer_count[0], one_slot, jnp.zeros((2 * frag_dev, nbasi...]
    convert_element_type x1 -> x0, local copies, waits for them, and re-layouts: 30.7 us -> none  [per_device(): charge = jnp.diagonal(masked_own.astype(jnp.float32), axis1=1, axis2=2)]
    dot_general x12 -> x0, matrix products: 27.8 us -> none  [the longest x6 14.3 us: one_slot(): jnp.dot(right_part, factor, preferred_element_type=jnp.float32)]
    unnamed x3 -> x0, waiting for transfers between devices: 17.3 us -> none
    reduce_scatter x1 -> x0, waiting for transfers between devices: 15.9 us -> none  [per_device(): lax.psum_scatter(totals, ('grid', 'sub'), scatter_dimension=1, tiled=True)]
    dynamic_slice x21 -> x1, local copies, waits for them, and re-layouts: 13.2 us -> 1 us  [per_device(): lax.dynamic_slice_in_dim(density, lax.axis_index('sub') * half, half)]
    pallas_call x0 -> x5, Pallas kernels: none -> 11.3 us  [the longest x1 5.79 us: per_device(): call(right_kernel, 'right', [hbm] * 4 + [vmem] + [hbm] * 3, (shape(halves...]
    ppermute x2 -> x8, waiting for transfers between devices: 16.9 us -> 7.99 us  [the longest x6 5.38 us: turned(): lax.ppermute(value, axis, [(s, (s + steps) % count) for s in range(count)])]
  transfers between devices with their start and end apart: 4 -> 8, of which waited for: 3 -> 3; matrix products, arithmetic and copies ran while one was open for 26% -> 0% of each run, Pallas kernels for 0% -> 28%
where the time goes in v2:
time: 35.4 us; the launch traced here: 35.2 us
  starting transfers between devices  12.5 us (35%)
  Pallas kernels  11.3 us (32%)
  waiting for transfers between devices  7.99 us (23%)
  local copies, waits for them, and re-layouts  2.06 us (6%)
  between operations  1.35 us (4%)
    ppermute x6, starting transfers between devices, turned(): lax.ppermute(value, axis, [(s, (s + steps) % count) for s in range(count)])  7.13 us
    pallas_call x1, Pallas kernels, per_device(): call(right_kernel, 'right', [hbm] * 4 + [vmem] + [hbm] * 3, (shape(halves...  5.79 us
    ppermute x2, starting transfers between devices, shifted(): lax.ppermute(value, axis, [(s, s + steps) for s in range(count) if 0 <= s...  5.39 us
    ppermute x6, waiting for transfers between devices, turned(): lax.ppermute(value, axis, [(s, (s + steps) % count) for s in range(count)])  5.38 us
    pallas_call x1, Pallas kernels, per_device(): call(left_kernel, 'left', [smem] + [vmem] * 5, (shape(halves, F32), shape...  4.02 us
    ppermute x2, waiting for transfers between devices, shifted(): lax.ppermute(value, axis, [(s, s + steps) for s in range(count) if 0 <= s...  2.61 us
    pallas_call x1, Pallas kernels, per_device(): call(functools.partial(last_kernel, scale, slots), 'last', [smem] + [vmem...  1.29 us
    unnamed x2, local copies, waits for them, and re-layouts  1.06 us
  transfers between devices with their start and end apart: 8, of which 3 were waited for; matrix products, arithmetic and copies ran while one was open for 0% of the time, Pallas kernels for 28%

profile of v2, /device:TPU:0, one launch (start us, length us, event | category | flops | bytes accessed | tf_op | source)
XLA Modules:
  0.0 35.2 jit_solution(8325767051904613116)
XLA Ops:
  0.6 1.0 %constant_dynamic-slice_fusion = bf16[1,384,384]{2,1,0:T(8,128)(2,1)S(1)} fusion(bf16[2,384,384]{2,1,0:T(8,128)(2,1)} %density_ref.1, s32[]{:T(128)S(6)} %select_n.3), kind=kLoop, calls=%fused_computation | loop fusion | bytes 589828 | tf_op jit(solution)/shard_map/dynamic_slice | solution.py:265
  1.6 1.3 %collective-permute-start = (bf16[1,384,384]{2,1,0:T(8,128)(2,1)S(1)}, bf16[1,384,384]{2,1,0:T(8,128)(2,1)S(1)}, u32[]{:S(2)}, u32[]{:S(2)}) collective-permute-start(bf16[1,384,384]{2,1,0:T(8,128)(2,1)S(1)} %constant_dynamic-slice_fusion), channel_id=1, source_target_pairs={{4,0},{8,4},{12,8},{5,1},{9,5},{13,9},{6,2},{10,6},{14,10},{7,3},{... | collective-permute-start | bytes 884744 | tf_op jit(solution)/shard_map/ppermute | solution.py:217
  3.6 0.0 copy-start
  3.6 1.1 %copy-done = bf16[2,384,384]{2,1,0:T(8,128)(2,1)S(1)} copy-done((bf16[2,384,384]{2,1,0:T(8,128)(2,1)S(1)}, bf16[2,384,384]{2,1,0:T(8,128)(2,1)}, u32[]{:S(2)}) %copy-start) | copy-done | bytes 589848
  4.6 5.8 %right.1 = (bf16[2,2,96,384]{3,2,1,0:T(8,128)(2,1)S(1)}, bf16[2,2,96,384]{3,2,1,0:T(8,128)(2,1)S(1)}, f32[2,384,384]{2,1,0:T(8,128)S(1)}, bf16[8,384,384]{2,1,0:...) custom-call(s32[8]{0:T(128)} %size_hbm.1, ...), custom_call_target="tpu_custom_call" | custom-call | flops 1811939328 | bytes 1048576 | tf_op jit(solution)/shard_map/right/pallas_call | solution.py:267
  10.4 0.5 %collective-permute-start.3 = (bf16[2,2,96,384]{3,2,1,0:T(8,128)(2,1)S(1)}, bf16[2,2,96,384]{3,2,1,0:T(8,128)(2,1)S(1)}, u32[]{:S(2)}, u32[]{:S(2)}) collective-permute-start(bf16[2,2,96,384]{3,2,1,0:T(8,128)(2,1)S(1)} %get-tuple-element.23), channel_id=1, source_target_pairs={{0,1},{1,0},{2,3},{3,2},{4,5},{5,4},{6,7},{7,6},{8,9},{9,8},{10,11... | collective-permute-start | bytes 884744 | tf_op jit(solution)/shard_map/ppermute | solution.py:222
  11.0 2.6 %collective-permute-done.mine_ref = bf16[1,384,384]{2,1,0:T(8,128)(2,1)S(1)} collective-permute-done((bf16[1,384,384]{2,1,0:T(8,128)(2,1)S(1)}, bf16[1,384,384]{2,1,0:T(8,128)(2,1)S(1)}, u32[]{:S(2)}, u32[]{:S(2)}) %collective-permute-start) | collective-permute-done | bytes 294944 | tf_op jit(solution)/shard_map/ppermute | solution.py:217
  13.6 0.0 collective-permute-start.1
  13.6 0.0 collective-permute-done.3.recv_ref
  13.6 0.1 next_sum.1
  13.6 4.1 %collective-permute-start.4 = (bf16[2,2,96,384]{3,2,1,0:T(8,128)(2,1)S(1)}, bf16[2,2,96,384]{3,2,1,0:T(8,128)(2,1)S(1)}, u32[]{:S(2)}, u32[]{:S(2)}) collective-permute-start(bf16[2,2,96,384]{3,2,1,0:T(8,128)(2,1)S(1)} %next_sum.1), channel_id=1, source_target_pairs={{0,4},{4,8},{8,12},{1,5},{5,9},{9,13},{2,6},{6,10},{10,14},{3,7},{... | collective-permute-start | bytes 884744 | tf_op jit(solution)/shard_map/ppermute | solution.py:217
  17.8 0.0 collective-permute-done.1.other_ref
  17.8 4.0 %left.1 = (f32[2,2,96,384]{3,2,1,0:T(8,128)S(1)}, bf16[2,2,96,384]{3,2,1,0:T(8,128)(2,1)S(1)}) custom-call(s32[36]{0:T(128)S(1)} %get-tuple-element.16.ids_ref, bf16[2,384,384]{2,1,0:T(8,128)(2,1)S(1)} %get-tuple-element.17.masked_ref, bf16[1,384,384]{2,1,0:T(8,128)(2,1)S(1)} %collective-permute-done.mine_ref, ...), custom_call_target="tpu_custom_call" | custom-call | flops 1811939328 | bytes 1048576 | tf_op jit(solution)/shard_map/left/pallas_call | solution.py:299
  21.8 0.1 collective-permute-start.2
  21.9 3.1 %collective-permute-start.5 = (f32[2,2,128]{2,1,0:T(2,128)S(1)}, f32[2,2,128]{2,1,0:T(2,128)S(1)}, u32[]{:S(2)}, u32[]{:S(2)}) collective-permute-start(f32[2,2,128]{2,1,0:T(2,128)S(1)} %get-tuple-element.25), channel_id=1, source_target_pairs={{0,8},{4,12},{8,0},{12,4},{1,9},{5,13},{9,1},{13,5},{2,10},{6,14},... | collective-permute-start | bytes 6152 | tf_op jit(solution)/shard_map/ppermute | solution.py:222
  25.0 1.6 %collective-permute-done.5.far_ref = f32[2,2,128]{2,1,0:T(2,128)S(1)} collective-permute-done((f32[2,2,128]{2,1,0:T(2,128)S(1)}, f32[2,2,128]{2,1,0:T(2,128)S(1)}, u32[]{:S(2)}, u32[]{:S(2)}) %collective-permute-start.5) | collective-permute-done | bytes 2080 | tf_op jit(solution)/shard_map/ppermute | solution.py:222
  26.5 0.0 collective-permute-done.4.before_ref
  26.5 0.0 collective-permute-done.2.recv_ref
  26.5 0.1 own_sum.1
  26.6 1.9 %collective-permute-start.7 = (bf16[2,96,384]{2,1,0:T(8,128)(2,1)S(1)}, bf16[2,96,384]{2,1,0:T(8,128)(2,1)S(1)}, u32[]{:S(2)}, u32[]{:S(2)}) collective-permute-start(bf16[2,96,384]{2,1,0:T(8,128)(2,1)S(1)} %get-tuple-element.29), channel_id=1, source_target_pairs={{0,2},{2,0},{1,3},{3,1},{4,6},{6,4},{5,7},{7,5},{8,10},{10,8},{9,1... | collective-permute-start | bytes 442376 | tf_op jit(solution)/shard_map/ppermute | solution.py:222
  28.5 1.6 %collective-permute-start.6 = (f32[1,2,128]{2,1,0:T(2,128)S(1)}, f32[1,2,128]{2,1,0:T(2,128)S(1)}, u32[]{:S(2)}, u32[]{:S(2)}) collective-permute-start(f32[1,2,128]{2,1,0:T(2,128)S(1)} %get-tuple-element.28), channel_id=1, source_target_pairs={{0,4},{4,8},{8,12},{12,0},{1,5},{5,9},{9,13},{13,1},{2,6},{6,10},{... | collective-permute-start | bytes 3080 | tf_op jit(solution)/shard_map/ppermute | solution.py:222
  30.1 3.8 %collective-permute-done.6.passed_ref = f32[1,2,128]{2,1,0:T(2,128)S(1)} collective-permute-done((f32[1,2,128]{2,1,0:T(2,128)S(1)}, f32[1,2,128]{2,1,0:T(2,128)S(1)}, u32[]{:S(2)}, u32[]{:S(2)}) %collective-permute-start.6) | collective-permute-done | bytes 1056 | tf_op jit(solution)/shard_map/ppermute | solution.py:222
  33.9 0.0 collective-permute-done.7.rest_0_
  33.9 1.3 %last.1 = (bf16[2,96,384]{2,1,0:T(8,128)(2,1)}, f32[2,128]{1,0:T(2,128)}) custom-call(s32[36]{0:T(128)S(1)} %get-tuple-element.16.ids_ref, bf16[2,384,384]{2,1,0:T(8,128)(2,1)S(1)} %get-tuple-element.17.masked_ref, f32[2,96,384]{2,1,0:T(8,128)S(1)} %get-tuple-element.26.own_ref, f32[1,2,128]{2,1,0:T(2,128)S(1)} %get-tuple-element.27.pot_ref, ...), custom_call_target="tpu_custom_call" | custom-call | bytes 1048576 | tf_op jit(solution)/shard_map/last/pallas_call | solution.py:322
Async XLA Ops:
  1.6 11.9 %collective-permute-start = (bf16[1,384,384]{2,1,0:T(8,128)(2,1)S(1)}, bf16[1,384,384]{2,1,0:T(8,128)(2,1)S(1)}, u32[]{:S(2)}, u32[]{:S(2)}) collective-permute-start(bf16[1,384,384]{2,1,0:T(8,128)(2,1)S(1)} %constant_dynamic-slice_fusion), channel_id=1, source_target_pairs={{4,0},{8,4},{12,8},{5,1},{9,5},{13,9},{6,2},{10,6},{14,10},{7,3},{... | collective-permute-start | bytes 884744 | tf_op jit(solution)/shard_map/ppermute | solution.py:217
  3.6 1.1 %copy-start = (bf16[2,384,384]{2,1,0:T(8,128)(2,1)S(1)}, bf16[2,384,384]{2,1,0:T(8,128)(2,1)}, u32[]{:S(2)}) copy-start(bf16[2,384,384]{2,1,0:T(8,128)(2,1)} %density_ref.1) | copy-start | bytes 1769476
  10.4 3.1 %collective-permute-start.3 = (bf16[2,2,96,384]{3,2,1,0:T(8,128)(2,1)S(1)}, bf16[2,2,96,384]{3,2,1,0:T(8,128)(2,1)S(1)}, u32[]{:S(2)}, u32[]{:S(2)}) collective-permute-start(bf16[2,2,96,384]{3,2,1,0:T(8,128)(2,1)S(1)} %get-tuple-element.23), channel_id=1, source_target_pairs={{0,1},{1,0},{2,3},{3,2},{4,5},{5,4},{6,7},{7,6},{8,9},{9,8},{10,11... | collective-permute-start | bytes 884744 | tf_op jit(solution)/shard_map/ppermute | solution.py:222
  13.6 4.2 %collective-permute-start.1 = (bf16[1,384,384]{2,1,0:T(8,128)(2,1)S(1)}, bf16[1,384,384]{2,1,0:T(8,128)(2,1)S(1)}, u32[]{:S(2)}, u32[]{:S(2)}) collective-permute-start(bf16[1,384,384]{2,1,0:T(8,128)(2,1)S(1)} %collective-permute-done.mine_ref), channel_id=1, source_target_pairs={{0,1},{1,0},{2,3},{3,2},{4,5},{5,4},{6,7},{7,6},{8,9},{9,8},{10,11... | collective-permute-start | bytes 884744 | tf_op jit(solution)/shard_map/ppermute | solution.py:222
  13.6 12.9 %collective-permute-start.4 = (bf16[2,2,96,384]{3,2,1,0:T(8,128)(2,1)S(1)}, bf16[2,2,96,384]{3,2,1,0:T(8,128)(2,1)S(1)}, u32[]{:S(2)}, u32[]{:S(2)}) collective-permute-start(bf16[2,2,96,384]{3,2,1,0:T(8,128)(2,1)S(1)} %next_sum.1), channel_id=1, source_target_pairs={{0,4},{4,8},{8,12},{1,5},{5,9},{9,13},{2,6},{6,10},{10,14},{3,7},{... | collective-permute-start | bytes 884744 | tf_op jit(solution)/shard_map/ppermute | solution.py:217
  21.8 4.7 %collective-permute-start.2 = (bf16[2,2,96,384]{3,2,1,0:T(8,128)(2,1)S(1)}, bf16[2,2,96,384]{3,2,1,0:T(8,128)(2,1)S(1)}, u32[]{:S(2)}, u32[]{:S(2)}) collective-permute-start(bf16[2,2,96,384]{3,2,1,0:T(8,128)(2,1)S(1)} %get-tuple-element.21), channel_id=1, source_target_pairs={{0,1},{1,0},{2,3},{3,2},{4,5},{5,4},{6,7},{7,6},{8,9},{9,8},{10,11... | collective-permute-start | bytes 884744 | tf_op jit(solution)/shard_map/ppermute | solution.py:222
  21.9 4.7 %collective-permute-start.5 = (f32[2,2,128]{2,1,0:T(2,128)S(1)}, f32[2,2,128]{2,1,0:T(2,128)S(1)}, u32[]{:S(2)}, u32[]{:S(2)}) collective-permute-start(f32[2,2,128]{2,1,0:T(2,128)S(1)} %get-tuple-element.25), channel_id=1, source_target_pairs={{0,8},{4,12},{8,0},{12,4},{1,9},{5,13},{9,1},{13,5},{2,10},{6,14},... | collective-permute-start | bytes 6152 | tf_op jit(solution)/shard_map/ppermute | solution.py:222
  26.6 7.3 %collective-permute-start.7 = (bf16[2,96,384]{2,1,0:T(8,128)(2,1)S(1)}, bf16[2,96,384]{2,1,0:T(8,128)(2,1)S(1)}, u32[]{:S(2)}, u32[]{:S(2)}) collective-permute-start(bf16[2,96,384]{2,1,0:T(8,128)(2,1)S(1)} %get-tuple-element.29), channel_id=1, source_target_pairs={{0,2},{2,0},{1,3},{3,1},{4,6},{6,4},{5,7},{7,5},{8,10},{10,8},{9,1... | collective-permute-start | bytes 442376 | tf_op jit(solution)/shard_map/ppermute | solution.py:222
  28.5 5.4 %collective-permute-start.6 = (f32[1,2,128]{2,1,0:T(2,128)S(1)}, f32[1,2,128]{2,1,0:T(2,128)S(1)}, u32[]{:S(2)}, u32[]{:S(2)}) collective-permute-start(f32[1,2,128]{2,1,0:T(2,128)S(1)} %get-tuple-element.28), channel_id=1, source_target_pairs={{0,4},{4,8},{8,12},{12,0},{1,5},{5,9},{9,13},{13,1},{2,6},{6,10},{... | collective-permute-start | bytes 3080 | tf_op jit(solution)/shard_map/ppermute | solution.py:222

commit v3 on v2

v3 whole, which is shorter than its diff:
```python
import functools
import math

import jax
import jax.numpy as jnp
from jax import lax
from jax.experimental import pallas as pl
from jax.experimental.pallas import tpu as pltpu
from jax.sharding import PartitionSpec as P

VMEM_LIMIT = 24 * 1024 * 1024
EXTRA = 16
BF16, F32, I32 = jnp.bfloat16, jnp.float32, jnp.int32


def live_square(values, size):
    rows = lax.broadcasted_iota(I32, values.shape, 0)
    cols = lax.broadcasted_iota(I32, values.shape, 1)
    return jnp.where((rows < size) & (cols < size), values.astype(F32), 0.0).astype(BF16)


def charges(read, nbasis):
    tile = 128
    parts = []
    for at in range(0, nbasis, tile):
        block = read(at, at + tile).astype(F32)
        rows = lax.broadcasted_iota(I32, block.shape, 0)
        cols = lax.broadcasted_iota(I32, block.shape, 1)
        parts.append(jnp.sum(jnp.where(rows == cols, block, 0.0), axis=1, keepdims=True))
    return jnp.concatenate(parts, axis=0)


def charge_row(masked_ref, f):
    nbasis, tile = masked_ref.shape[1], 128
    parts = []
    for at in range(0, nbasis, tile):
        block = masked_ref[f, at : at + tile, at : at + tile].astype(F32)
        rows = lax.broadcasted_iota(I32, block.shape, 0)
        cols = lax.broadcasted_iota(I32, block.shape, 1)
        parts.append(jnp.sum(jnp.where(rows == cols, block, 0.0), axis=0, keepdims=True))
    return jnp.concatenate(parts, axis=1)


def at_rows(block, size):
    return pl.ds(pl.multiple_of(block * size, size), size)


def thirds(values):
    high = values.astype(BF16).astype(F32)
    middle = (values - high).astype(BF16).astype(F32)
    return [high, middle, values - high - middle]


def field(charge, place, point, row_x):
    src_x, src_y, src_z = place
    point_y, point_z = point
    in_plane = (point_y - src_y) ** 2 + (point_z - src_z) ** 2 + 1.0
    return [
        jnp.sum(charge * lax.rsqrt((x - src_x) ** 2 + in_plane), axis=0, keepdims=True) for x in row_x
    ]


def block_points(block, block_cols):
    col = block * block_cols + lax.broadcasted_iota(I32, (1, block_cols), 1)
    return 0.25 * (col // 64).astype(F32), 0.25 * (col % 64).astype(F32)


def row_places(pts_rows):
    member = lax.axis_index("grid") * lax.axis_size("sub") + lax.axis_index("sub")
    return [0.25 * (member * pts_rows + r).astype(F32) for r in range(pts_rows)]


def as_columns(rows):
    turned_rows = jnp.transpose(jnp.concatenate(rows + [jnp.zeros((8 - len(rows), rows[0].shape[1]), F32)]))
    return [turned_rows[:, d : d + 1] for d in range(len(rows))]


def place_rows(extra):
    return [sum(extra[3 * d + k : 3 * d + k + 1] for k in range(3)) for d in range(3)]


def by_core(total_ref, row, keep_ref, send_ref):
    me, rows = lax.axis_index("sub"), keep_ref.shape[-2]
    for f in range(keep_ref.shape[0]):
        keep_ref[f] = total_ref[f, pl.ds(row + pl.multiple_of(me * rows, rows), rows), :].astype(keep_ref.dtype)
        other = total_ref[f, pl.ds(row + pl.multiple_of((1 - me) * rows, rows), rows), :]
        send_ref[f, :rows] = other.astype(send_ref.dtype)


def pipelined(slots, first_dot, second_dot, add):
    held = None
    for slot in range(slots + 1):
        now = first_dot(slot).astype(BF16) if slot < slots else None
        if held is not None:
            add(slot - 1, second_dot(slot - 1, held))
        held = now


def dot(a, b):
    return jnp.dot(a, b, preferred_element_type=F32)


def dot_t(a, b):
    return lax.dot_general(a, b, (((1,), (1,)), ((), ())), preferred_element_type=F32)


def fetch(pairs, sems):
    copies = [pltpu.make_async_copy(source, target, sems.at[i]) for i, (source, target) in enumerate(pairs)]
    for copy in copies:
        copy.start()
    return copies


def head_kernel(density_hbm, coords_hbm, payload_ref, coords_ref, sems):
    half, nbasis = payload_ref.shape[0], payload_ref.shape[2]
    at = lax.axis_index("sub") * half
    copies = fetch(
        [(density_hbm.at[pl.ds(at, half)], payload_ref.at[:, pl.ds(0, nbasis)]), (coords_hbm, coords_ref)], sems
    )
    copies[1].wait()
    for f in range(half):
        rows = [part for d in range(3) for part in thirds(coords_ref[d, pl.ds(at + f, 1), :])]
        rows.append(jnp.zeros((EXTRA - len(rows), nbasis), F32))
        payload_ref[f, nbasis:, :] = jnp.concatenate(rows).astype(BF16)
    copies[0].wait()


def right_kernel(
    size_hbm, first_hbm, second_hbm, count_ref, density_hbm, coupling_hbm, coords_hbm, region_hbm,
    keep_ref, send_ref, own_ref, factor_ref, masked_ref, ids_ref, sizes_ref, here_ref, sources_ref, *rest,
):
    slab_refs, rest = rest[:4], rest[4:]
    size_ref, first_ref, second_ref, density_ref, coords_ref, region_ref, total_ref, sems = rest
    frag_dev, nbasis, slots = masked_ref.shape[0], masked_ref.shape[1], factor_ref.shape[0]
    copies = fetch(
        [
            (size_hbm, size_ref), (first_hbm, first_ref), (second_hbm, second_ref),
            (density_hbm, density_ref), (coords_hbm, coords_ref), (region_hbm, region_ref),
        ]
        + [(coupling_hbm.at[s], factor_ref.at[s]) for s in range(slots)],
        sems,
    )
    total_ref[...] = jnp.zeros_like(total_ref)
    for copy in copies[:6]:
        copy.wait()
    team = lax.axis_index("frag")
    base = team * frag_dev
    trash = 2 * frag_dev
    for s in range(slots):
        live = s < count_ref[0]
        first = jnp.clip(first_ref[s] - base, 0, frag_dev - 1)
        second = jnp.clip(second_ref[s] - base, 0, trash - 1)
        ids_ref[s] = first
        ids_ref[slots + s] = second
        ids_ref[2 * slots + s] = jnp.where(live, first, frag_dev)
        ids_ref[3 * slots + s] = jnp.where(live, second, trash)
    for f in range(2 * frag_dev):
        sizes_ref[f] = jnp.full((8, 128), size_ref[lax.rem(base + f, size_ref.shape[0])], I32)
    for f in range(frag_dev):
        masked_ref[f] = live_square(density_ref[f], size_ref[base + f])
    for copy in copies[6:]:
        copy.wait()

    for f in range(frag_dev):
        rows = [part for d in range(3) for part in thirds(coords_ref[d, f : f + 1, :])]
        rows.append(charge_row(masked_ref, f))
        rows.append(jnp.zeros((EXTRA - len(rows), nbasis), F32))
        sources_ref[f] = jnp.concatenate(rows).astype(BF16)

    pts_rows = region_ref.shape[0]
    each, block_cols = slab_refs[0].shape[0], slab_refs[0].shape[2]
    teams = len(slab_refs) * each
    sources = [
        (
            charges(lambda low, high, f=f: masked_ref[f, low:high, low:high], nbasis),
            as_columns([coords_ref[d, f : f + 1, :] for d in range(3)]),
        )
        for f in range(frag_dev)
    ]
    row_x = row_places(pts_rows)

    def one_block(step, slab_ref, at):
        block = lax.rem(team + step, teams)
        point = block_points(block, block_cols)
        region = region_ref[:, pl.ds(pl.multiple_of(block * block_cols, block_cols), block_cols)]
        fields = [field(charge, place, point, row_x) for charge, place in sources]
        for r in range(pts_rows):
            here = [jnp.where(region[r : r + 1] != base + f, fields[f][r], 0.0) for f in range(frag_dev)]
            slab_ref[at, r : r + 1, :] = sum(here)

    if each == 1:
        one_block(0, slab_refs[0], 0)
        one_block(2, slab_refs[2], 0)
    else:

        @pl.loop(0, each)
        def _(step):
            for k, slab_ref in enumerate(slab_refs):
                one_block(k * each + step, slab_ref, step)

    for k in (1, teams - 1):
        slab_refs[k // each][k % each] = jnp.zeros((pts_rows, block_cols), F32)
    here_ref[...] = region_ref[:, pl.ds(pl.multiple_of(team * block_cols, block_cols), block_cols)]

    def add(s, corr):
        target = ids_ref[3 * slots + s]
        total_ref[target] = total_ref[target] + corr

    pipelined(
        slots,
        lambda s: dot(factor_ref[s].T, masked_ref[ids_ref[s]]),
        lambda s, right: dot(right, factor_ref[s]),
        add,
    )
    own_ref[...] = total_ref[:frag_dev]
    by_core(total_ref.at[pl.ds(frag_dev, frag_dev)], 0, keep_ref, send_ref)
    send_ref[:, keep_ref.shape[1] :, :] = jnp.zeros((frag_dev, EXTRA, nbasis), BF16)


def left_kernel(
    ids_ref, sizes_ref, masked_ref, mine_ref, other_ref, own_ref, factor_ref, after_ref,
    keep_ref, send_ref,
    all_ref, total_ref,
):
    frag_dev, nbasis = masked_ref.shape[0], masked_ref.shape[1]
    slots, half = factor_ref.shape[0], mine_ref.shape[0]
    me = lax.axis_index("sub")
    for f in range(frag_dev):
        all_ref[f] = masked_ref[f]
    for f in range(half):
        at = frag_dev + me * half + f
        all_ref[at] = live_square(mine_ref[f, :nbasis], sizes_ref[at, 0:1, 0:1])
        at = frag_dev + (1 - me) * half + f
        all_ref[at] = live_square(other_ref[f, :nbasis], sizes_ref[at, 0:1, 0:1])
    total_ref[:frag_dev] = own_ref[...]
    total_ref[frag_dev] = jnp.zeros_like(total_ref[frag_dev])

    def add(s, corr):
        target = ids_ref[2 * slots + s]
        total_ref[target] = total_ref[target] + corr

    pipelined(
        slots,
        lambda s: dot(factor_ref[s], all_ref[ids_ref[slots + s]]),
        lambda s, left: dot_t(left, factor_ref[s]),
        add,
    )
    for g in range(keep_ref.shape[0]):
        by_core(total_ref, 2 * g * keep_ref.shape[2], keep_ref.at[g], send_ref.at[g])


def own_sum_kernel(keep_ref, recv_ref, own_ref, *part_refs):
    grid_size, frag_dev, share, nbasis = keep_ref.shape
    me = lax.axis_index("grid")
    own_ref[...] = keep_ref[me] + recv_ref[me].astype(F32)
    for step, part_ref in enumerate(part_refs, 1):
        at = lax.rem(me + step, grid_size)
        for f in range(frag_dev):
            part_ref[f * share : (f + 1) * share] = (keep_ref[at, f] + recv_ref[at, f].astype(F32)).astype(BF16)
        part_ref[frag_dev * share :] = jnp.zeros((EXTRA, nbasis), BF16)


def relay_kernel(here_ref, in_ref, out_ref):
    out_ref[...] = in_ref[...]


def next_kernel(keep_ref, recv_ref, sources_ref, *out_refs):
    out_refs, after_ref = out_refs[:-1], out_refs[-1]
    after_ref[...] = jnp.zeros_like(after_ref)
    rounds = len(out_refs)
    rows = out_refs[0].shape[1] - EXTRA
    for j, out_ref in enumerate(out_refs):
        at = at_rows(lax.rem(lax.axis_index("grid") + j, rounds), rows) if rounds > 1 else slice(0, rows)
        total = keep_ref[:, at, :].astype(F32) + recv_ref[:, at, :].astype(F32)
        out_ref[:, :rows, :] = total.astype(BF16)
        out_ref[:, rows:, :] = sources_ref[...]


def before_kernel(own_ref, far_ref, later_ref, *refs):
    in_refs, (keep_ref, send_ref, pot_ref) = refs[:-3], refs[-3:]
    me, rows = lax.axis_index("sub"), keep_ref.shape[1]
    keep_ref[...] = own_ref[...] + sum(r[:, at_rows(me, rows), :].astype(F32) for r in in_refs)
    send_ref[...] = sum(r[:, at_rows(1 - me, rows), :].astype(F32) for r in in_refs).astype(BF16)
    pot_ref[...] = far_ref[...] + later_ref[...]


def felt(sources, here_ref, out_ref):
    pts_rows, block_cols = here_ref.shape
    point, row_x = block_points(lax.axis_index("frag"), block_cols), row_places(pts_rows)
    totals = [jnp.zeros((1, block_cols), F32) for _ in range(pts_rows)]
    for fragment, charge, place in sources:
        fields = field(charge, place, point, row_x)
        for r in range(pts_rows):
            totals[r] = totals[r] + jnp.where(here_ref[r : r + 1, :] != fragment, fields[r], 0.0)
    for r in range(pts_rows):
        out_ref[0, r : r + 1, :] = totals[r]


def after_kernel(sizes_ref, mine_ref, other_ref, here_ref, out_ref):
    half, nbasis = mine_ref.shape[0], mine_ref.shape[2]
    me, team, teams = lax.axis_index("sub"), lax.axis_index("frag"), lax.axis_size("frag")
    column = lax.broadcasted_iota(I32, (nbasis, 1), 0)
    sources = []
    for ref, start in ((mine_ref, me * half), (other_ref, (1 - me) * half)):
        for f in range(half):
            charge = charges(lambda low, high, ref=ref, f=f: ref[f, low:high, low:high], nbasis)
            charge = jnp.where(column < sizes_ref[2 * half + start + f, 0:1, 0:1], charge, 0.0)
            place = as_columns(place_rows(ref[f, nbasis:, :].astype(F32)))
            sources.append((lax.rem(team + 1, teams) * 2 * half + start + f, charge, place))
    felt(sources, here_ref, out_ref)


def prior_kernel(here_ref, piece_ref, out_ref):
    frag_dev, team, teams = piece_ref.shape[0], lax.axis_index("frag"), lax.axis_size("frag")
    sources = []
    for f in range(frag_dev):
        extra = piece_ref[f, piece_ref.shape[1] - EXTRA :, :].astype(F32)
        *place, charge = as_columns(place_rows(extra) + [extra[9:10]])
        sources.append((lax.rem(team + teams - 1, teams) * frag_dev + f, charge, place))
    felt(sources, here_ref, out_ref)


def last_kernel(scale, slab_count, sizes_ref, masked_ref, own_ref, recv_ref, *rest):
    slab_refs, part_refs, (out_ref, potential_ref) = rest[:slab_count], rest[slab_count:-2], rest[-2:]
    frag_dev, share, nbasis = out_ref.shape
    member = lax.axis_index("grid") * lax.axis_size("sub") + lax.axis_index("sub")
    row_start = pl.multiple_of(member * share, share)
    rows = row_start + lax.broadcasted_iota(I32, (share, nbasis), 0)
    cols = lax.broadcasted_iota(I32, (share, nbasis), 1)
    for f in range(frag_dev):
        size = sizes_ref[f, 0:1, 0:1]
        correction = own_ref[f] + recv_ref[f].astype(F32)
        for part_ref in part_refs:
            correction = correction + part_ref[f * share : (f + 1) * share, :].astype(F32)
        correction = jnp.where((rows < size) & (cols < size), correction, 0.0)
        out_ref[f] = (masked_ref[f, pl.ds(row_start, share), :].astype(F32) + correction).astype(BF16)
    potential_ref[...] = sum(slab_ref[0] for slab_ref in slab_refs) * scale


def turned(value, axis, steps):
    count = lax.axis_size(axis)
    return lax.ppermute(value, axis, [(s, (s + steps) % count) for s in range(count)])


def in_hbm(value):
    return pltpu.with_memory_space_constraint(value, pltpu.HBM)


def shape(dims, dtype):
    return jax.ShapeDtypeStruct(dims, dtype)


def per_device(
    density, basis_size, coupling, pair_first, pair_second, dimer_count, source_coords, grid_region
):
    frag_dev, nbasis, _ = density.shape
    slots = coupling.shape[0]
    teams, grid_size, sub_size = (lax.axis_size(a) for a in ("frag", "grid", "sub"))
    assert sub_size == 2 and frag_dev == 2 and grid_size % sub_size == 0
    rounds = grid_size // sub_size
    assert teams >= 4 and teams & (teams - 1) == 0
    share = nbasis // (grid_size * sub_size)
    half = frag_dev // sub_size
    pts_rows, total_cols = grid_region.shape
    block_cols = total_cols // teams

    smem = pl.BlockSpec(memory_space=pltpu.SMEM)
    vmem = pl.BlockSpec(memory_space=pltpu.VMEM)
    hbm = pl.BlockSpec(memory_space=pltpu.HBM)
    square = (nbasis, nbasis)

    def call(kernel, name, ins, outs, out_specs, scratch=(), flops=0):
        return pl.pallas_call(
            kernel,
            out_shape=outs,
            in_specs=ins,
            out_specs=out_specs,
            scratch_shapes=scratch,
            compiler_params=pltpu.CompilerParams(vmem_limit_bytes=VMEM_LIMIT),
            cost_estimate=pl.CostEstimate(flops=flops, bytes_accessed=1 << 20, transcendentals=0),
            name=name,
        )

    work = 4 * slots * nbasis**3
    by_chip = (grid_size, frag_dev, share, nbasis)
    halves = shape((frag_dev, nbasis // sub_size, nbasis), BF16)
    sent_halves = shape((frag_dev, nbasis // sub_size + EXTRA, nbasis), BF16)
    places = in_hbm(jnp.transpose(source_coords, (1, 0, 2)))
    payload = call(
        head_kernel,
        "head",
        [hbm] * 2,
        shape((half, nbasis + EXTRA, nbasis), BF16),
        vmem,
        [pltpu.VMEM((3, frag_dev, nbasis), F32), pltpu.SemaphoreType.DMA((2,))],
    )(in_hbm(density), places)
    mine = turned(payload, "frag", -1)

    next_keep, next_send, own_part, factors, masked, ids, sizes, here, sources, *slabs = call(
        right_kernel,
        "right",
        [hbm] * 3 + [smem] + [hbm] * 4,
        (
            halves, sent_halves, shape((frag_dev,) + square, F32),
            shape((slots,) + square, BF16), shape((frag_dev,) + square, BF16),
            shape((4 * slots,), I32), shape((2 * frag_dev, 8, 128), I32), shape((pts_rows, block_cols), I32),
            shape((frag_dev, EXTRA, nbasis), BF16),
        ) + (shape((teams // 4, pts_rows, block_cols), F32),) * 4,
        (vmem,) * 5 + (smem,) + (vmem,) * 7,
        [
            pltpu.SMEM(basis_size.shape, I32), pltpu.SMEM((slots,), I32), pltpu.SMEM((slots,), I32),
            pltpu.VMEM(density.shape, BF16), pltpu.VMEM((3, frag_dev, nbasis), F32),
            pltpu.VMEM(grid_region.shape, I32), pltpu.VMEM((2 * frag_dev + 1,) + square, F32),
            pltpu.SemaphoreType.DMA((6 + slots,)),
        ],
        work,
    )(
        in_hbm(basis_size), in_hbm(pair_first), in_hbm(pair_second), dimer_count, in_hbm(density),
        in_hbm(coupling), places, in_hbm(grid_region),
    )

    if teams == 4:
        home, far = slabs[0], turned(slabs[2], "frag", 2)
    else:
        slabs = jnp.concatenate(slabs)
        while slabs.shape[0] > 1:
            rest = slabs.shape[0] // 2
            slabs = slabs[:rest] + turned(slabs[rest:], "frag", rest)
        home, far = slabs, jnp.zeros_like(slabs)

    *pieces, after = call(
        next_kernel,
        "next_sum",
        [vmem] * 3,
        [shape((frag_dev, nbasis // grid_size + EXTRA, nbasis), BF16)] * rounds + [shape((8, 128), F32)],
        (vmem,) * (rounds + 1),
    )(next_keep, turned(next_send, "sub", 1), sources)
    for j, value in enumerate(pieces):
        pairs = [
            (
                (t * grid_size + g) * sub_size + c,
                ((t + 1) % teams * grid_size + c * rounds + (g + j) % rounds) * sub_size + g // rounds,
            )
            for t in range(teams)
            for g in range(grid_size)
            for c in range(sub_size)
        ]
        pieces[j] = lax.ppermute(value, ("frag", "grid", "sub"), pairs)

    mine = call(relay_kernel, "relay", [vmem] * 2, shape(payload.shape, BF16), vmem)(here, mine)
    other = turned(mine, "sub", 1)
    own_keep, own_send = call(
        left_kernel,
        "left",
        [smem] + [vmem] * 7,
        (shape(by_chip, F32), shape(by_chip, BF16)),
        (vmem,) * 2,
        [pltpu.VMEM((2 * frag_dev,) + square, BF16), pltpu.VMEM((frag_dev + 1,) + square, F32)],
        work,
    )(ids, sizes, masked, mine, other, own_part, factors, after)
    mine_rows = (frag_dev, share, nbasis)
    own, *parts = call(
        own_sum_kernel,
        "own_sum",
        [vmem] * 2,
        [shape(mine_rows, F32)] + [shape((frag_dev * share + EXTRA, nbasis), BF16)] * (grid_size - 1),
        (vmem,) * grid_size,
    )(own_keep, turned(own_send, "sub", 1))
    parts = [turned(part, "grid", step) for step, part in enumerate(parts, 1)]

    slab = shape((1, pts_rows, block_cols), F32)
    later = call(after_kernel, "after", [vmem] * 4, slab, vmem)(sizes, mine, other, here)
    own, passed, far = call(
        before_kernel,
        "before",
        [vmem] * (3 + rounds),
        (shape(mine_rows, F32), shape(mine_rows, BF16), slab),
        (vmem,) * 3,
    )(own, far, later, *pieces)
    passed = turned(passed, "sub", 1)
    prior = call(prior_kernel, "prior", [vmem] * 2, slab, vmem)(here, pieces[0])

    scale = 8.0 / math.sqrt(frag_dev * teams * nbasis)
    return call(
        functools.partial(last_kernel, scale, 3),
        "last",
        [vmem] * (7 + len(parts)),
        (shape(mine_rows, BF16), shape((pts_rows, block_cols), F32)),
        (vmem,) * 2,
    )(sizes, masked, own, passed, home, far, prior, *parts)


def solution(mesh):
    placed = (
        P(("groups", "frag"), None, None),
        P(),
        P(("groups", "frag", "grid", "sub"), None, None),
        P(("frag", "grid", "sub")),
        P(("frag", "grid", "sub")),
        P(("frag", "grid", "sub")),
        P(("groups", "frag"), None, None),
        P(("grid", "sub"), None),
    )
    return jax.shard_map(
        per_device,
        mesh=mesh,
        in_specs=placed,
        out_specs=(
            P(("groups", "frag"), ("grid", "sub"), None),
            P(("groups", "grid", "sub"), "frag"),
        ),
        check_vma=False,
    )
```

time: 35.4 us -> 30 us (0.85)
  waiting for transfers between devices: 7.99 us -> 4.4 us
  local copies, waits for them, and re-layouts: 2.06 us -> 0 us
  Pallas kernels: 11.3 us -> 13.3 us
  starting transfers between devices: 12.5 us -> 10.8 us
    ppermute x2 -> x1, starting transfers between devices: 5.39 us -> 0.06 us  [per_device(): pieces[j] = lax.ppermute(value, ('frag', 'grid', 'sub'), pairs)]
    ppermute x6 -> x7, starting transfers between devices: 7.13 us -> 10.7 us  [turned(): lax.ppermute(value, axis, [(s, (s + steps) % count) for s in range(count)])]
    ppermute x2 -> x1, waiting for transfers between devices: 2.61 us -> 0.01 us  [per_device(): pieces[j] = lax.ppermute(value, ('frag', 'grid', 'sub'), pairs)]
    pallas_call x5 -> x10, Pallas kernels: 11.3 us -> 13.3 us  [the longest x1 5.56 us: per_device(): call(right_kernel, 'right', [hbm] * 3 + [smem] + [hbm] * 4, (halves, sent...]
    unnamed x2 -> x0, local copies, waits for them, and re-layouts: 1.06 us -> none
    dynamic_slice x1 -> x0, local copies, waits for them, and re-layouts: 1 us -> none  [per_device(): lax.dynamic_slice_in_dim(density, lax.axis_index('sub') * half, half)]
    ppermute x6 -> x7, waiting for transfers between devices: 5.38 us -> 4.4 us  [turned(): lax.ppermute(value, axis, [(s, (s + steps) % count) for s in range(count)])]
  transfers between devices with their start and end apart: 8 -> 8, of which waited for: 3 -> 7; matrix products, arithmetic and copies ran while one was open for 0% -> 0% of each run, Pallas kernels for 28% -> 39%
where the time goes in v3:
time: 30 us; the launch traced here: 29.8 us
  Pallas kernels  13.3 us (44%)
  starting transfers between devices  10.8 us (36%)
  waiting for transfers between devices  4.4 us (15%)
  between operations  1.35 us (4%)
    ppermute x7, starting transfers between devices, turned(): lax.ppermute(value, axis, [(s, (s + steps) % count) for s in range(count)])  10.7 us
    pallas_call x1, Pallas kernels, per_device(): call(right_kernel, 'right', [hbm] * 3 + [smem] + [hbm] * 4, (halves, sent...  5.56 us
    ppermute x7, waiting for transfers between devices, turned(): lax.ppermute(value, axis, [(s, (s + steps) % count) for s in range(count)])  4.4 us
    pallas_call x1, Pallas kernels, per_device(): call(left_kernel, 'left', [smem] + [vmem] * 7, (shape(by_chip, F32), shap...  4.05 us
    pallas_call x1, Pallas kernels, per_device(): call(head_kernel, 'head', [hbm] * 2, shape((half, nbasis + EXTRA, nbasis)...  0.99 us
    pallas_call x1, Pallas kernels, per_device(): call(after_kernel, 'after', [vmem] * 4, slab, vmem)  0.91 us
    pallas_call x1, Pallas kernels, per_device(): prior = call(prior_kernel, 'prior', [vmem] * 2, slab, vmem)(here, pieces[0])  0.78 us
    pallas_call x1, Pallas kernels, per_device(): call(functools.partial(last_kernel, scale, 3), 'last', [vmem] * (7 + len(...  0.78 us
  transfers between devices with their start and end apart: 8, of which 7 were waited for; matrix products, arithmetic and copies ran while one was open for 0% of the time, Pallas kernels for 39%

profile of v3, /device:TPU:0, one launch (start us, length us, event | category | flops | bytes accessed | tf_op | source)
XLA Modules:
  0.0 29.8 jit_solution(9230658212614523473)
XLA Ops:
  0.6 1.0 %head.1 = bf16[1,400,384]{2,1,0:T(8,128)(2,1)S(1)} custom-call(bf16[2,384,384]{2,1,0:T(8,128)(2,1)} %density_hbm.3, f32[3,2,384]{2,1,0:T(2,128)} %bitcast.1), custom_call_target="tpu_custom_call" | custom-call | bytes 1048576 | tf_op jit(solution)/shard_map/head/pallas_call | solution.py:389
  1.6 5.1 %collective-permute-start = (bf16[1,400,384]{2,1,0:T(8,128)(2,1)S(1)}, bf16[1,400,384]{2,1,0:T(8,128)(2,1)S(1)}, u32[]{:S(2)}, u32[]{:S(2)}) collective-permute-start(bf16[1,400,384]{2,1,0:T(8,128)(2,1)S(1)} %head.1), channel_id=1, source_target_pairs={{0,12},{4,0},{8,4},{12,8},{1,13},{5,1},{9,5},{13,9},{2,14},{6,2},{... | collective-permute-start | bytes 921608 | tf_op jit(solution)/shard_map/ppermute | solution.py:342
  7.4 5.6 %right.1 = (bf16[2,192,384]{2,1,0:T(8,128)(2,1)S(1)}, bf16[2,208,384]{2,1,0:T(8,128)(2,1)S(1)}, f32[2,384,384]{2,1,0:T(8,128)S(1)}, bf16[8,384,384]{2,1,0:T(8,12...) custom-call(s32[8]{0:T(128)} %size_hbm.1, ...), custom_call_target="tpu_custom_call" | custom-call | flops 1811939328 | bytes 1048576 | tf_op jit(solution)/shard_map/right/pallas_call | solution.py:399
  12.9 0.1 collective-permute-start.2
  13.0 0.2 collective-permute-done.in_ref
  13.3 0.3 %collective-permute-start.1 = (bf16[1,400,384]{2,1,0:T(8,128)(2,1)S(1)}, bf16[1,400,384]{2,1,0:T(8,128)(2,1)S(1)}, u32[]{:S(2)}, u32[]{:S(2)}) collective-permute-start(bf16[1,400,384]{2,1,0:T(8,128)(2,1)S(1)} %relay.1.mine_ref), channel_id=1, source_target_pairs={{0,1},{1,0},{2,3},{3,2},{4,5},{5,4},{6,7},{7,6},{8,9},{9,8},{10,11... | collective-permute-start | bytes 921608 | tf_op jit(solution)/shard_map/ppermute | solution.py:342
  13.6 1.0 %collective-permute-done.2.recv_ref = bf16[2,208,384]{2,1,0:T(8,128)(2,1)S(1)} collective-permute-done((bf16[2,208,384]{2,1,0:T(8,128)(2,1)S(1)}, bf16[2,208,384]{2,1,0:T(8,128)(2,1)S(1)}, u32[]{:S(2)}, u32[]{:S(2)}) %collective-permute-start.2) | collective-permute-done | bytes 319520 | tf_op jit(solution)/shard_map/ppermute | solution.py:342
  14.6 0.1 next_sum.1
  14.7 0.1 collective-permute-start.5
  14.8 0.3 collective-permute-done.1.other_ref
  15.1 4.1 %left.1 = (f32[2,2,96,384]{3,2,1,0:T(8,128)S(1)}, bf16[2,2,96,384]{3,2,1,0:T(8,128)(2,1)S(1)}) custom-call(s32[32]{0:T(128)S(1)} %get-tuple-element.24.ids_ref, s32[4,8,128]{2,1,0:T(8,128)S(1)} %get-tuple-element.22.sizes_ref, bf16[2,384,384]{2,1,0:T(8,128)(2,1)S(1)} %get-tuple-element.23.masked_ref, bf16[1,400,384]{2,1,0:T(8,128)(2,1)S(1)} %relay.1.mine_ref, ...), custom_call_target="tpu_custom_call" | custom-call | flops 1811939328 | bytes 1048576 | tf_op jit(solution)/shard_map/left/pallas_call | solution.py:452
  19.1 0.2 collective-permute-start.3
  19.3 1.4 %collective-permute-done.3.recv_ref = bf16[2,2,96,384]{3,2,1,0:T(8,128)(2,1)S(1)} collective-permute-done((bf16[2,2,96,384]{3,2,1,0:T(8,128)(2,1)S(1)}, bf16[2,2,96,384]{3,2,1,0:T(8,128)(2,1)S(1)}, u32[]{:S(2)}, u32[]{:S(2)}) %collective-permute-start.3) | collective-permute-done | bytes 294944 | tf_op jit(solution)/shard_map/ppermute | solution.py:342
  20.8 0.1 own_sum.1
  20.8 1.6 %collective-permute-start.7 = (bf16[208,384]{1,0:T(8,128)(2,1)S(1)}, bf16[208,384]{1,0:T(8,128)(2,1)S(1)}, u32[]{:S(2)}, u32[]{:S(2)}) collective-permute-start(bf16[208,384]{1,0:T(8,128)(2,1)S(1)} %get-tuple-element.41), channel_id=1, source_target_pairs={{0,2},{2,0},{1,3},{3,1},{4,6},{6,4},{5,7},{7,5},{8,10},{10,8},{9,1... | collective-permute-start | bytes 479240 | tf_op jit(solution)/shard_map/ppermute | solution.py:342
  22.4 3.4 %collective-permute-start.4 = (f32[1,2,128]{2,1,0:T(2,128)S(1)}, f32[1,2,128]{2,1,0:T(2,128)S(1)}, u32[]{:S(2)}, u32[]{:S(2)}) collective-permute-start(f32[1,2,128]{2,1,0:T(2,128)S(1)} %get-tuple-element.35), channel_id=1, source_target_pairs={{0,8},{4,12},{8,0},{12,4},{1,9},{5,13},{9,1},{13,5},{2,10},{6,14},... | collective-permute-start | bytes 3080 | tf_op jit(solution)/shard_map/ppermute | solution.py:342
  25.7 0.9 %after.1.later_ref = f32[1,2,128]{2,1,0:T(2,128)S(1)} custom-call(s32[4,8,128]{2,1,0:T(8,128)S(1)} %get-tuple-element.22.sizes_ref, bf16[1,400,384]{2,1,0:T(8,128)(2,1)S(1)} %relay.1.mine_ref, bf16[1,400,384]{2,1,0:T(8,128)(2,1)S(1)} %collective-permute-done.1.other_ref, s32[2,128]{1,0:T(2,128)S(1)} %get-tuple-element.25.here_ref), custom_call_target="tpu_custom_call" | custom-call | bytes 1048576 | tf_op jit(solution)/shard_map/after/pallas_call | solution.py:472
  26.7 0.6 %collective-permute-done.4.far_ref = f32[1,2,128]{2,1,0:T(2,128)S(1)} collective-permute-done((f32[1,2,128]{2,1,0:T(2,128)S(1)}, f32[1,2,128]{2,1,0:T(2,128)S(1)}, u32[]{:S(2)}, u32[]{:S(2)}) %collective-permute-start.4) | collective-permute-done | bytes 1056 | tf_op jit(solution)/shard_map/ppermute | solution.py:342
  27.3 0.0 collective-permute-done.5.refs_0_.piece_ref
  27.3 0.1 collective-permute-start.6
  27.4 0.8 %prior.1.rest_2_ = f32[1,2,128]{2,1,0:T(2,128)S(1)} custom-call(s32[2,128]{1,0:T(2,128)S(1)} %get-tuple-element.25.here_ref, bf16[2,208,384]{2,1,0:T(8,128)(2,1)S(1)} %collective-permute-done.5.refs_0_.piece_ref), custom_call_target="tpu_custom_call" | custom-call | bytes 1048576 | tf_op jit(solution)/shard_map/prior/pallas_call | solution.py:481
  28.2 0.6 %collective-permute-done.6.recv_ref = bf16[2,96,384]{2,1,0:T(8,128)(2,1)S(1)} collective-permute-done((bf16[2,96,384]{2,1,0:T(8,128)(2,1)S(1)}, bf16[2,96,384]{2,1,0:T(8,128)(2,1)S(1)}, u32[]{:S(2)}, u32[]{:S(2)}) %collective-permute-start.6) | collective-permute-done | bytes 147488 | tf_op jit(solution)/shard_map/ppermute | solution.py:342
  28.8 0.2 collective-permute-done.7.rest_3_
  29.0 0.8 %last.1 = (bf16[2,96,384]{2,1,0:T(8,128)(2,1)}, f32[2,128]{1,0:T(2,128)}) custom-call(s32[4,8,128]{2,1,0:T(8,128)S(1)} %get-tuple-element.22.sizes_ref, bf16[2,384,384]{2,1,0:T(8,128)(2,1)S(1)} %get-tuple-element.23.masked_ref, f32[2,96,384]{2,1,0:T(8,128)S(1)} %get-tuple-element.37.own_ref, bf16[2,96,384]{2,1,0:T(8,128)(2,1)S(1)} %collective-permute-done.6.recv_ref, ...), custom_call_target="tpu_custom_call" | custom-call | bytes 1048576 | tf_op jit(solution)/shard_map/last/pallas_call | solution.py:484
  (2 shorter events, 0.1 us)
Async XLA Ops:
  1.6 11.6 %collective-permute-start = (bf16[1,400,384]{2,1,0:T(8,128)(2,1)S(1)}, bf16[1,400,384]{2,1,0:T(8,128)(2,1)S(1)}, u32[]{:S(2)}, u32[]{:S(2)}) collective-permute-start(bf16[1,400,384]{2,1,0:T(8,128)(2,1)S(1)} %head.1), channel_id=1, source_target_pairs={{0,12},{4,0},{8,4},{12,8},{1,13},{5,1},{9,5},{13,9},{2,14},{6,2},{... | collective-permute-start | bytes 921608 | tf_op jit(solution)/shard_map/ppermute | solution.py:342
  12.9 1.7 %collective-permute-start.2 = (bf16[2,208,384]{2,1,0:T(8,128)(2,1)S(1)}, bf16[2,208,384]{2,1,0:T(8,128)(2,1)S(1)}, u32[]{:S(2)}, u32[]{:S(2)}) collective-permute-start(bf16[2,208,384]{2,1,0:T(8,128)(2,1)S(1)} %get-tuple-element.29), channel_id=1, source_target_pairs={{0,1},{1,0},{2,3},{3,2},{4,5},{5,4},{6,7},{7,6},{8,9},{9,8},{10,11... | collective-permute-start | bytes 958472 | tf_op jit(solution)/shard_map/ppermute | solution.py:342
  13.3 1.8 %collective-permute-start.1 = (bf16[1,400,384]{2,1,0:T(8,128)(2,1)S(1)}, bf16[1,400,384]{2,1,0:T(8,128)(2,1)S(1)}, u32[]{:S(2)}, u32[]{:S(2)}) collective-permute-start(bf16[1,400,384]{2,1,0:T(8,128)(2,1)S(1)} %relay.1.mine_ref), channel_id=1, source_target_pairs={{0,1},{1,0},{2,3},{3,2},{4,5},{5,4},{6,7},{7,6},{8,9},{9,8},{10,11... | collective-permute-start | bytes 921608 | tf_op jit(solution)/shard_map/ppermute | solution.py:342
  14.7 12.6 %collective-permute-start.5 = (bf16[2,208,384]{2,1,0:T(8,128)(2,1)S(1)}, bf16[2,208,384]{2,1,0:T(8,128)(2,1)S(1)}, u32[]{:S(2)}, u32[]{:S(2)}) collective-permute-start(bf16[2,208,384]{2,1,0:T(8,128)(2,1)S(1)} %get-tuple-element.36), channel_id=1, source_target_pairs={{0,4},{1,6},{2,5},{3,7},{4,8},{5,10},{6,9},{7,11},{8,12},{9,14},{1... | collective-permute-start | bytes 958472 | tf_op jit(solution)/shard_map/ppermute | solution.py:448
  19.1 1.6 %collective-permute-start.3 = (bf16[2,2,96,384]{3,2,1,0:T(8,128)(2,1)S(1)}, bf16[2,2,96,384]{3,2,1,0:T(8,128)(2,1)S(1)}, u32[]{:S(2)}, u32[]{:S(2)}) collective-permute-start(bf16[2,2,96,384]{3,2,1,0:T(8,128)(2,1)S(1)} %get-tuple-element.33), channel_id=1, source_target_pairs={{0,1},{1,0},{2,3},{3,2},{4,5},{5,4},{6,7},{7,6},{8,9},{9,8},{10,11... | collective-permute-start | bytes 884744 | tf_op jit(solution)/shard_map/ppermute | solution.py:342
  20.8 8.2 %collective-permute-start.7 = (bf16[208,384]{1,0:T(8,128)(2,1)S(1)}, bf16[208,384]{1,0:T(8,128)(2,1)S(1)}, u32[]{:S(2)}, u32[]{:S(2)}) collective-permute-start(bf16[208,384]{1,0:T(8,128)(2,1)S(1)} %get-tuple-element.41), channel_id=1, source_target_pairs={{0,2},{2,0},{1,3},{3,1},{4,6},{6,4},{5,7},{7,5},{8,10},{10,8},{9,1... | collective-permute-start | bytes 479240 | tf_op jit(solution)/shard_map/ppermute | solution.py:342
  22.4 4.9 %collective-permute-start.4 = (f32[1,2,128]{2,1,0:T(2,128)S(1)}, f32[1,2,128]{2,1,0:T(2,128)S(1)}, u32[]{:S(2)}, u32[]{:S(2)}) collective-permute-start(f32[1,2,128]{2,1,0:T(2,128)S(1)} %get-tuple-element.35), channel_id=1, source_target_pairs={{0,8},{4,12},{8,0},{12,4},{1,9},{5,13},{9,1},{13,5},{2,10},{6,14},... | collective-permute-start | bytes 3080 | tf_op jit(solution)/shard_map/ppermute | solution.py:342
  27.3 1.4 %collective-permute-start.6 = (bf16[2,96,384]{2,1,0:T(8,128)(2,1)S(1)}, bf16[2,96,384]{2,1,0:T(8,128)(2,1)S(1)}, u32[]{:S(2)}, u32[]{:S(2)}) collective-permute-start(bf16[2,96,384]{2,1,0:T(8,128)(2,1)S(1)} %get-tuple-element.38), channel_id=1, source_target_pairs={{0,1},{1,0},{2,3},{3,2},{4,5},{5,4},{6,7},{7,6},{8,9},{9,8},{10,11... | collective-permute-start | bytes 442376 | tf_op jit(solution)/shard_map/ppermute | solution.py:342

commit v4 on v3

--- a/solution.py
+++ b/solution.py
@@ -19,24 +19,13 @@
     return jnp.where((rows < size) & (cols < size), values.astype(F32), 0.0).astype(BF16)
 
 
-def charges(read, nbasis):
+def charge_row(read, nbasis):
     tile = 128
     parts = []
     for at in range(0, nbasis, tile):
         block = read(at, at + tile).astype(F32)
         rows = lax.broadcasted_iota(I32, block.shape, 0)
         cols = lax.broadcasted_iota(I32, block.shape, 1)
-        parts.append(jnp.sum(jnp.where(rows == cols, block, 0.0), axis=1, keepdims=True))
-    return jnp.concatenate(parts, axis=0)
-
-
-def charge_row(masked_ref, f):
-    nbasis, tile = masked_ref.shape[1], 128
-    parts = []
-    for at in range(0, nbasis, tile):
-        block = masked_ref[f, at : at + tile, at : at + tile].astype(F32)
-        rows = lax.broadcasted_iota(I32, block.shape, 0)
-        cols = lax.broadcasted_iota(I32, block.shape, 1)
         parts.append(jnp.sum(jnp.where(rows == cols, block, 0.0), axis=0, keepdims=True))
     return jnp.concatenate(parts, axis=1)
 
@@ -51,28 +40,34 @@
     return [high, middle, values - high - middle]
 
 
-def field(charge, place, point, row_x):
+def field(charge, place, block, block_cols, row_x):
     src_x, src_y, src_z = place
-    point_y, point_z = point
-    in_plane = (point_y - src_y) ** 2 + (point_z - src_z) ** 2 + 1.0
+    point_z = 0.25 * lax.broadcasted_iota(I32, (64, charge.shape[1]), 0).astype(F32)
+    along_z = (point_z - src_z) ** 2 + 1.0
+    parts = []
+    for x in row_x:
+        for step in range(block_cols // 64):
+            point_y = 0.25 * (block * (block_cols // 64) + step).astype(F32)
+            in_plane = (x - src_x) ** 2 + (point_y - src_y) ** 2
+            value = charge * lax.rsqrt(along_z + in_plane)
+            parts.append(sum(value[:, at : at + 128] for at in range(0, value.shape[1], 128)))
+    return jnp.concatenate(parts)
+
+
+def over_lanes(points, block_cols, pts_rows):
+    rows = jnp.concatenate(points)
+    ones = jnp.ones((16, 128), BF16)
+    total = sum(dot_t(ones, part.astype(BF16)) for part in thirds(rows))
+    size = pts_rows * block_cols
     return [
-        jnp.sum(charge * lax.rsqrt((x - src_x) ** 2 + in_plane), axis=0, keepdims=True) for x in row_x
+        [total[0:1, k * size + r * block_cols : k * size + (r + 1) * block_cols] for r in range(pts_rows)]
+        for k in range(len(points))
     ]
-
-
-def block_points(block, block_cols):
-    col = block * block_cols + lax.broadcasted_iota(I32, (1, block_cols), 1)
-    return 0.25 * (col // 64).astype(F32), 0.25 * (col % 64).astype(F32)
 
 
 def row_places(pts_rows):
     member = lax.axis_index("grid") * lax.axis_size("sub") + lax.axis_index("sub")
     return [0.25 * (member * pts_rows + r).astype(F32) for r in range(pts_rows)]
-
-
-def as_columns(rows):
-    turned_rows = jnp.transpose(jnp.concatenate(rows + [jnp.zeros((8 - len(rows), rows[0].shape[1]), F32)]))
-    return [turned_rows[:, d : d + 1] for d in range(len(rows))]
 
 
 def place_rows(extra):
@@ -158,32 +153,29 @@
         sizes_ref[f] = jnp.full((8, 128), size_ref[lax.rem(base + f, size_ref.shape[0])], I32)
     for f in range(frag_dev):
         masked_ref[f] = live_square(density_ref[f], size_ref[base + f])
-    for copy in copies[6:]:
-        copy.wait()
-
+    sources = [
+        (
+            charge_row(lambda low, high, f=f: masked_ref[f, low:high, low:high], nbasis),
+            [coords_ref[d, f : f + 1, :] for d in range(3)],
+        )
+        for f in range(frag_dev)
+    ]
     for f in range(frag_dev):
         rows = [part for d in range(3) for part in thirds(coords_ref[d, f : f + 1, :])]
-        rows.append(charge_row(masked_ref, f))
+        rows.append(sources[f][0])
         rows.append(jnp.zeros((EXTRA - len(rows), nbasis), F32))
         sources_ref[f] = jnp.concatenate(rows).astype(BF16)
 
     pts_rows = region_ref.shape[0]
     each, block_cols = slab_refs[0].shape[0], slab_refs[0].shape[2]
     teams = len(slab_refs) * each
-    sources = [
-        (
-            charges(lambda low, high, f=f: masked_ref[f, low:high, low:high], nbasis),
-            as_columns([coords_ref[d, f : f + 1, :] for d in range(3)]),
-        )
-        for f in range(frag_dev)
-    ]
     row_x = row_places(pts_rows)
 
     def one_block(step, slab_ref, at):
         block = lax.rem(team + step, teams)
-        point = block_points(block, block_cols)
         region = region_ref[:, pl.ds(pl.multiple_of(block * block_cols, block_cols), block_cols)]
-        fields = [field(charge, place, point, row_x) for charge, place in sources]
+        fields = [field(charge, place, block, block_cols, row_x) for charge, place in sources]
+        fields = over_lanes(fields, block_cols, pts_rows)
         for r in range(pts_rows):
             here = [jnp.where(region[r : r + 1] != base + f, fields[f][r], 0.0) for f in range(frag_dev)]
             slab_ref[at, r : r + 1, :] = sum(here)
@@ -201,6 +193,9 @@
     for k in (1, teams - 1):
         slab_refs[k // each][k % each] = jnp.zeros((pts_rows, block_cols), F32)
     here_ref[...] = region_ref[:, pl.ds(pl.multiple_of(team * block_cols, block_cols), block_cols)]
+
+    for copy in copies[6:]:
+        copy.wait()
 
     def add(s, corr):
         target = ids_ref[3 * slots + s]
@@ -219,9 +214,9 @@
 
 def left_kernel(
     ids_ref, sizes_ref, masked_ref, mine_ref, other_ref, own_ref, factor_ref, after_ref,
-    keep_ref, send_ref,
-    all_ref, total_ref,
+    keep_ref, *rest,
 ):
+    send_refs, (all_ref, total_ref) = rest[:-2], rest[-2:]
     frag_dev, nbasis = masked_ref.shape[0], masked_ref.shape[1]
     slots, half = factor_ref.shape[0], mine_ref.shape[0]
     me = lax.axis_index("sub")
@@ -245,19 +240,23 @@
         lambda s, left: dot_t(left, factor_ref[s]),
         add,
     )
-    for g in range(keep_ref.shape[0]):
-        by_core(total_ref, 2 * g * keep_ref.shape[2], keep_ref.at[g], send_ref.at[g])
-
-
-def own_sum_kernel(keep_ref, recv_ref, own_ref, *part_refs):
+    grid_size, _, share, _ = keep_ref.shape
+    for g in range(grid_size):
+        for f in range(frag_dev):
+            chip = total_ref.at[f, 2 * g * share : 2 * (g + 1) * share]
+            keep_ref[g, f] = chip[at_rows(me, share), :]
+            send_refs[f][g] = chip[at_rows(1 - me, share), :].astype(BF16)
+
+
+def own_sum_kernel(keep_ref, *rest):
     grid_size, frag_dev, share, nbasis = keep_ref.shape
+    recv_refs, own_ref, part_refs = rest[:frag_dev], rest[frag_dev], rest[frag_dev + 1 :]
     me = lax.axis_index("grid")
-    own_ref[...] = keep_ref[me] + recv_ref[me].astype(F32)
-    for step, part_ref in enumerate(part_refs, 1):
-        at = lax.rem(me + step, grid_size)
-        for f in range(frag_dev):
-            part_ref[f * share : (f + 1) * share] = (keep_ref[at, f] + recv_ref[at, f].astype(F32)).astype(BF16)
-        part_ref[frag_dev * share :] = jnp.zeros((EXTRA, nbasis), BF16)
+    for f in range(frag_dev):
+        own_ref[f] = keep_ref[me, f] + recv_refs[f][me].astype(F32)
+        for step, part_ref in enumerate(part_refs, 1):
+            at = lax.rem(me + step, grid_size)
+            part_ref[f] = (keep_ref[at, f] + recv_refs[f][at].astype(F32)).astype(BF16)
 
 
 def relay_kernel(here_ref, in_ref, out_ref):
@@ -276,22 +275,27 @@
         out_ref[:, rows:, :] = sources_ref[...]
 
 
-def before_kernel(own_ref, far_ref, later_ref, *refs):
-    in_refs, (keep_ref, send_ref, pot_ref) = refs[:-3], refs[-3:]
+def before_kernel(*refs):
+    in_refs, (keep_ref, send_ref) = refs[:-2], refs[-2:]
     me, rows = lax.axis_index("sub"), keep_ref.shape[1]
-    keep_ref[...] = own_ref[...] + sum(r[:, at_rows(me, rows), :].astype(F32) for r in in_refs)
+    keep_ref[...] = sum(r[:, at_rows(me, rows), :].astype(F32) for r in in_refs)
     send_ref[...] = sum(r[:, at_rows(1 - me, rows), :].astype(F32) for r in in_refs).astype(BF16)
-    pot_ref[...] = far_ref[...] + later_ref[...]
+
+
+def middle_kernel(own_ref, home_ref, far_ref, later_ref, prior_ref, *rest):
+    part_refs, (out_ref, pot_ref) = rest[:-2], rest[-2:]
+    out_ref[...] = own_ref[...] + sum(part_ref[...].astype(F32) for part_ref in part_refs)
+    pot_ref[...] = home_ref[...] + far_ref[...] + later_ref[...] + prior_ref[...]
 
 
 def felt(sources, here_ref, out_ref):
     pts_rows, block_cols = here_ref.shape
-    point, row_x = block_points(lax.axis_index("frag"), block_cols), row_places(pts_rows)
+    team, row_x = lax.axis_index("frag"), row_places(pts_rows)
     totals = [jnp.zeros((1, block_cols), F32) for _ in range(pts_rows)]
-    for fragment, charge, place in sources:
-        fields = field(charge, place, point, row_x)
+    fields = [field(charge, place, team, block_cols, row_x) for _, charge, place in sources]
+    for (fragment, _, _), rows in zip(sources, over_lanes(fields, block_cols, pts_rows)):
         for r in range(pts_rows):
-            totals[r] = totals[r] + jnp.where(here_ref[r : r + 1, :] != fragment, fields[r], 0.0)
+            totals[r] = totals[r] + jnp.where(here_ref[r : r + 1, :] != fragment, rows[r], 0.0)
     for r in range(pts_rows):
         out_ref[0, r : r + 1, :] = totals[r]
 
@@ -299,13 +303,13 @@
 def after_kernel(sizes_ref, mine_ref, other_ref, here_ref, out_ref):
     half, nbasis = mine_ref.shape[0], mine_ref.shape[2]
     me, team, teams = lax.axis_index("sub"), lax.axis_index("frag"), lax.axis_size("frag")
-    column = lax.broadcasted_iota(I32, (nbasis, 1), 0)
+    column = lax.broadcasted_iota(I32, (1, nbasis), 1)
     sources = []
     for ref, start in ((mine_ref, me * half), (other_ref, (1 - me) * half)):
         for f in range(half):
-            charge = charges(lambda low, high, ref=ref, f=f: ref[f, low:high, low:high], nbasis)
+            charge = charge_row(lambda low, high, ref=ref, f=f: ref[f, low:high, low:high], nbasis)
             charge = jnp.where(column < sizes_ref[2 * half + start + f, 0:1, 0:1], charge, 0.0)
-            place = as_columns(place_rows(ref[f, nbasis:, :].astype(F32)))
+            place = place_rows(ref[f, nbasis:, :].astype(F32))
             sources.append((lax.rem(team + 1, teams) * 2 * half + start + f, charge, place))
     felt(sources, here_ref, out_ref)
 
@@ -315,13 +319,11 @@
     sources = []
     for f in range(frag_dev):
         extra = piece_ref[f, piece_ref.shape[1] - EXTRA :, :].astype(F32)
-        *place, charge = as_columns(place_rows(extra) + [extra[9:10]])
-        sources.append((lax.rem(team + teams - 1, teams) * frag_dev + f, charge, place))
+        sources.append((lax.rem(team + teams - 1, teams) * frag_dev + f, extra[9:10], place_rows(extra)))
     felt(sources, here_ref, out_ref)
 
 
-def last_kernel(scale, slab_count, sizes_ref, masked_ref, own_ref, recv_ref, *rest):
-    slab_refs, part_refs, (out_ref, potential_ref) = rest[:slab_count], rest[slab_count:-2], rest[-2:]
+def last_kernel(scale, sizes_ref, masked_ref, own_ref, before_ref, recv_ref, pot_ref, out_ref, potential_ref):
     frag_dev, share, nbasis = out_ref.shape
     member = lax.axis_index("grid") * lax.axis_size("sub") + lax.axis_index("sub")
     row_start = pl.multiple_of(member * share, share)
@@ -329,12 +331,10 @@
     cols = lax.broadcasted_iota(I32, (share, nbasis), 1)
     for f in range(frag_dev):
         size = sizes_ref[f, 0:1, 0:1]
-        correction = own_ref[f] + recv_ref[f].astype(F32)
-        for part_ref in part_refs:
-            correction = correction + part_ref[f * share : (f + 1) * share, :].astype(F32)
+        correction = own_ref[f] + before_ref[f] + recv_ref[f].astype(F32)
         correction = jnp.where((rows < size) & (cols < size), correction, 0.0)
         out_ref[f] = (masked_ref[f, pl.ds(row_start, share), :].astype(F32) + correction).astype(BF16)
-    potential_ref[...] = sum(slab_ref[0] for slab_ref in slab_refs) * scale
+    potential_ref[...] = pot_ref[0] * scale
 
 
 def turned(value, axis, steps):
@@ -436,25 +436,23 @@
         (vmem,) * (rounds + 1),
     )(next_keep, turned(next_send, "sub", 1), sources)
     for j, value in enumerate(pieces):
-        pairs = [
-            (
-                (t * grid_size + g) * sub_size + c,
-                ((t + 1) % teams * grid_size + c * rounds + (g + j) % rounds) * sub_size + g // rounds,
-            )
-            for t in range(teams)
-            for g in range(grid_size)
-            for c in range(sub_size)
-        ]
+        pairs = []
+        for t in range(teams):
+            for g in range(grid_size):
+                for c in range(sub_size):
+                    to = (c * rounds + (g + j) % rounds, g // rounds) if t + 1 < teams else (g, c)
+                    to = ((t + 1) % teams * grid_size + to[0]) * sub_size + to[1]
+                    pairs.append(((t * grid_size + g) * sub_size + c, to))
         pieces[j] = lax.ppermute(value, ("frag", "grid", "sub"), pairs)
 
     mine = call(relay_kernel, "relay", [vmem] * 2, shape(payload.shape, BF16), vmem)(here, mine)
     other = turned(mine, "sub", 1)
-    own_keep, own_send = call(
+    own_keep, *own_sends = call(
         left_kernel,
         "left",
         [smem] + [vmem] * 7,
-        (shape(by_chip, F32), shape(by_chip, BF16)),
-        (vmem,) * 2,
+        [shape(by_chip, F32)] + [shape((grid_size, share, nbasis), BF16)] * frag_dev,
+        (vmem,) * (1 + frag_dev),
         [pltpu.VMEM((2 * frag_dev,) + square, BF16), pltpu.VMEM((frag_dev + 1,) + square, F32)],
         work,
     )(ids, sizes, masked, mine, other, own_part, factors, after)
@@ -462,32 +460,41 @@
     own, *parts = call(
         own_sum_kernel,
         "own_sum",
-        [vmem] * 2,
-        [shape(mine_rows, F32)] + [shape((frag_dev * share + EXTRA, nbasis), BF16)] * (grid_size - 1),
+        [vmem] * (1 + frag_dev),
+        [shape(mine_rows, F32)] + [shape(mine_rows, BF16)] * (grid_size - 1),
         (vmem,) * grid_size,
-    )(own_keep, turned(own_send, "sub", 1))
+    )(own_keep, *[turned(value, "sub", 1) for value in own_sends])
     parts = [turned(part, "grid", step) for step, part in enumerate(parts, 1)]
 
     slab = shape((1, pts_rows, block_cols), F32)
     later = call(after_kernel, "after", [vmem] * 4, slab, vmem)(sizes, mine, other, here)
-    own, passed, far = call(
+    before, passed = call(
         before_kernel,
         "before",
-        [vmem] * (3 + rounds),
-        (shape(mine_rows, F32), shape(mine_rows, BF16), slab),
-        (vmem,) * 3,
-    )(own, far, later, *pieces)
+        [vmem] * rounds,
+        (shape(mine_rows, F32), shape(mine_rows, BF16)),
+        (vmem,) * 2,
+    )(*pieces)
     passed = turned(passed, "sub", 1)
     prior = call(prior_kernel, "prior", [vmem] * 2, slab, vmem)(here, pieces[0])
+    own, pot = call(
+        middle_kernel,
+        "middle",
+        [vmem] * (5 + len(parts)),
+        (shape(mine_rows, F32), slab),
+        (vmem,) * 2,
+        (),
+        10**10,
+    )(own, home, far, later, prior, *parts)
 
     scale = 8.0 / math.sqrt(frag_dev * teams * nbasis)
     return call(
-        functools.partial(last_kernel, scale, 3),
+        functools.partial(last_kernel, scale),
         "last",
-        [vmem] * (7 + len(parts)),
+        [vmem] * 6,
         (shape(mine_rows, BF16), shape((pts_rows, block_cols), F32)),
         (vmem,) * 2,
-    )(sizes, masked, own, passed, home, far, prior, *parts)
+    )(sizes, masked, own, before, passed, pot)
 
 
 def solution(mesh):

time: 30 us -> 28.7 us (0.957)
  Pallas kernels: 13.3 us -> 12.3 us
  waiting for transfers between devices: 4.4 us -> 3.74 us
    ppermute x7 -> x8, waiting for transfers between devices: 4.4 us -> 3.74 us  [turned(): lax.ppermute(value, axis, [(s, (s + steps) % count) for s in range(count)])]
    pallas_call x1, Pallas kernels: 0.91 us -> 0.42 us  [per_device(): call(after_kernel, 'after', [vmem] * 4, slab, vmem)]
    pallas_call x1, Pallas kernels: 0.78 us -> 0.37 us  [per_device(): prior = call(prior_kernel, 'prior', [vmem] * 2, slab, vmem)(here, pieces[0])]
    ppermute x7 -> x8, starting transfers between devices: 10.7 us -> 11 us  [turned(): lax.ppermute(value, axis, [(s, (s + steps) % count) for s in range(count)])]
    pallas_call x4 -> x5, Pallas kernels: 4.93 us -> 4.97 us  [the longest x1 4.05 us: per_device(): call(left_kernel, 'left', [smem] + [vmem] * 7, [shape(by_chip, F32)] + [s...]
  transfers between devices with their start and end apart: 8 -> 9, of which waited for: 7 -> 7; matrix products, arithmetic and copies ran while one was open for 0% -> 0% of each run, Pallas kernels for 39% -> 37%
where the time goes in v4:
time: 28.7 us; the launch traced here: 28.5 us
  Pallas kernels  12.3 us (43%)
  starting transfers between devices  11.1 us (39%)
  waiting for transfers between devices  3.74 us (13%)
  between operations  1.36 us (5%)
    ppermute x8, starting transfers between devices, turned(): lax.ppermute(value, axis, [(s, (s + steps) % count) for s in range(count)])  11 us
    pallas_call x1, Pallas kernels, per_device(): call(right_kernel, 'right', [hbm] * 3 + [smem] + [hbm] * 4, (halves, sent...  5.41 us
    pallas_call x1, Pallas kernels, per_device(): call(left_kernel, 'left', [smem] + [vmem] * 7, [shape(by_chip, F32)] + [s...  4.05 us
    ppermute x8, waiting for transfers between devices, turned(): lax.ppermute(value, axis, [(s, (s + steps) % count) for s in range(count)])  3.74 us
    pallas_call x1, Pallas kernels, per_device(): call(head_kernel, 'head', [hbm] * 2, shape((half, nbasis + EXTRA, nbasis)...  0.99 us
    pallas_call x1, Pallas kernels, per_device(): call(functools.partial(last_kernel, scale), 'last', [vmem] * 6, (shape(mi...  0.78 us
  transfers between devices with their start and end apart: 9, of which 7 were waited for; matrix products, arithmetic and copies ran while one was open for 0% of the time, Pallas kernels for 37%

profile of v4, /device:TPU:0, one launch (start us, length us, event | category | flops | bytes accessed | tf_op | source)
XLA Modules:
  0.0 28.5 jit_solution(6935063817669562198)
XLA Ops:
  0.6 1.0 %head.1 = bf16[1,400,384]{2,1,0:T(8,128)(2,1)S(1)} custom-call(bf16[2,384,384]{2,1,0:T(8,128)(2,1)} %density_hbm.3, f32[3,2,384]{2,1,0:T(2,128)} %bitcast.1), custom_call_target="tpu_custom_call" | custom-call | bytes 1048576 | tf_op jit(solution)/shard_map/head/pallas_call | solution.py:389
  1.6 5.1 %collective-permute-start = (bf16[1,400,384]{2,1,0:T(8,128)(2,1)S(1)}, bf16[1,400,384]{2,1,0:T(8,128)(2,1)S(1)}, u32[]{:S(2)}, u32[]{:S(2)}) collective-permute-start(bf16[1,400,384]{2,1,0:T(8,128)(2,1)S(1)} %head.1), channel_id=1, source_target_pairs={{0,12},{4,0},{8,4},{12,8},{1,13},{5,1},{9,5},{13,9},{2,14},{6,2},{... | collective-permute-start | bytes 921608 | tf_op jit(solution)/shard_map/ppermute | solution.py:342
  7.4 5.4 %right.1 = (bf16[2,192,384]{2,1,0:T(8,128)(2,1)S(1)}, bf16[2,208,384]{2,1,0:T(8,128)(2,1)S(1)}, f32[2,384,384]{2,1,0:T(8,128)S(1)}, bf16[8,384,384]{2,1,0:T(8,12...) custom-call(s32[8]{0:T(128)} %size_hbm.1, ...), custom_call_target="tpu_custom_call" | custom-call | flops 1811939328 | bytes 1048576 | tf_op jit(solution)/shard_map/right/pallas_call | solution.py:399
  12.8 0.1 collective-permute-start.2
  12.9 0.4 %collective-permute-done.in_ref = bf16[1,400,384]{2,1,0:T(8,128)(2,1)S(1)} collective-permute-done((bf16[1,400,384]{2,1,0:T(8,128)(2,1)S(1)}, bf16[1,400,384]{2,1,0:T(8,128)(2,1)S(1)}, u32[]{:S(2)}, u32[]{:S(2)}) %collective-permute-start) | collective-permute-done | bytes 307232 | tf_op jit(solution)/shard_map/ppermute | solution.py:342
  13.3 0.2 collective-permute-start.1
  13.5 1.0 %collective-permute-done.2.recv_ref = bf16[2,208,384]{2,1,0:T(8,128)(2,1)S(1)} collective-permute-done((bf16[2,208,384]{2,1,0:T(8,128)(2,1)S(1)}, bf16[2,208,384]{2,1,0:T(8,128)(2,1)S(1)}, u32[]{:S(2)}, u32[]{:S(2)}) %collective-permute-start.2) | collective-permute-done | bytes 319520 | tf_op jit(solution)/shard_map/ppermute | solution.py:342
  14.5 0.1 next_sum.1
  14.6 0.1 collective-permute-start.6
  14.6 0.3 %collective-permute-done.1.other_ref = bf16[1,400,384]{2,1,0:T(8,128)(2,1)S(1)} collective-permute-done((bf16[1,400,384]{2,1,0:T(8,128)(2,1)S(1)}, bf16[1,400,384]{2,1,0:T(8,128)(2,1)S(1)}, u32[]{:S(2)}, u32[]{:S(2)}) %collective-permute-start.1) | collective-permute-done | bytes 307232 | tf_op jit(solution)/shard_map/ppermute | solution.py:342
  15.0 4.0 %left.1 = (f32[2,2,96,384]{3,2,1,0:T(8,128)S(1)}, bf16[2,96,384]{2,1,0:T(8,128)(2,1)S(1)}, bf16[2,96,384]{2,1,0:T(8,128)(2,1)S(1)}) custom-call(s32[32]{0:T(128)S(1)} %get-tuple-element.26.ids_ref, s32[4,8,128]{2,1,0:T(8,128)S(1)} %get-tuple-element.24.sizes_ref, bf16[2,384,384]{2,1,0:T(8,128)(2,1)S(1)} %get-tuple-element.25.masked_ref, ...), custom_call_target="tpu_custom_call" | custom-call | flops 1811939328 | bytes 1048576 | tf_op jit(solution)/shard_map/left/pallas_call | solution.py:450
  19.0 0.2 collective-permute-start.3
  19.2 0.4 %collective-permute-start.4 = (bf16[2,96,384]{2,1,0:T(8,128)(2,1)S(1)}, bf16[2,96,384]{2,1,0:T(8,128)(2,1)S(1)}, u32[]{:S(2)}, u32[]{:S(2)}) collective-permute-start(bf16[2,96,384]{2,1,0:T(8,128)(2,1)S(1)} %get-tuple-element.36), channel_id=1, source_target_pairs={{0,1},{1,0},{2,3},{3,2},{4,5},{5,4},{6,7},{7,6},{8,9},{9,8},{10,11... | collective-permute-start | bytes 442376 | tf_op jit(solution)/shard_map/ppermute | solution.py:342
  19.6 0.9 %collective-permute-done.3.rest_0_ = bf16[2,96,384]{2,1,0:T(8,128)(2,1)S(1)} collective-permute-done((bf16[2,96,384]{2,1,0:T(8,128)(2,1)S(1)}, bf16[2,96,384]{2,1,0:T(8,128)(2,1)S(1)}, u32[]{:S(2)}, u32[]{:S(2)}) %collective-permute-start.3) | collective-permute-done | bytes 147488 | tf_op jit(solution)/shard_map/ppermute | solution.py:342
  20.4 0.2 collective-permute-done.4.rest_1_
  20.7 0.1 own_sum.1
  20.7 1.6 %collective-permute-start.7 = (bf16[2,96,384]{2,1,0:T(8,128)(2,1)S(1)}, bf16[2,96,384]{2,1,0:T(8,128)(2,1)S(1)}, u32[]{:S(2)}, u32[]{:S(2)}) collective-permute-start(bf16[2,96,384]{2,1,0:T(8,128)(2,1)S(1)} %get-tuple-element.41), channel_id=1, source_target_pairs={{0,2},{2,0},{1,3},{3,1},{4,6},{6,4},{5,7},{7,5},{8,10},{10,8},{9,1... | collective-permute-start | bytes 442376 | tf_op jit(solution)/shard_map/ppermute | solution.py:342
  22.3 3.5 %collective-permute-start.5 = (f32[1,2,128]{2,1,0:T(2,128)S(1)}, f32[1,2,128]{2,1,0:T(2,128)S(1)}, u32[]{:S(2)}, u32[]{:S(2)}) collective-permute-start(f32[1,2,128]{2,1,0:T(2,128)S(1)} %get-tuple-element.39), channel_id=1, source_target_pairs={{0,8},{4,12},{8,0},{12,4},{1,9},{5,13},{9,1},{13,5},{2,10},{6,14},... | collective-permute-start | bytes 3080 | tf_op jit(solution)/shard_map/ppermute | solution.py:342
  25.8 0.4 %after.1.later_ref = f32[1,2,128]{2,1,0:T(2,128)S(1)} custom-call(s32[4,8,128]{2,1,0:T(8,128)S(1)} %get-tuple-element.24.sizes_ref, bf16[1,400,384]{2,1,0:T(8,128)(2,1)S(1)} %relay.1.mine_ref, bf16[1,400,384]{2,1,0:T(8,128)(2,1)S(1)} %collective-permute-done.1.other_ref, s32[2,128]{1,0:T(2,128)S(1)} %get-tuple-element.27.here_ref), custom_call_target="tpu_custom_call" | custom-call | bytes 1048576 | tf_op jit(solution)/shard_map/after/pallas_call | solution.py:470
  26.2 0.0 collective-permute-done.6.piece_ref.refs_0_
  26.2 0.1 before.1
  26.2 0.1 collective-permute-start.8
  26.3 0.4 %prior.1.prior_ref = f32[1,2,128]{2,1,0:T(2,128)S(1)} custom-call(s32[2,128]{1,0:T(2,128)S(1)} %get-tuple-element.27.here_ref, bf16[2,208,384]{2,1,0:T(8,128)(2,1)S(1)} %collective-permute-done.6.piece_ref.refs_0_), custom_call_target="tpu_custom_call" | custom-call | bytes 1048576 | tf_op jit(solution)/shard_map/prior/pallas_call | solution.py:479
  26.7 0.6 %collective-permute-done.5.far_ref = f32[1,2,128]{2,1,0:T(2,128)S(1)} collective-permute-done((f32[1,2,128]{2,1,0:T(2,128)S(1)}, f32[1,2,128]{2,1,0:T(2,128)S(1)}, u32[]{:S(2)}, u32[]{:S(2)}) %collective-permute-start.5) | collective-permute-done | bytes 1056 | tf_op jit(solution)/shard_map/ppermute | solution.py:342
  27.3 0.0 collective-permute-done.7.rest_0_
  27.3 0.3 %collective-permute-done.8.recv_ref = bf16[2,96,384]{2,1,0:T(8,128)(2,1)S(1)} collective-permute-done((bf16[2,96,384]{2,1,0:T(8,128)(2,1)S(1)}, bf16[2,96,384]{2,1,0:T(8,128)(2,1)S(1)}, u32[]{:S(2)}, u32[]{:S(2)}) %collective-permute-start.8) | collective-permute-done | bytes 147488 | tf_op jit(solution)/shard_map/ppermute | solution.py:342
  27.7 0.8 %last.1 = (bf16[2,96,384]{2,1,0:T(8,128)(2,1)}, f32[2,128]{1,0:T(2,128)}) custom-call(s32[4,8,128]{2,1,0:T(8,128)S(1)} %get-tuple-element.24.sizes_ref, bf16[2,384,384]{2,1,0:T(8,128)(2,1)S(1)} %get-tuple-element.25.masked_ref, f32[2,96,384]{2,1,0:T(8,128)S(1)} %get-tuple-element.42.own_ref, f32[2,96,384]{2,1,0:T(8,128)S(1)} %get-tuple-element.43.before_ref, ...), custom_call_target="tpu_custom_call" | custom-call | bytes 1048576 | tf_op jit(solution)/shard_map/last/pallas_call | solution.py:491
  (2 shorter events, 0.1 us)
Async XLA Ops:
  1.6 11.6 %collective-permute-start = (bf16[1,400,384]{2,1,0:T(8,128)(2,1)S(1)}, bf16[1,400,384]{2,1,0:T(8,128)(2,1)S(1)}, u32[]{:S(2)}, u32[]{:S(2)}) collective-permute-start(bf16[1,400,384]{2,1,0:T(8,128)(2,1)S(1)} %head.1), channel_id=1, source_target_pairs={{0,12},{4,0},{8,4},{12,8},{1,13},{5,1},{9,5},{13,9},{2,14},{6,2},{... | collective-permute-start | bytes 921608 | tf_op jit(solution)/shard_map/ppermute | solution.py:342
  12.8 1.7 %collective-permute-start.2 = (bf16[2,208,384]{2,1,0:T(8,128)(2,1)S(1)}, bf16[2,208,384]{2,1,0:T(8,128)(2,1)S(1)}, u32[]{:S(2)}, u32[]{:S(2)}) collective-permute-start(bf16[2,208,384]{2,1,0:T(8,128)(2,1)S(1)} %get-tuple-element.31), channel_id=1, source_target_pairs={{0,1},{1,0},{2,3},{3,2},{4,5},{5,4},{6,7},{7,6},{8,9},{9,8},{10,11... | collective-permute-start | bytes 958472 | tf_op jit(solution)/shard_map/ppermute | solution.py:342
  13.3 1.7 %collective-permute-start.1 = (bf16[1,400,384]{2,1,0:T(8,128)(2,1)S(1)}, bf16[1,400,384]{2,1,0:T(8,128)(2,1)S(1)}, u32[]{:S(2)}, u32[]{:S(2)}) collective-permute-start(bf16[1,400,384]{2,1,0:T(8,128)(2,1)S(1)} %relay.1.mine_ref), channel_id=1, source_target_pairs={{0,1},{1,0},{2,3},{3,2},{4,5},{5,4},{6,7},{7,6},{8,9},{9,8},{10,11... | collective-permute-start | bytes 921608 | tf_op jit(solution)/shard_map/ppermute | solution.py:342
  14.6 11.6 %collective-permute-start.6 = (bf16[2,208,384]{2,1,0:T(8,128)(2,1)S(1)}, bf16[2,208,384]{2,1,0:T(8,128)(2,1)S(1)}, u32[]{:S(2)}, u32[]{:S(2)}) collective-permute-start(bf16[2,208,384]{2,1,0:T(8,128)(2,1)S(1)} %get-tuple-element.40), channel_id=1, source_target_pairs={{0,4},{1,6},{2,5},{3,7},{4,8},{5,10},{6,9},{7,11},{8,12},{9,14},{1... | collective-permute-start | bytes 958472 | tf_op jit(solution)/shard_map/ppermute | solution.py:446
  19.0 1.4 %collective-permute-start.3 = (bf16[2,96,384]{2,1,0:T(8,128)(2,1)S(1)}, bf16[2,96,384]{2,1,0:T(8,128)(2,1)S(1)}, u32[]{:S(2)}, u32[]{:S(2)}) collective-permute-start(bf16[2,96,384]{2,1,0:T(8,128)(2,1)S(1)} %get-tuple-element.35), channel_id=1, source_target_pairs={{0,1},{1,0},{2,3},{3,2},{4,5},{5,4},{6,7},{7,6},{8,9},{9,8},{10,11... | collective-permute-start | bytes 442376 | tf_op jit(solution)/shard_map/ppermute | solution.py:342
  19.2 1.4 %collective-permute-start.4 = (bf16[2,96,384]{2,1,0:T(8,128)(2,1)S(1)}, bf16[2,96,384]{2,1,0:T(8,128)(2,1)S(1)}, u32[]{:S(2)}, u32[]{:S(2)}) collective-permute-start(bf16[2,96,384]{2,1,0:T(8,128)(2,1)S(1)} %get-tuple-element.36), channel_id=1, source_target_pairs={{0,1},{1,0},{2,3},{3,2},{4,5},{5,4},{6,7},{7,6},{8,9},{9,8},{10,11... | collective-permute-start | bytes 442376 | tf_op jit(solution)/shard_map/ppermute | solution.py:342
  20.7 6.6 %collective-permute-start.7 = (bf16[2,96,384]{2,1,0:T(8,128)(2,1)S(1)}, bf16[2,96,384]{2,1,0:T(8,128)(2,1)S(1)}, u32[]{:S(2)}, u32[]{:S(2)}) collective-permute-start(bf16[2,96,384]{2,1,0:T(8,128)(2,1)S(1)} %get-tuple-element.41), channel_id=1, source_target_pairs={{0,2},{2,0},{1,3},{3,1},{4,6},{6,4},{5,7},{7,5},{8,10},{10,8},{9,1... | collective-permute-start | bytes 442376 | tf_op jit(solution)/shard_map/ppermute | solution.py:342
  22.3 5.0 %collective-permute-start.5 = (f32[1,2,128]{2,1,0:T(2,128)S(1)}, f32[1,2,128]{2,1,0:T(2,128)S(1)}, u32[]{:S(2)}, u32[]{:S(2)}) collective-permute-start(f32[1,2,128]{2,1,0:T(2,128)S(1)} %get-tuple-element.39), channel_id=1, source_target_pairs={{0,8},{4,12},{8,0},{12,4},{1,9},{5,13},{9,1},{13,5},{2,10},{6,14},... | collective-permute-start | bytes 3080 | tf_op jit(solution)/shard_map/ppermute | solution.py:342
  26.2 1.4 %collective-permute-start.8 = (bf16[2,96,384]{2,1,0:T(8,128)(2,1)S(1)}, bf16[2,96,384]{2,1,0:T(8,128)(2,1)S(1)}, u32[]{:S(2)}, u32[]{:S(2)}) collective-permute-start(bf16[2,96,384]{2,1,0:T(8,128)(2,1)S(1)} %get-tuple-element.44), channel_id=1, source_target_pairs={{0,1},{1,0},{2,3},{3,2},{4,5},{5,4},{6,7},{7,6},{8,9},{9,8},{10,11... | collective-permute-start | bytes 442376 | tf_op jit(solution)/shard_map/ppermute | solution.py:342

commit v5 on v4

--- a/solution.py
+++ b/solution.py
@@ -110,27 +110,35 @@
     half, nbasis = payload_ref.shape[0], payload_ref.shape[2]
     at = lax.axis_index("sub") * half
     copies = fetch(
-        [(density_hbm.at[pl.ds(at, half)], payload_ref.at[:, pl.ds(0, nbasis)]), (coords_hbm, coords_ref)], sems
-    )
-    copies[1].wait()
+        [(coords_hbm, coords_ref)]
+        + [
+            (density_hbm.at[pl.ds(at, half), pl.ds(low, 128)], payload_ref.at[:, pl.ds(low, 128)])
+            for low in range(0, nbasis, 128)
+        ],
+        sems,
+    )
+    copies[0].wait()
     for f in range(half):
         rows = [part for d in range(3) for part in thirds(coords_ref[d, pl.ds(at + f, 1), :])]
         rows.append(jnp.zeros((EXTRA - len(rows), nbasis), F32))
         payload_ref[f, nbasis:, :] = jnp.concatenate(rows).astype(BF16)
-    copies[0].wait()
+    for copy in copies[1:]:
+        copy.wait()
 
 
 def right_kernel(
-    size_hbm, first_hbm, second_hbm, count_ref, density_hbm, coupling_hbm, coords_hbm, region_hbm,
-    keep_ref, send_ref, own_ref, factor_ref, masked_ref, ids_ref, sizes_ref, here_ref, sources_ref, *rest,
+    size_hbm, first_hbm, second_hbm, count_ref, payload_ref, density_hbm, coupling_hbm, coords_hbm, region_hbm,
+    keep_ref, send_ref, own_ref, factor_ref, masked_ref, slots_ref, sizes_ref, here_ref, sources_ref, *rest,
 ):
     slab_refs, rest = rest[:4], rest[4:]
-    size_ref, first_ref, second_ref, density_ref, coords_ref, region_ref, total_ref, sems = rest
+    size_ref, first_ref, second_ref, ids_ref, density_ref, coords_ref, region_ref, total_ref, sems = rest
     frag_dev, nbasis, slots = masked_ref.shape[0], masked_ref.shape[1], factor_ref.shape[0]
+    half = payload_ref.shape[0]
+    mine, theirs = lax.axis_index("sub") * half, (1 - lax.axis_index("sub")) * half
     copies = fetch(
         [
             (size_hbm, size_ref), (first_hbm, first_ref), (second_hbm, second_ref),
-            (density_hbm, density_ref), (coords_hbm, coords_ref), (region_hbm, region_ref),
+            (density_hbm.at[pl.ds(theirs, half)], density_ref), (coords_hbm, coords_ref), (region_hbm, region_ref),
         ]
         + [(coupling_hbm.at[s], factor_ref.at[s]) for s in range(slots)],
         sems,
@@ -147,12 +155,13 @@
         second = jnp.clip(second_ref[s] - base, 0, trash - 1)
         ids_ref[s] = first
         ids_ref[slots + s] = second
-        ids_ref[2 * slots + s] = jnp.where(live, first, frag_dev)
-        ids_ref[3 * slots + s] = jnp.where(live, second, trash)
+        ids_ref[2 * slots + s] = jnp.where(live, second, trash)
+        ids_ref[3 * slots + s] = jnp.where(live, first, frag_dev)
     for f in range(2 * frag_dev):
         sizes_ref[f] = jnp.full((8, 128), size_ref[lax.rem(base + f, size_ref.shape[0])], I32)
-    for f in range(frag_dev):
-        masked_ref[f] = live_square(density_ref[f], size_ref[base + f])
+    for f in range(half):
+        masked_ref[mine + f] = live_square(payload_ref[f, :nbasis], size_ref[base + mine + f])
+        masked_ref[theirs + f] = live_square(density_ref[f], size_ref[base + theirs + f])
     sources = [
         (
             charge_row(lambda low, high, f=f: masked_ref[f, low:high, low:high], nbasis),
@@ -160,11 +169,11 @@
         )
         for f in range(frag_dev)
     ]
-    for f in range(frag_dev):
-        rows = [part for d in range(3) for part in thirds(coords_ref[d, f : f + 1, :])]
-        rows.append(sources[f][0])
-        rows.append(jnp.zeros((EXTRA - len(rows), nbasis), F32))
-        sources_ref[f] = jnp.concatenate(rows).astype(BF16)
+    rows = []
+    for charge, place in sources:
+        rows += [part for values in place for part in thirds(values)[:2]] + [charge]
+    rows.append(jnp.zeros((EXTRA - len(rows), nbasis), F32))
+    sources_ref[...] = jnp.concatenate(rows).astype(BF16)
 
     pts_rows = region_ref.shape[0]
     each, block_cols = slab_refs[0].shape[0], slab_refs[0].shape[2]
@@ -198,7 +207,7 @@
         copy.wait()
 
     def add(s, corr):
-        target = ids_ref[3 * slots + s]
+        target = ids_ref[2 * slots + s]
         total_ref[target] = total_ref[target] + corr
 
     pipelined(
@@ -207,16 +216,20 @@
         lambda s, right: dot(right, factor_ref[s]),
         add,
     )
+    for s in range(slots):
+        for k, row in ((1, s), (3, slots + s)):
+            slots_ref[row : row + 1] = jnp.full((1, 128), ids_ref[k * slots + s], I32)
     own_ref[...] = total_ref[:frag_dev]
     by_core(total_ref.at[pl.ds(frag_dev, frag_dev)], 0, keep_ref, send_ref)
     send_ref[:, keep_ref.shape[1] :, :] = jnp.zeros((frag_dev, EXTRA, nbasis), BF16)
 
 
 def left_kernel(
-    ids_ref, sizes_ref, masked_ref, mine_ref, other_ref, own_ref, factor_ref, after_ref,
+    slots_ref, sizes_ref, masked_ref, mine_ref, other_ref, own_ref, factor_ref, after_ref,
     keep_ref, *rest,
 ):
-    send_refs, (all_ref, total_ref) = rest[:-2], rest[-2:]
+    send_refs, (ids_ref, all_ref, total_ref, sems) = rest[:-4], rest[-4:]
+    copies = fetch([(slots_ref, ids_ref)], sems)
     frag_dev, nbasis = masked_ref.shape[0], masked_ref.shape[1]
     slots, half = factor_ref.shape[0], mine_ref.shape[0]
     me = lax.axis_index("sub")
@@ -229,14 +242,15 @@
         all_ref[at] = live_square(other_ref[f, :nbasis], sizes_ref[at, 0:1, 0:1])
     total_ref[:frag_dev] = own_ref[...]
     total_ref[frag_dev] = jnp.zeros_like(total_ref[frag_dev])
+    copies[0].wait()
 
     def add(s, corr):
-        target = ids_ref[2 * slots + s]
+        target = ids_ref[slots + s, 0]
         total_ref[target] = total_ref[target] + corr
 
     pipelined(
         slots,
-        lambda s: dot(factor_ref[s], all_ref[ids_ref[slots + s]]),
+        lambda s: dot(factor_ref[s], all_ref[ids_ref[s, 0]]),
         lambda s, left: dot_t(left, factor_ref[s]),
         add,
     )
@@ -266,31 +280,49 @@
 def next_kernel(keep_ref, recv_ref, sources_ref, *out_refs):
     out_refs, after_ref = out_refs[:-1], out_refs[-1]
     after_ref[...] = jnp.zeros_like(after_ref)
-    rounds = len(out_refs)
-    rows = out_refs[0].shape[1] - EXTRA
+    rounds, frag_dev = len(out_refs), keep_ref.shape[0]
+    rows = keep_ref.shape[1] // rounds
     for j, out_ref in enumerate(out_refs):
         at = at_rows(lax.rem(lax.axis_index("grid") + j, rounds), rows) if rounds > 1 else slice(0, rows)
-        total = keep_ref[:, at, :].astype(F32) + recv_ref[:, at, :].astype(F32)
-        out_ref[:, :rows, :] = total.astype(BF16)
-        out_ref[:, rows:, :] = sources_ref[...]
+        for f in range(frag_dev):
+            total = keep_ref[f, at, :].astype(F32) + recv_ref[f, at, :].astype(F32)
+            out_ref[f * rows : (f + 1) * rows, :] = total.astype(BF16)
+        out_ref[frag_dev * rows :, :] = sources_ref[...]
 
 
 def before_kernel(*refs):
     in_refs, (keep_ref, send_ref) = refs[:-2], refs[-2:]
-    me, rows = lax.axis_index("sub"), keep_ref.shape[1]
-    keep_ref[...] = sum(r[:, at_rows(me, rows), :].astype(F32) for r in in_refs)
-    send_ref[...] = sum(r[:, at_rows(1 - me, rows), :].astype(F32) for r in in_refs).astype(BF16)
-
-
-def middle_kernel(own_ref, home_ref, far_ref, later_ref, prior_ref, *rest):
+    me, (frag_dev, share, _) = lax.axis_index("sub"), keep_ref.shape
+    for f in range(frag_dev):
+        for at, ref in ((me, keep_ref), (1 - me, send_ref)):
+            place = pl.ds(2 * f * share + pl.multiple_of(at * share, share), share)
+            ref[f] = sum(in_ref[place, :].astype(F32) for in_ref in in_refs).astype(ref.dtype)
+
+
+def middle_kernel(own_ref, home_ref, far_ref, around_ref, *rest):
     part_refs, (out_ref, pot_ref) = rest[:-2], rest[-2:]
     out_ref[...] = own_ref[...] + sum(part_ref[...].astype(F32) for part_ref in part_refs)
-    pot_ref[...] = home_ref[...] + far_ref[...] + later_ref[...] + prior_ref[...]
-
-
-def felt(sources, here_ref, out_ref):
+    pot_ref[...] = home_ref[...] + far_ref[...] + around_ref[...]
+
+
+def around_kernel(frag_dev, sizes_ref, mine_ref, other_ref, here_ref, piece_ref, out_ref):
+    half, nbasis = mine_ref.shape[0], mine_ref.shape[2]
+    me, team, teams = lax.axis_index("sub"), lax.axis_index("frag"), lax.axis_size("frag")
+    column = lax.broadcasted_iota(I32, (1, nbasis), 1)
+    sources = []
+    for ref, start in ((mine_ref, me * half), (other_ref, (1 - me) * half)):
+        for f in range(half):
+            charge = charge_row(lambda low, high, ref=ref, f=f: ref[f, low:high, low:high], nbasis)
+            charge = jnp.where(column < sizes_ref[frag_dev + start + f, 0:1, 0:1], charge, 0.0)
+            place = place_rows(ref[f, nbasis:, :].astype(F32))
+            sources.append((lax.rem(team + 1, teams) * frag_dev + start + f, charge, place))
+    extra = piece_ref[piece_ref.shape[0] - EXTRA :, :].astype(F32)
+    for f in range(frag_dev):
+        rows = [extra[7 * f + k : 7 * f + k + 1] for k in range(7)]
+        place = [rows[2 * d] + rows[2 * d + 1] for d in range(3)]
+        sources.append((lax.rem(team + teams - 1, teams) * frag_dev + f, rows[6], place))
     pts_rows, block_cols = here_ref.shape
-    team, row_x = lax.axis_index("frag"), row_places(pts_rows)
+    row_x = row_places(pts_rows)
     totals = [jnp.zeros((1, block_cols), F32) for _ in range(pts_rows)]
     fields = [field(charge, place, team, block_cols, row_x) for _, charge, place in sources]
     for (fragment, _, _), rows in zip(sources, over_lanes(fields, block_cols, pts_rows)):
@@ -298,29 +330,6 @@
             totals[r] = totals[r] + jnp.where(here_ref[r : r + 1, :] != fragment, rows[r], 0.0)
     for r in range(pts_rows):
         out_ref[0, r : r + 1, :] = totals[r]
-
-
-def after_kernel(sizes_ref, mine_ref, other_ref, here_ref, out_ref):
-    half, nbasis = mine_ref.shape[0], mine_ref.shape[2]
-    me, team, teams = lax.axis_index("sub"), lax.axis_index("frag"), lax.axis_size("frag")
-    column = lax.broadcasted_iota(I32, (1, nbasis), 1)
-    sources = []
-    for ref, start in ((mine_ref, me * half), (other_ref, (1 - me) * half)):
-        for f in range(half):
-            charge = charge_row(lambda low, high, ref=ref, f=f: ref[f, low:high, low:high], nbasis)
-            charge = jnp.where(column < sizes_ref[2 * half + start + f, 0:1, 0:1], charge, 0.0)
-            place = place_rows(ref[f, nbasis:, :].astype(F32))
-            sources.append((lax.rem(team + 1, teams) * 2 * half + start + f, charge, place))
-    felt(sources, here_ref, out_ref)
-
-
-def prior_kernel(here_ref, piece_ref, out_ref):
-    frag_dev, team, teams = piece_ref.shape[0], lax.axis_index("frag"), lax.axis_size("frag")
-    sources = []
-    for f in range(frag_dev):
-        extra = piece_ref[f, piece_ref.shape[1] - EXTRA :, :].astype(F32)
-        sources.append((lax.rem(team + teams - 1, teams) * frag_dev + f, extra[9:10], place_rows(extra)))
-    felt(sources, here_ref, out_ref)
 
 
 def last_kernel(scale, sizes_ref, masked_ref, own_ref, before_ref, recv_ref, pot_ref, out_ref, potential_ref):
@@ -392,30 +401,30 @@
         [hbm] * 2,
         shape((half, nbasis + EXTRA, nbasis), BF16),
         vmem,
-        [pltpu.VMEM((3, frag_dev, nbasis), F32), pltpu.SemaphoreType.DMA((2,))],
+        [pltpu.VMEM((3, frag_dev, nbasis), F32), pltpu.SemaphoreType.DMA((1 + nbasis // 128,))],
     )(in_hbm(density), places)
     mine = turned(payload, "frag", -1)
 
-    next_keep, next_send, own_part, factors, masked, ids, sizes, here, sources, *slabs = call(
+    next_keep, next_send, own_part, factors, masked, slot_ids, sizes, here, sources, *slabs = call(
         right_kernel,
         "right",
-        [hbm] * 3 + [smem] + [hbm] * 4,
+        [hbm] * 3 + [smem, vmem] + [hbm] * 4,
         (
             halves, sent_halves, shape((frag_dev,) + square, F32),
             shape((slots,) + square, BF16), shape((frag_dev,) + square, BF16),
-            shape((4 * slots,), I32), shape((2 * frag_dev, 8, 128), I32), shape((pts_rows, block_cols), I32),
-            shape((frag_dev, EXTRA, nbasis), BF16),
+            shape((2 * slots, 128), I32), shape((2 * frag_dev, 8, 128), I32), shape((pts_rows, block_cols), I32),
+            shape((EXTRA, nbasis), BF16),
         ) + (shape((teams // 4, pts_rows, block_cols), F32),) * 4,
-        (vmem,) * 5 + (smem,) + (vmem,) * 7,
+        (vmem,) * 13,
         [
             pltpu.SMEM(basis_size.shape, I32), pltpu.SMEM((slots,), I32), pltpu.SMEM((slots,), I32),
-            pltpu.VMEM(density.shape, BF16), pltpu.VMEM((3, frag_dev, nbasis), F32),
+            pltpu.SMEM((4 * slots,), I32), pltpu.VMEM((half,) + square, BF16), pltpu.VMEM((3, frag_dev, nbasis), F32),
             pltpu.VMEM(grid_region.shape, I32), pltpu.VMEM((2 * frag_dev + 1,) + square, F32),
             pltpu.SemaphoreType.DMA((6 + slots,)),
         ],
         work,
     )(
-        in_hbm(basis_size), in_hbm(pair_first), in_hbm(pair_second), dimer_count, in_hbm(density),
+        in_hbm(basis_size), in_hbm(pair_first), in_hbm(pair_second), dimer_count, payload, in_hbm(density),
         in_hbm(coupling), places, in_hbm(grid_region),
     )
 
@@ -432,7 +441,7 @@
         next_kernel,
         "next_sum",
         [vmem] * 3,
-        [shape((frag_dev, nbasis // grid_size + EXTRA, nbasis), BF16)] * rounds + [shape((8, 128), F32)],
+        [shape((frag_dev * nbasis // grid_size + EXTRA, nbasis), BF16)] * rounds + [shape((8, 128), F32)],
         (vmem,) * (rounds + 1),
     )(next_keep, turned(next_send, "sub", 1), sources)
     for j, value in enumerate(pieces):
@@ -450,12 +459,15 @@
     own_keep, *own_sends = call(
         left_kernel,
         "left",
-        [smem] + [vmem] * 7,
+        [vmem] * 8,
         [shape(by_chip, F32)] + [shape((grid_size, share, nbasis), BF16)] * frag_dev,
         (vmem,) * (1 + frag_dev),
-        [pltpu.VMEM((2 * frag_dev,) + square, BF16), pltpu.VMEM((frag_dev + 1,) + square, F32)],
+        [
+            pltpu.SMEM((2 * slots, 128), I32), pltpu.VMEM((2 * frag_dev,) + square, BF16),
+            pltpu.VMEM((frag_dev + 1,) + square, F32), pltpu.SemaphoreType.DMA((1,)),
+        ],
         work,
-    )(ids, sizes, masked, mine, other, own_part, factors, after)
+    )(slot_ids, sizes, masked, mine, other, own_part, factors, after)
     mine_rows = (frag_dev, share, nbasis)
     own, *parts = call(
         own_sum_kernel,
@@ -467,7 +479,6 @@
     parts = [turned(part, "grid", step) for step, part in enumerate(parts, 1)]
 
     slab = shape((1, pts_rows, block_cols), F32)
-    later = call(after_kernel, "after", [vmem] * 4, slab, vmem)(sizes, mine, other, here)
     before, passed = call(
         before_kernel,
         "before",
@@ -476,16 +487,18 @@
         (vmem,) * 2,
     )(*pieces)
     passed = turned(passed, "sub", 1)
-    prior = call(prior_kernel, "prior", [vmem] * 2, slab, vmem)(here, pieces[0])
+    around = call(functools.partial(around_kernel, frag_dev), "around", [vmem] * 5, slab, vmem)(
+        sizes, mine, other, here, pieces[0]
+    )
     own, pot = call(
         middle_kernel,
         "middle",
-        [vmem] * (5 + len(parts)),
+        [vmem] * (4 + len(parts)),
         (shape(mine_rows, F32), slab),
         (vmem,) * 2,
         (),
         10**10,
-    )(own, home, far, later, prior, *parts)
+    )(own, home, far, around, *parts)
 
     scale = 8.0 / math.sqrt(frag_dev * teams * nbasis)
     return call(

time: 28.7 us -> 28.2 us (0.983)
  Pallas kernels: 12.3 us -> 11.9 us
    pallas_call x6 -> x5, Pallas kernels: 10.4 us -> 9.95 us  [the longest x1 5.3 us: per_device(): call(right_kernel, 'right', [hbm] * 3 + [smem, vmem] + [hbm] * 4, (halves...]
  transfers between devices with their start and end apart: 9 -> 9, of which waited for: 7 -> 7; matrix products, arithmetic and copies ran while one was open for 0% -> 0% of each run, Pallas kernels for 37% -> 36%
where the time goes in v5:
time: 28.2 us; the launch traced here: 28 us
  Pallas kernels  11.9 us (42%)
  starting transfers between devices  11 us (39%)
  waiting for transfers between devices  3.79 us (13%)
  between operations  1.36 us (5%)
    ppermute x8, starting transfers between devices, turned(): lax.ppermute(value, axis, [(s, (s + steps) % count) for s in range(count)])  10.9 us
    pallas_call x1, Pallas kernels, per_device(): call(right_kernel, 'right', [hbm] * 3 + [smem, vmem] + [hbm] * 4, (halves...  5.3 us
    pallas_call x1, Pallas kernels, per_device(): call(left_kernel, 'left', [vmem] * 8, [shape(by_chip, F32)] + [shape((gri...  3.87 us
    ppermute x8, waiting for transfers between devices, turned(): lax.ppermute(value, axis, [(s, (s + steps) % count) for s in range(count)])  3.64 us
    pallas_call x1, Pallas kernels, per_device(): call(head_kernel, 'head', [hbm] * 2, shape((half, nbasis + EXTRA, nbasis)...  1.04 us
    pallas_call x1, Pallas kernels, per_device(): call(functools.partial(last_kernel, scale), 'last', [vmem] * 6, (shape(mi...  0.78 us
    pallas_call x1, Pallas kernels, per_device(): call(functools.partial(around_kernel, frag_dev), 'around', [vmem] * 5, sl...  0.67 us
  transfers between devices with their start and end apart: 9, of which 7 were waited for; matrix products, arithmetic and copies ran while one was open for 0% of the time, Pallas kernels for 36%

profile of v5, /device:TPU:0, one launch (start us, length us, event | category | flops | bytes accessed | tf_op | source)
XLA Modules:
  0.0 28.0 jit_solution(7307113165167068660)
XLA Ops:
  0.6 1.0 %head.1.payload_ref = bf16[1,400,384]{2,1,0:T(8,128)(2,1)S(1)} custom-call(bf16[2,384,384]{2,1,0:T(8,128)(2,1)} %density_hbm.3, f32[3,2,384]{2,1,0:T(2,128)} %bitcast.1), custom_call_target="tpu_custom_call" | custom-call | bytes 1048576 | tf_op jit(solution)/shard_map/head/pallas_call | solution.py:398
  1.7 5.1 %collective-permute-start = (bf16[1,400,384]{2,1,0:T(8,128)(2,1)S(1)}, bf16[1,400,384]{2,1,0:T(8,128)(2,1)S(1)}, u32[]{:S(2)}, u32[]{:S(2)}) collective-permute-start(bf16[1,400,384]{2,1,0:T(8,128)(2,1)S(1)} %head.1.payload_ref), channel_id=1, source_target_pairs={{0,12},{4,0},{8,4},{12,8},{1,13},{5,1},{9,5},{13,9},{2,14},{6,2},{... | collective-permute-start | bytes 921608 | tf_op jit(solution)/shard_map/ppermute | solution.py:351
  7.4 5.3 %right.1 = (bf16[2,192,384]{2,1,0:T(8,128)(2,1)S(1)}, bf16[2,208,384]{2,1,0:T(8,128)(2,1)S(1)}, f32[2,384,384]{2,1,0:T(8,128)S(1)}, bf16[8,384,384]{2,1,0:T(8,12...) custom-call(s32[8]{0:T(128)} %size_hbm.1, ...), custom_call_target="tpu_custom_call" | custom-call | flops 1811939328 | bytes 1048576 | tf_op jit(solution)/shard_map/right/pallas_call | solution.py:408
  12.7 0.1 collective-permute-start.2
  12.8 0.5 %collective-permute-done.in_ref = bf16[1,400,384]{2,1,0:T(8,128)(2,1)S(1)} collective-permute-done((bf16[1,400,384]{2,1,0:T(8,128)(2,1)S(1)}, bf16[1,400,384]{2,1,0:T(8,128)(2,1)S(1)}, u32[]{:S(2)}, u32[]{:S(2)}) %collective-permute-start) | collective-permute-done | bytes 307232 | tf_op jit(solution)/shard_map/ppermute | solution.py:351
  13.3 0.1 collective-permute-start.1
  13.4 1.0 %collective-permute-done.2.recv_ref = bf16[2,208,384]{2,1,0:T(8,128)(2,1)S(1)} collective-permute-done((bf16[2,208,384]{2,1,0:T(8,128)(2,1)S(1)}, bf16[2,208,384]{2,1,0:T(8,128)(2,1)S(1)}, u32[]{:S(2)}, u32[]{:S(2)}) %collective-permute-start.2) | collective-permute-done | bytes 319520 | tf_op jit(solution)/shard_map/ppermute | solution.py:351
  14.4 0.1 next_sum.1
  14.5 0.1 collective-permute-start.6
  14.6 0.4 %collective-permute-done.1.other_ref = bf16[1,400,384]{2,1,0:T(8,128)(2,1)S(1)} collective-permute-done((bf16[1,400,384]{2,1,0:T(8,128)(2,1)S(1)}, bf16[1,400,384]{2,1,0:T(8,128)(2,1)S(1)}, u32[]{:S(2)}, u32[]{:S(2)}) %collective-permute-start.1) | collective-permute-done | bytes 307232 | tf_op jit(solution)/shard_map/ppermute | solution.py:351
  15.0 3.9 %left.1 = (f32[2,2,96,384]{3,2,1,0:T(8,128)S(1)}, bf16[2,96,384]{2,1,0:T(8,128)(2,1)S(1)}, bf16[2,96,384]{2,1,0:T(8,128)(2,1)S(1)}) custom-call(s32[16,128]{1,0:T(8,128)S(1)} %get-tuple-element.26.slots_ref, s32[4,8,128]{2,1,0:T(8,128)S(1)} %get-tuple-element.24.sizes_ref, bf16[2,384,384]{2,1,0:T(8,128)(2,1)S(1)} %get-tuple-element.25.masked_ref, ...), custom_call_target="tpu_custom_call" | custom-call | flops 1811939328 | bytes 1048576 | tf_op jit(solution)/shard_map/left/pallas_call | solution.py:459
  18.9 0.2 collective-permute-start.3
  19.1 0.4 %collective-permute-start.4 = (bf16[2,96,384]{2,1,0:T(8,128)(2,1)S(1)}, bf16[2,96,384]{2,1,0:T(8,128)(2,1)S(1)}, u32[]{:S(2)}, u32[]{:S(2)}) collective-permute-start(bf16[2,96,384]{2,1,0:T(8,128)(2,1)S(1)} %get-tuple-element.36), channel_id=1, source_target_pairs={{0,1},{1,0},{2,3},{3,2},{4,5},{5,4},{6,7},{7,6},{8,9},{9,8},{10,11... | collective-permute-start | bytes 442376 | tf_op jit(solution)/shard_map/ppermute | solution.py:351
  19.5 0.9 %collective-permute-done.3.rest_0_ = bf16[2,96,384]{2,1,0:T(8,128)(2,1)S(1)} collective-permute-done((bf16[2,96,384]{2,1,0:T(8,128)(2,1)S(1)}, bf16[2,96,384]{2,1,0:T(8,128)(2,1)S(1)}, u32[]{:S(2)}, u32[]{:S(2)}) %collective-permute-start.3) | collective-permute-done | bytes 147488 | tf_op jit(solution)/shard_map/ppermute | solution.py:351
  20.3 0.2 collective-permute-done.4.rest_1_
  20.5 0.1 own_sum.1
  20.6 1.6 %collective-permute-start.7 = (bf16[2,96,384]{2,1,0:T(8,128)(2,1)S(1)}, bf16[2,96,384]{2,1,0:T(8,128)(2,1)S(1)}, u32[]{:S(2)}, u32[]{:S(2)}) collective-permute-start(bf16[2,96,384]{2,1,0:T(8,128)(2,1)S(1)} %get-tuple-element.41), channel_id=1, source_target_pairs={{0,2},{2,0},{1,3},{3,1},{4,6},{6,4},{5,7},{7,5},{8,10},{10,8},{9,1... | collective-permute-start | bytes 442376 | tf_op jit(solution)/shard_map/ppermute | solution.py:351
  22.2 3.5 %collective-permute-start.5 = (f32[1,2,128]{2,1,0:T(2,128)S(1)}, f32[1,2,128]{2,1,0:T(2,128)S(1)}, u32[]{:S(2)}, u32[]{:S(2)}) collective-permute-start(f32[1,2,128]{2,1,0:T(2,128)S(1)} %get-tuple-element.39), channel_id=1, source_target_pairs={{0,8},{4,12},{8,0},{12,4},{1,9},{5,13},{9,1},{13,5},{2,10},{6,14},... | collective-permute-start | bytes 3080 | tf_op jit(solution)/shard_map/ppermute | solution.py:351
  25.6 0.1 collective-permute-done.6.piece_ref.refs_0_
  25.8 0.1 collective-permute-start.8
  25.9 0.7 %around.1.around_ref = f32[1,2,128]{2,1,0:T(2,128)S(1)} custom-call(s32[4,8,128]{2,1,0:T(8,128)S(1)} %get-tuple-element.24.sizes_ref, bf16[1,400,384]{2,1,0:T(8,128)(2,1)S(1)} %relay.1.mine_ref, bf16[1,400,384]{2,1,0:T(8,128)(2,1)S(1)} %collective-permute-done.1.other_ref, s32[2,128]{1,0:T(2,128)S(1)} %get-tuple-element.27.here_ref, ...), custom_call_target="tpu_custom_call" | custom-call | bytes 1048576 | tf_op jit(solution)/shard_map/around/pallas_call | solution.py:490
  26.6 0.6 %collective-permute-done.5.far_ref = f32[1,2,128]{2,1,0:T(2,128)S(1)} collective-permute-done((f32[1,2,128]{2,1,0:T(2,128)S(1)}, f32[1,2,128]{2,1,0:T(2,128)S(1)}, u32[]{:S(2)}, u32[]{:S(2)}) %collective-permute-start.5) | collective-permute-done | bytes 1056 | tf_op jit(solution)/shard_map/ppermute | solution.py:351
  27.2 0.0 collective-permute-done.7.rest_0_
  27.2 0.0 collective-permute-done.8.recv_ref
  27.2 0.8 %last.1 = (bf16[2,96,384]{2,1,0:T(8,128)(2,1)}, f32[2,128]{1,0:T(2,128)}) custom-call(s32[4,8,128]{2,1,0:T(8,128)S(1)} %get-tuple-element.24.sizes_ref, bf16[2,384,384]{2,1,0:T(8,128)(2,1)S(1)} %get-tuple-element.25.masked_ref, f32[2,96,384]{2,1,0:T(8,128)S(1)} %get-tuple-element.42.own_ref, f32[2,96,384]{2,1,0:T(8,128)S(1)} %get-tuple-element.43.before_ref, ...), custom_call_target="tpu_custom_call" | custom-call | bytes 1048576 | tf_op jit(solution)/shard_map/last/pallas_call | solution.py:504
  (3 shorter events, 0.1 us)
Async XLA Ops:
  1.7 11.6 %collective-permute-start = (bf16[1,400,384]{2,1,0:T(8,128)(2,1)S(1)}, bf16[1,400,384]{2,1,0:T(8,128)(2,1)S(1)}, u32[]{:S(2)}, u32[]{:S(2)}) collective-permute-start(bf16[1,400,384]{2,1,0:T(8,128)(2,1)S(1)} %head.1.payload_ref), channel_id=1, source_target_pairs={{0,12},{4,0},{8,4},{12,8},{1,13},{5,1},{9,5},{13,9},{2,14},{6,2},{... | collective-permute-start | bytes 921608 | tf_op jit(solution)/shard_map/ppermute | solution.py:351
  12.7 1.7 %collective-permute-start.2 = (bf16[2,208,384]{2,1,0:T(8,128)(2,1)S(1)}, bf16[2,208,384]{2,1,0:T(8,128)(2,1)S(1)}, u32[]{:S(2)}, u32[]{:S(2)}) collective-permute-start(bf16[2,208,384]{2,1,0:T(8,128)(2,1)S(1)} %get-tuple-element.31), channel_id=1, source_target_pairs={{0,1},{1,0},{2,3},{3,2},{4,5},{5,4},{6,7},{7,6},{8,9},{9,8},{10,11... | collective-permute-start | bytes 958472 | tf_op jit(solution)/shard_map/ppermute | solution.py:351
  13.3 1.7 %collective-permute-start.1 = (bf16[1,400,384]{2,1,0:T(8,128)(2,1)S(1)}, bf16[1,400,384]{2,1,0:T(8,128)(2,1)S(1)}, u32[]{:S(2)}, u32[]{:S(2)}) collective-permute-start(bf16[1,400,384]{2,1,0:T(8,128)(2,1)S(1)} %relay.1.mine_ref), channel_id=1, source_target_pairs={{0,1},{1,0},{2,3},{3,2},{4,5},{5,4},{6,7},{7,6},{8,9},{9,8},{10,11... | collective-permute-start | bytes 921608 | tf_op jit(solution)/shard_map/ppermute | solution.py:351
  14.5 11.3 %collective-permute-start.6 = (bf16[400,384]{1,0:T(8,128)(2,1)S(1)}, bf16[400,384]{1,0:T(8,128)(2,1)S(1)}, u32[]{:S(2)}, u32[]{:S(2)}) collective-permute-start(bf16[400,384]{1,0:T(8,128)(2,1)S(1)} %get-tuple-element.40), channel_id=1, source_target_pairs={{0,4},{1,6},{2,5},{3,7},{4,8},{5,10},{6,9},{7,11},{8,12},{9,14},{1... | collective-permute-start | bytes 921608 | tf_op jit(solution)/shard_map/ppermute | solution.py:455
  18.9 1.4 %collective-permute-start.3 = (bf16[2,96,384]{2,1,0:T(8,128)(2,1)S(1)}, bf16[2,96,384]{2,1,0:T(8,128)(2,1)S(1)}, u32[]{:S(2)}, u32[]{:S(2)}) collective-permute-start(bf16[2,96,384]{2,1,0:T(8,128)(2,1)S(1)} %get-tuple-element.35), channel_id=1, source_target_pairs={{0,1},{1,0},{2,3},{3,2},{4,5},{5,4},{6,7},{7,6},{8,9},{9,8},{10,11... | collective-permute-start | bytes 442376 | tf_op jit(solution)/shard_map/ppermute | solution.py:351
  19.1 1.4 %collective-permute-start.4 = (bf16[2,96,384]{2,1,0:T(8,128)(2,1)S(1)}, bf16[2,96,384]{2,1,0:T(8,128)(2,1)S(1)}, u32[]{:S(2)}, u32[]{:S(2)}) collective-permute-start(bf16[2,96,384]{2,1,0:T(8,128)(2,1)S(1)} %get-tuple-element.36), channel_id=1, source_target_pairs={{0,1},{1,0},{2,3},{3,2},{4,5},{5,4},{6,7},{7,6},{8,9},{9,8},{10,11... | collective-permute-start | bytes 442376 | tf_op jit(solution)/shard_map/ppermute | solution.py:351
  20.6 6.6 %collective-permute-start.7 = (bf16[2,96,384]{2,1,0:T(8,128)(2,1)S(1)}, bf16[2,96,384]{2,1,0:T(8,128)(2,1)S(1)}, u32[]{:S(2)}, u32[]{:S(2)}) collective-permute-start(bf16[2,96,384]{2,1,0:T(8,128)(2,1)S(1)} %get-tuple-element.41), channel_id=1, source_target_pairs={{0,2},{2,0},{1,3},{3,1},{4,6},{6,4},{5,7},{7,5},{8,10},{10,8},{9,1... | collective-permute-start | bytes 442376 | tf_op jit(solution)/shard_map/ppermute | solution.py:351
  22.2 5.0 %collective-permute-start.5 = (f32[1,2,128]{2,1,0:T(2,128)S(1)}, f32[1,2,128]{2,1,0:T(2,128)S(1)}, u32[]{:S(2)}, u32[]{:S(2)}) collective-permute-start(f32[1,2,128]{2,1,0:T(2,128)S(1)} %get-tuple-element.39), channel_id=1, source_target_pairs={{0,8},{4,12},{8,0},{12,4},{1,9},{5,13},{9,1},{13,5},{2,10},{6,14},... | collective-permute-start | bytes 3080 | tf_op jit(solution)/shard_map/ppermute | solution.py:351
  25.8 1.4 %collective-permute-start.8 = (bf16[2,96,384]{2,1,0:T(8,128)(2,1)S(1)}, bf16[2,96,384]{2,1,0:T(8,128)(2,1)S(1)}, u32[]{:S(2)}, u32[]{:S(2)}) collective-permute-start(bf16[2,96,384]{2,1,0:T(8,128)(2,1)S(1)} %get-tuple-element.44), channel_id=1, source_target_pairs={{0,1},{1,0},{2,3},{3,2},{4,5},{5,4},{6,7},{7,6},{8,9},{9,8},{10,11... | collective-permute-start | bytes 442376 | tf_op jit(solution)/shard_map/ppermute | solution.py:351

commit v6 on v5

--- a/solution.py
+++ b/solution.py
@@ -190,7 +190,6 @@
             slab_ref[at, r : r + 1, :] = sum(here)
 
     if each == 1:
-        one_block(0, slab_refs[0], 0)
         one_block(2, slab_refs[2], 0)
     else:
 
@@ -199,7 +198,7 @@
             for k, slab_ref in enumerate(slab_refs):
                 one_block(k * each + step, slab_ref, step)
 
-    for k in (1, teams - 1):
+    for k in (0, 1, teams - 1):
         slab_refs[k // each][k % each] = jnp.zeros((pts_rows, block_cols), F32)
     here_ref[...] = region_ref[:, pl.ds(pl.multiple_of(team * block_cols, block_cols), block_cols)]
 
@@ -255,22 +254,17 @@
         add,
     )
     grid_size, _, share, _ = keep_ref.shape
-    for g in range(grid_size):
+    for step in range(grid_size):
+        chip = lax.rem(lax.axis_index("grid") + step, grid_size)
         for f in range(frag_dev):
-            chip = total_ref.at[f, 2 * g * share : 2 * (g + 1) * share]
-            keep_ref[g, f] = chip[at_rows(me, share), :]
-            send_refs[f][g] = chip[at_rows(1 - me, share), :].astype(BF16)
-
-
-def own_sum_kernel(keep_ref, *rest):
-    grid_size, frag_dev, share, nbasis = keep_ref.shape
-    recv_refs, own_ref, part_refs = rest[:frag_dev], rest[frag_dev], rest[frag_dev + 1 :]
-    me = lax.axis_index("grid")
-    for f in range(frag_dev):
-        own_ref[f] = keep_ref[me, f] + recv_refs[f][me].astype(F32)
-        for step, part_ref in enumerate(part_refs, 1):
-            at = lax.rem(me + step, grid_size)
-            part_ref[f] = (keep_ref[at, f] + recv_refs[f][at].astype(F32)).astype(BF16)
+            keep_ref[step, f] = total_ref[f, at_rows(2 * chip + me, share), :]
+            send_refs[step][f] = total_ref[f, at_rows(2 * chip + 1 - me, share), :].astype(BF16)
+
+
+def away_sum_kernel(keep_ref, *refs):
+    count = len(refs) // 2
+    for step, (recv_ref, part_ref) in enumerate(zip(refs[:count], refs[count:]), 1):
+        part_ref[...] = (keep_ref[step] + recv_ref[...].astype(F32)).astype(BF16)
 
 
 def relay_kernel(here_ref, in_ref, out_ref):
@@ -299,13 +293,14 @@
             ref[f] = sum(in_ref[place, :].astype(F32) for in_ref in in_refs).astype(ref.dtype)
 
 
-def middle_kernel(own_ref, home_ref, far_ref, around_ref, *rest):
+def middle_kernel(keep_ref, home_ref, far_ref, around_ref, recv_ref, *rest):
     part_refs, (out_ref, pot_ref) = rest[:-2], rest[-2:]
-    out_ref[...] = own_ref[...] + sum(part_ref[...].astype(F32) for part_ref in part_refs)
+    total = keep_ref[0] + recv_ref[...].astype(F32)
+    out_ref[...] = total + sum(part_ref[...].astype(F32) for part_ref in part_refs)
     pot_ref[...] = home_ref[...] + far_ref[...] + around_ref[...]
 
 
-def around_kernel(frag_dev, sizes_ref, mine_ref, other_ref, here_ref, piece_ref, out_ref):
+def around_kernel(frag_dev, sizes_ref, mine_ref, other_ref, here_ref, sources_ref, piece_ref, out_ref):
     half, nbasis = mine_ref.shape[0], mine_ref.shape[2]
     me, team, teams = lax.axis_index("sub"), lax.axis_index("frag"), lax.axis_size("frag")
     column = lax.broadcasted_iota(I32, (1, nbasis), 1)
@@ -316,11 +311,11 @@
             charge = jnp.where(column < sizes_ref[frag_dev + start + f, 0:1, 0:1], charge, 0.0)
             place = place_rows(ref[f, nbasis:, :].astype(F32))
             sources.append((lax.rem(team + 1, teams) * frag_dev + start + f, charge, place))
-    extra = piece_ref[piece_ref.shape[0] - EXTRA :, :].astype(F32)
-    for f in range(frag_dev):
-        rows = [extra[7 * f + k : 7 * f + k + 1] for k in range(7)]
-        place = [rows[2 * d] + rows[2 * d + 1] for d in range(3)]
-        sources.append((lax.rem(team + teams - 1, teams) * frag_dev + f, rows[6], place))
+    for whose, extra in ((team, sources_ref[...]), (team + teams - 1, piece_ref[piece_ref.shape[0] - EXTRA :, :])):
+        for f in range(frag_dev):
+            rows = [extra[7 * f + k : 7 * f + k + 1].astype(F32) for k in range(7)]
+            place = [rows[2 * d] + rows[2 * d + 1] for d in range(3)]
+            sources.append((lax.rem(whose, teams) * frag_dev + f, rows[6], place))
     pts_rows, block_cols = here_ref.shape
     row_x = row_places(pts_rows)
     totals = [jnp.zeros((1, block_cols), F32) for _ in range(pts_rows)]
@@ -460,8 +455,8 @@
         left_kernel,
         "left",
         [vmem] * 8,
-        [shape(by_chip, F32)] + [shape((grid_size, share, nbasis), BF16)] * frag_dev,
-        (vmem,) * (1 + frag_dev),
+        [shape(by_chip, F32)] + [shape((frag_dev, share, nbasis), BF16)] * grid_size,
+        (vmem,) * (1 + grid_size),
         [
             pltpu.SMEM((2 * slots, 128), I32), pltpu.VMEM((2 * frag_dev,) + square, BF16),
             pltpu.VMEM((frag_dev + 1,) + square, F32), pltpu.SemaphoreType.DMA((1,)),
@@ -469,13 +464,14 @@
         work,
     )(slot_ids, sizes, masked, mine, other, own_part, factors, after)
     mine_rows = (frag_dev, share, nbasis)
-    own, *parts = call(
-        own_sum_kernel,
-        "own_sum",
-        [vmem] * (1 + frag_dev),
-        [shape(mine_rows, F32)] + [shape(mine_rows, BF16)] * (grid_size - 1),
-        (vmem,) * grid_size,
-    )(own_keep, *[turned(value, "sub", 1) for value in own_sends])
+    own_recv, *away_recvs = [turned(value, "sub", 1) for value in own_sends]
+    parts = call(
+        away_sum_kernel,
+        "away_sum",
+        [vmem] * grid_size,
+        [shape(mine_rows, BF16)] * (grid_size - 1),
+        (vmem,) * (grid_size - 1),
+    )(own_keep, *away_recvs)
     parts = [turned(part, "grid", step) for step, part in enumerate(parts, 1)]
 
     slab = shape((1, pts_rows, block_cols), F32)
@@ -487,18 +483,18 @@
         (vmem,) * 2,
     )(*pieces)
     passed = turned(passed, "sub", 1)
-    around = call(functools.partial(around_kernel, frag_dev), "around", [vmem] * 5, slab, vmem)(
-        sizes, mine, other, here, pieces[0]
+    around = call(functools.partial(around_kernel, frag_dev), "around", [vmem] * 6, slab, vmem)(
+        sizes, mine, other, here, sources, pieces[0]
     )
     own, pot = call(
         middle_kernel,
         "middle",
-        [vmem] * (4 + len(parts)),
+        [vmem] * (5 + len(parts)),
         (shape(mine_rows, F32), slab),
         (vmem,) * 2,
         (),
         10**10,
-    )(own, home, far, around, *parts)
+    )(own_keep, home, far, around, own_recv, *parts)
 
     scale = 8.0 / math.sqrt(frag_dev * teams * nbasis)
     return call(

time: 28.2 us -> 28.2 us (level)
    ppermute x8, waiting for transfers between devices: 3.64 us -> 3.3 us  [turned(): lax.ppermute(value, axis, [(s, (s + steps) % count) for s in range(count)])]
where the time goes in v6:
time: 28.2 us; the launch traced here: 28 us
  Pallas kernels  12 us (43%)
  starting transfers between devices  11 us (39%)
  waiting for transfers between devices  3.68 us (13%)
  between operations  1.36 us (5%)
    ppermute x8, starting transfers between devices, turned(): lax.ppermute(value, axis, [(s, (s + steps) % count) for s in range(count)])  10.9 us
    pallas_call x1, Pallas kernels, per_device(): call(right_kernel, 'right', [hbm] * 3 + [smem, vmem] + [hbm] * 4, (halves...  5.16 us
    pallas_call x1, Pallas kernels, per_device(): call(left_kernel, 'left', [vmem] * 8, [shape(by_chip, F32)] + [shape((fra...  3.87 us
    ppermute x8, waiting for transfers between devices, turned(): lax.ppermute(value, axis, [(s, (s + steps) % count) for s in range(count)])  3.3 us
    pallas_call x1, Pallas kernels, per_device(): call(head_kernel, 'head', [hbm] * 2, shape((half, nbasis + EXTRA, nbasis)...  1.04 us
    pallas_call x1, Pallas kernels, per_device(): call(functools.partial(around_kernel, frag_dev), 'around', [vmem] * 6, sl...  0.92 us
    pallas_call x1, Pallas kernels, per_device(): call(functools.partial(last_kernel, scale), 'last', [vmem] * 6, (shape(mi...  0.78 us
  transfers between devices with their start and end apart: 9, of which 7 were waited for; matrix products, arithmetic and copies ran while one was open for 0% of the time, Pallas kernels for 36%

profile of v6, /device:TPU:0, one launch (start us, length us, event | category | flops | bytes accessed | tf_op | source)
XLA Modules:
  0.0 28.0 jit_solution(14934527449423811366)
XLA Ops:
  0.6 1.0 %head.1.payload_ref = bf16[1,400,384]{2,1,0:T(8,128)(2,1)S(1)} custom-call(bf16[2,384,384]{2,1,0:T(8,128)(2,1)} %density_hbm.3, f32[3,2,384]{2,1,0:T(2,128)} %bitcast.1), custom_call_target="tpu_custom_call" | custom-call | bytes 1048576 | tf_op jit(solution)/shard_map/head/pallas_call | solution.py:393
  1.7 5.1 %collective-permute-start = (bf16[1,400,384]{2,1,0:T(8,128)(2,1)S(1)}, bf16[1,400,384]{2,1,0:T(8,128)(2,1)S(1)}, u32[]{:S(2)}, u32[]{:S(2)}) collective-permute-start(bf16[1,400,384]{2,1,0:T(8,128)(2,1)S(1)} %head.1.payload_ref), channel_id=1, source_target_pairs={{0,12},{4,0},{8,4},{12,8},{1,13},{5,1},{9,5},{13,9},{2,14},{6,2},{... | collective-permute-start | bytes 921608 | tf_op jit(solution)/shard_map/ppermute | solution.py:346
  7.4 5.2 %right.1 = (bf16[2,192,384]{2,1,0:T(8,128)(2,1)S(1)}, bf16[2,208,384]{2,1,0:T(8,128)(2,1)S(1)}, f32[2,384,384]{2,1,0:T(8,128)S(1)}, bf16[8,384,384]{2,1,0:T(8,12...) custom-call(s32[8]{0:T(128)} %size_hbm.1, ...), custom_call_target="tpu_custom_call" | custom-call | flops 1811939328 | bytes 1048576 | tf_op jit(solution)/shard_map/right/pallas_call | solution.py:403
  12.6 0.1 collective-permute-start.2
  12.7 0.6 %collective-permute-done.in_ref = bf16[1,400,384]{2,1,0:T(8,128)(2,1)S(1)} collective-permute-done((bf16[1,400,384]{2,1,0:T(8,128)(2,1)S(1)}, bf16[1,400,384]{2,1,0:T(8,128)(2,1)S(1)}, u32[]{:S(2)}, u32[]{:S(2)}) %collective-permute-start) | collective-permute-done | bytes 307232 | tf_op jit(solution)/shard_map/ppermute | solution.py:346
  13.3 0.1 collective-permute-start.1
  13.4 0.9 %collective-permute-done.2.recv_ref = bf16[2,208,384]{2,1,0:T(8,128)(2,1)S(1)} collective-permute-done((bf16[2,208,384]{2,1,0:T(8,128)(2,1)S(1)}, bf16[2,208,384]{2,1,0:T(8,128)(2,1)S(1)}, u32[]{:S(2)}, u32[]{:S(2)}) %collective-permute-start.2) | collective-permute-done | bytes 319520 | tf_op jit(solution)/shard_map/ppermute | solution.py:346
  14.3 0.1 next_sum.1
  14.4 0.1 collective-permute-start.4
  14.4 0.6 %collective-permute-done.1.other_ref = bf16[1,400,384]{2,1,0:T(8,128)(2,1)S(1)} collective-permute-done((bf16[1,400,384]{2,1,0:T(8,128)(2,1)S(1)}, bf16[1,400,384]{2,1,0:T(8,128)(2,1)S(1)}, u32[]{:S(2)}, u32[]{:S(2)}) %collective-permute-start.1) | collective-permute-done | bytes 307232 | tf_op jit(solution)/shard_map/ppermute | solution.py:346
  15.0 3.9 %left.1 = (f32[2,2,96,384]{3,2,1,0:T(8,128)S(1)}, bf16[2,96,384]{2,1,0:T(8,128)(2,1)S(1)}, bf16[2,96,384]{2,1,0:T(8,128)(2,1)S(1)}) custom-call(s32[16,128]{1,0:T(8,128)S(1)} %get-tuple-element.24.slots_ref, s32[4,8,128]{2,1,0:T(8,128)S(1)} %get-tuple-element.22.sizes_ref, bf16[2,384,384]{2,1,0:T(8,128)(2,1)S(1)} %get-tuple-element.23.masked_ref, ...), custom_call_target="tpu_custom_call" | custom-call | flops 1811939328 | bytes 1048576 | tf_op jit(solution)/shard_map/left/pallas_call | solution.py:454
  18.9 0.2 collective-permute-start.6
  19.1 0.4 %collective-permute-start.5 = (bf16[2,96,384]{2,1,0:T(8,128)(2,1)S(1)}, bf16[2,96,384]{2,1,0:T(8,128)(2,1)S(1)}, u32[]{:S(2)}, u32[]{:S(2)}) collective-permute-start(bf16[2,96,384]{2,1,0:T(8,128)(2,1)S(1)} %get-tuple-element.36), channel_id=1, source_target_pairs={{0,1},{1,0},{2,3},{3,2},{4,5},{5,4},{6,7},{7,6},{8,9},{9,8},{10,11... | collective-permute-start | bytes 442376 | tf_op jit(solution)/shard_map/ppermute | solution.py:346
  19.5 0.9 %collective-permute-done.6.refs_0_ = bf16[2,96,384]{2,1,0:T(8,128)(2,1)S(1)} collective-permute-done((bf16[2,96,384]{2,1,0:T(8,128)(2,1)S(1)}, bf16[2,96,384]{2,1,0:T(8,128)(2,1)S(1)}, u32[]{:S(2)}, u32[]{:S(2)}) %collective-permute-start.6) | collective-permute-done | bytes 147488 | tf_op jit(solution)/shard_map/ppermute | solution.py:346
  20.4 1.6 %collective-permute-start.7 = (bf16[2,96,384]{2,1,0:T(8,128)(2,1)S(1)}, bf16[2,96,384]{2,1,0:T(8,128)(2,1)S(1)}, u32[]{:S(2)}, u32[]{:S(2)}) collective-permute-start(bf16[2,96,384]{2,1,0:T(8,128)(2,1)S(1)} %away_sum.1), channel_id=1, source_target_pairs={{0,2},{2,0},{1,3},{3,1},{4,6},{6,4},{5,7},{7,5},{8,10},{10,8},{9,1... | collective-permute-start | bytes 442376 | tf_op jit(solution)/shard_map/ppermute | solution.py:346
  21.9 3.5 %collective-permute-start.3 = (f32[1,2,128]{2,1,0:T(2,128)S(1)}, f32[1,2,128]{2,1,0:T(2,128)S(1)}, u32[]{:S(2)}, u32[]{:S(2)}) collective-permute-start(f32[1,2,128]{2,1,0:T(2,128)S(1)} %get-tuple-element.34), channel_id=1, source_target_pairs={{0,8},{4,12},{8,0},{12,4},{1,9},{5,13},{9,1},{13,5},{2,10},{6,14},... | collective-permute-start | bytes 3080 | tf_op jit(solution)/shard_map/ppermute | solution.py:346
  25.4 0.4 %collective-permute-done.4.piece_ref.refs_0_ = bf16[400,384]{1,0:T(8,128)(2,1)S(1)} collective-permute-done((bf16[400,384]{1,0:T(8,128)(2,1)S(1)}, bf16[400,384]{1,0:T(8,128)(2,1)S(1)}, u32[]{:S(2)}, u32[]{:S(2)}) %collective-permute-start.4) | collective-permute-done | bytes 307232 | tf_op jit(solution)/shard_map/ppermute | solution.py:450
  25.8 0.1 collective-permute-start.8
  25.9 0.9 %around.1.around_ref = f32[1,2,128]{2,1,0:T(2,128)S(1)} custom-call(s32[4,8,128]{2,1,0:T(8,128)S(1)} %get-tuple-element.22.sizes_ref, bf16[1,400,384]{2,1,0:T(8,128)(2,1)S(1)} %relay.1.mine_ref, bf16[1,400,384]{2,1,0:T(8,128)(2,1)S(1)} %collective-permute-done.1.other_ref, s32[2,128]{1,0:T(2,128)S(1)} %get-tuple-element.25.here_ref, ...), custom_call_target="tpu_custom_call" | custom-call | bytes 1048576 | tf_op jit(solution)/shard_map/around/pallas_call | solution.py:486
  26.8 0.1 collective-permute-done.3.far_ref
  26.9 0.0 collective-permute-done.5.recv_ref
  26.9 0.0 collective-permute-done.7.rest_0_
  26.9 0.1 middle.1
  27.0 0.2 collective-permute-done.8.recv_ref
  27.2 0.8 %last.1 = (bf16[2,96,384]{2,1,0:T(8,128)(2,1)}, f32[2,128]{1,0:T(2,128)}) custom-call(s32[4,8,128]{2,1,0:T(8,128)S(1)} %get-tuple-element.22.sizes_ref, bf16[2,384,384]{2,1,0:T(8,128)(2,1)S(1)} %get-tuple-element.23.masked_ref, f32[2,96,384]{2,1,0:T(8,128)S(1)} %get-tuple-element.38.own_ref, f32[2,96,384]{2,1,0:T(8,128)S(1)} %get-tuple-element.39.before_ref, ...), custom_call_target="tpu_custom_call" | custom-call | bytes 1048576 | tf_op jit(solution)/shard_map/last/pallas_call | solution.py:500
  (3 shorter events, 0.1 us)
Async XLA Ops:
  1.7 11.6 %collective-permute-start = (bf16[1,400,384]{2,1,0:T(8,128)(2,1)S(1)}, bf16[1,400,384]{2,1,0:T(8,128)(2,1)S(1)}, u32[]{:S(2)}, u32[]{:S(2)}) collective-permute-start(bf16[1,400,384]{2,1,0:T(8,128)(2,1)S(1)} %head.1.payload_ref), channel_id=1, source_target_pairs={{0,12},{4,0},{8,4},{12,8},{1,13},{5,1},{9,5},{13,9},{2,14},{6,2},{... | collective-permute-start | bytes 921608 | tf_op jit(solution)/shard_map/ppermute | solution.py:346
  12.6 1.7 %collective-permute-start.2 = (bf16[2,208,384]{2,1,0:T(8,128)(2,1)S(1)}, bf16[2,208,384]{2,1,0:T(8,128)(2,1)S(1)}, u32[]{:S(2)}, u32[]{:S(2)}) collective-permute-start(bf16[2,208,384]{2,1,0:T(8,128)(2,1)S(1)} %get-tuple-element.29), channel_id=1, source_target_pairs={{0,1},{1,0},{2,3},{3,2},{4,5},{5,4},{6,7},{7,6},{8,9},{9,8},{10,11... | collective-permute-start | bytes 958472 | tf_op jit(solution)/shard_map/ppermute | solution.py:346
  13.3 1.7 %collective-permute-start.1 = (bf16[1,400,384]{2,1,0:T(8,128)(2,1)S(1)}, bf16[1,400,384]{2,1,0:T(8,128)(2,1)S(1)}, u32[]{:S(2)}, u32[]{:S(2)}) collective-permute-start(bf16[1,400,384]{2,1,0:T(8,128)(2,1)S(1)} %relay.1.mine_ref), channel_id=1, source_target_pairs={{0,1},{1,0},{2,3},{3,2},{4,5},{5,4},{6,7},{7,6},{8,9},{9,8},{10,11... | collective-permute-start | bytes 921608 | tf_op jit(solution)/shard_map/ppermute | solution.py:346
  14.4 11.4 %collective-permute-start.4 = (bf16[400,384]{1,0:T(8,128)(2,1)S(1)}, bf16[400,384]{1,0:T(8,128)(2,1)S(1)}, u32[]{:S(2)}, u32[]{:S(2)}) collective-permute-start(bf16[400,384]{1,0:T(8,128)(2,1)S(1)} %get-tuple-element.35), channel_id=1, source_target_pairs={{0,4},{1,6},{2,5},{3,7},{4,8},{5,10},{6,9},{7,11},{8,12},{9,14},{1... | collective-permute-start | bytes 921608 | tf_op jit(solution)/shard_map/ppermute | solution.py:450
  18.9 1.4 %collective-permute-start.6 = (bf16[2,96,384]{2,1,0:T(8,128)(2,1)S(1)}, bf16[2,96,384]{2,1,0:T(8,128)(2,1)S(1)}, u32[]{:S(2)}, u32[]{:S(2)}) collective-permute-start(bf16[2,96,384]{2,1,0:T(8,128)(2,1)S(1)} %get-tuple-element.37), channel_id=1, source_target_pairs={{0,1},{1,0},{2,3},{3,2},{4,5},{5,4},{6,7},{7,6},{8,9},{9,8},{10,11... | collective-permute-start | bytes 442376 | tf_op jit(solution)/shard_map/ppermute | solution.py:346
  19.1 7.8 %collective-permute-start.5 = (bf16[2,96,384]{2,1,0:T(8,128)(2,1)S(1)}, bf16[2,96,384]{2,1,0:T(8,128)(2,1)S(1)}, u32[]{:S(2)}, u32[]{:S(2)}) collective-permute-start(bf16[2,96,384]{2,1,0:T(8,128)(2,1)S(1)} %get-tuple-element.36), channel_id=1, source_target_pairs={{0,1},{1,0},{2,3},{3,2},{4,5},{5,4},{6,7},{7,6},{8,9},{9,8},{10,11... | collective-permute-start | bytes 442376 | tf_op jit(solution)/shard_map/ppermute | solution.py:346
  20.4 6.6 %collective-permute-start.7 = (bf16[2,96,384]{2,1,0:T(8,128)(2,1)S(1)}, bf16[2,96,384]{2,1,0:T(8,128)(2,1)S(1)}, u32[]{:S(2)}, u32[]{:S(2)}) collective-permute-start(bf16[2,96,384]{2,1,0:T(8,128)(2,1)S(1)} %away_sum.1), channel_id=1, source_target_pairs={{0,2},{2,0},{1,3},{3,1},{4,6},{6,4},{5,7},{7,5},{8,10},{10,8},{9,1... | collective-permute-start | bytes 442376 | tf_op jit(solution)/shard_map/ppermute | solution.py:346
  21.9 5.0 %collective-permute-start.3 = (f32[1,2,128]{2,1,0:T(2,128)S(1)}, f32[1,2,128]{2,1,0:T(2,128)S(1)}, u32[]{:S(2)}, u32[]{:S(2)}) collective-permute-start(f32[1,2,128]{2,1,0:T(2,128)S(1)} %get-tuple-element.34), channel_id=1, source_target_pairs={{0,8},{4,12},{8,0},{12,4},{1,9},{5,13},{9,1},{13,5},{2,10},{6,14},... | collective-permute-start | bytes 3080 | tf_op jit(solution)/shard_map/ppermute | solution.py:346
  25.8 1.4 %collective-permute-start.8 = (bf16[2,96,384]{2,1,0:T(8,128)(2,1)S(1)}, bf16[2,96,384]{2,1,0:T(8,128)(2,1)S(1)}, u32[]{:S(2)}, u32[]{:S(2)}) collective-permute-start(bf16[2,96,384]{2,1,0:T(8,128)(2,1)S(1)} %get-tuple-element.40), channel_id=1, source_target_pairs={{0,1},{1,0},{2,3},{3,2},{4,5},{5,4},{6,7},{7,6},{8,9},{9,8},{10,11... | collective-permute-start | bytes 442376 | tf_op jit(solution)/shard_map/ppermute | solution.py:346

commit v7 on v6

--- a/solution.py
+++ b/solution.py
@@ -239,9 +239,9 @@
         all_ref[at] = live_square(mine_ref[f, :nbasis], sizes_ref[at, 0:1, 0:1])
         at = frag_dev + (1 - me) * half + f
         all_ref[at] = live_square(other_ref[f, :nbasis], sizes_ref[at, 0:1, 0:1])
+    copies[0].wait()
     total_ref[:frag_dev] = own_ref[...]
     total_ref[frag_dev] = jnp.zeros_like(total_ref[frag_dev])
-    copies[0].wait()
 
     def add(s, corr):
         target = ids_ref[slots + s, 0]
@@ -293,10 +293,9 @@
             ref[f] = sum(in_ref[place, :].astype(F32) for in_ref in in_refs).astype(ref.dtype)
 
 
-def middle_kernel(keep_ref, home_ref, far_ref, around_ref, recv_ref, *rest):
+def middle_kernel(keep_ref, home_ref, far_ref, around_ref, *rest):
     part_refs, (out_ref, pot_ref) = rest[:-2], rest[-2:]
-    total = keep_ref[0] + recv_ref[...].astype(F32)
-    out_ref[...] = total + sum(part_ref[...].astype(F32) for part_ref in part_refs)
+    out_ref[...] = keep_ref[0] + sum(part_ref[...].astype(F32) for part_ref in part_refs)
     pot_ref[...] = home_ref[...] + far_ref[...] + around_ref[...]
 
 
@@ -327,7 +326,9 @@
         out_ref[0, r : r + 1, :] = totals[r]
 
 
-def last_kernel(scale, sizes_ref, masked_ref, own_ref, before_ref, recv_ref, pot_ref, out_ref, potential_ref):
+def last_kernel(
+    scale, sizes_ref, masked_ref, own_ref, too_ref, before_ref, recv_ref, pot_ref, out_ref, potential_ref
+):
     frag_dev, share, nbasis = out_ref.shape
     member = lax.axis_index("grid") * lax.axis_size("sub") + lax.axis_index("sub")
     row_start = pl.multiple_of(member * share, share)
@@ -335,7 +336,7 @@
     cols = lax.broadcasted_iota(I32, (share, nbasis), 1)
     for f in range(frag_dev):
         size = sizes_ref[f, 0:1, 0:1]
-        correction = own_ref[f] + before_ref[f] + recv_ref[f].astype(F32)
+        correction = own_ref[f] + before_ref[f] + (recv_ref[f].astype(F32) + too_ref[f].astype(F32))
         correction = jnp.where((rows < size) & (cols < size), correction, 0.0)
         out_ref[f] = (masked_ref[f, pl.ds(row_start, share), :].astype(F32) + correction).astype(BF16)
     potential_ref[...] = pot_ref[0] * scale
@@ -489,21 +490,21 @@
     own, pot = call(
         middle_kernel,
         "middle",
-        [vmem] * (5 + len(parts)),
+        [vmem] * (4 + len(parts)),
         (shape(mine_rows, F32), slab),
         (vmem,) * 2,
         (),
         10**10,
-    )(own_keep, home, far, around, own_recv, *parts)
+    )(own_keep, home, far, around, *parts)
 
     scale = 8.0 / math.sqrt(frag_dev * teams * nbasis)
     return call(
         functools.partial(last_kernel, scale),
         "last",
-        [vmem] * 6,
+        [vmem] * 7,
         (shape(mine_rows, BF16), shape((pts_rows, block_cols), F32)),
         (vmem,) * 2,
-    )(sizes, masked, own, before, passed, pot)
+    )(sizes, masked, own, own_recv, before, passed, pot)
 
 
 def solution(mesh):

time: 28.2 us -> 28.3 us (level)
  starting transfers between devices: 11 us -> 10.7 us
  transfers between devices with their start and end apart: 9 -> 9, of which waited for: 7 -> 6; matrix products, arithmetic and copies ran while one was open for 0% -> 0% of each run, Pallas kernels for 36% -> 36%
where the time goes in v7:
time: 28.3 us; the launch traced here: 28.1 us
  Pallas kernels  12 us (42%)
  starting transfers between devices  10.7 us (38%)
  waiting for transfers between devices  3.95 us (14%)
  between operations  1.36 us (5%)
    ppermute x8, starting transfers between devices, turned(): lax.ppermute(value, axis, [(s, (s + steps) % count) for s in range(count)])  10.7 us
    pallas_call x1, Pallas kernels, per_device(): call(right_kernel, 'right', [hbm] * 3 + [smem, vmem] + [hbm] * 4, (halves...  5.16 us
    pallas_call x1, Pallas kernels, per_device(): call(left_kernel, 'left', [vmem] * 8, [shape(by_chip, F32)] + [shape((fra...  3.86 us
    ppermute x8, waiting for transfers between devices, turned(): lax.ppermute(value, axis, [(s, (s + steps) % count) for s in range(count)])  3.57 us
    pallas_call x1, Pallas kernels, per_device(): call(head_kernel, 'head', [hbm] * 2, shape((half, nbasis + EXTRA, nbasis)...  1.04 us
    pallas_call x1, Pallas kernels, per_device(): call(functools.partial(around_kernel, frag_dev), 'around', [vmem] * 6, sl...  0.92 us
    pallas_call x1, Pallas kernels, per_device(): call(functools.partial(last_kernel, scale), 'last', [vmem] * 7, (shape(mi...  0.81 us
  transfers between devices with their start and end apart: 9, of which 6 were waited for; matrix products, arithmetic and copies ran while one was open for 0% of the time, Pallas kernels for 36%

profile of v7, /device:TPU:0, one launch (start us, length us, event | category | flops | bytes accessed | tf_op | source)
XLA Modules:
  0.0 28.1 jit_solution(7957287289145300387)
XLA Ops:
  0.6 1.0 %head.1.payload_ref = bf16[1,400,384]{2,1,0:T(8,128)(2,1)S(1)} custom-call(bf16[2,384,384]{2,1,0:T(8,128)(2,1)} %density_hbm.3, f32[3,2,384]{2,1,0:T(2,128)} %bitcast.1), custom_call_target="tpu_custom_call" | custom-call | bytes 1048576 | tf_op jit(solution)/shard_map/head/pallas_call | solution.py:394
  1.7 5.1 %collective-permute-start = (bf16[1,400,384]{2,1,0:T(8,128)(2,1)S(1)}, bf16[1,400,384]{2,1,0:T(8,128)(2,1)S(1)}, u32[]{:S(2)}, u32[]{:S(2)}) collective-permute-start(bf16[1,400,384]{2,1,0:T(8,128)(2,1)S(1)} %head.1.payload_ref), channel_id=1, source_target_pairs={{0,12},{4,0},{8,4},{12,8},{1,13},{5,1},{9,5},{13,9},{2,14},{6,2},{... | collective-permute-start | bytes 921608 | tf_op jit(solution)/shard_map/ppermute | solution.py:347
  7.4 5.2 %right.1 = (bf16[2,192,384]{2,1,0:T(8,128)(2,1)S(1)}, bf16[2,208,384]{2,1,0:T(8,128)(2,1)S(1)}, f32[2,384,384]{2,1,0:T(8,128)S(1)}, bf16[8,384,384]{2,1,0:T(8,12...) custom-call(s32[8]{0:T(128)} %size_hbm.1, ...), custom_call_target="tpu_custom_call" | custom-call | flops 1811939328 | bytes 1048576 | tf_op jit(solution)/shard_map/right/pallas_call | solution.py:404
  12.6 0.1 collective-permute-start.2
  12.7 0.6 %collective-permute-done.in_ref = bf16[1,400,384]{2,1,0:T(8,128)(2,1)S(1)} collective-permute-done((bf16[1,400,384]{2,1,0:T(8,128)(2,1)S(1)}, bf16[1,400,384]{2,1,0:T(8,128)(2,1)S(1)}, u32[]{:S(2)}, u32[]{:S(2)}) %collective-permute-start) | collective-permute-done | bytes 307232 | tf_op jit(solution)/shard_map/ppermute | solution.py:347
  13.3 0.1 collective-permute-start.1
  13.4 0.9 %collective-permute-done.2.recv_ref = bf16[2,208,384]{2,1,0:T(8,128)(2,1)S(1)} collective-permute-done((bf16[2,208,384]{2,1,0:T(8,128)(2,1)S(1)}, bf16[2,208,384]{2,1,0:T(8,128)(2,1)S(1)}, u32[]{:S(2)}, u32[]{:S(2)}) %collective-permute-start.2) | collective-permute-done | bytes 319520 | tf_op jit(solution)/shard_map/ppermute | solution.py:347
  14.3 0.1 next_sum.1
  14.4 0.1 collective-permute-start.4
  14.4 0.6 %collective-permute-done.1.other_ref = bf16[1,400,384]{2,1,0:T(8,128)(2,1)S(1)} collective-permute-done((bf16[1,400,384]{2,1,0:T(8,128)(2,1)S(1)}, bf16[1,400,384]{2,1,0:T(8,128)(2,1)S(1)}, u32[]{:S(2)}, u32[]{:S(2)}) %collective-permute-start.1) | collective-permute-done | bytes 307232 | tf_op jit(solution)/shard_map/ppermute | solution.py:347
  15.0 3.9 %left.1 = (f32[2,2,96,384]{3,2,1,0:T(8,128)S(1)}, bf16[2,96,384]{2,1,0:T(8,128)(2,1)S(1)}, bf16[2,96,384]{2,1,0:T(8,128)(2,1)S(1)}) custom-call(s32[16,128]{1,0:T(8,128)S(1)} %get-tuple-element.24.slots_ref, s32[4,8,128]{2,1,0:T(8,128)S(1)} %get-tuple-element.22.sizes_ref, bf16[2,384,384]{2,1,0:T(8,128)(2,1)S(1)} %get-tuple-element.23.masked_ref, ...), custom_call_target="tpu_custom_call" | custom-call | flops 1811939328 | bytes 1048576 | tf_op jit(solution)/shard_map/left/pallas_call | solution.py:455
  18.9 0.2 collective-permute-start.5
  19.1 1.2 %collective-permute-done.5.refs_0_ = bf16[2,96,384]{2,1,0:T(8,128)(2,1)S(1)} collective-permute-done((bf16[2,96,384]{2,1,0:T(8,128)(2,1)S(1)}, bf16[2,96,384]{2,1,0:T(8,128)(2,1)S(1)}, u32[]{:S(2)}, u32[]{:S(2)}) %collective-permute-start.5) | collective-permute-done | bytes 147488 | tf_op jit(solution)/shard_map/ppermute | solution.py:347
  20.4 1.6 %collective-permute-start.6 = (bf16[2,96,384]{2,1,0:T(8,128)(2,1)S(1)}, bf16[2,96,384]{2,1,0:T(8,128)(2,1)S(1)}, u32[]{:S(2)}, u32[]{:S(2)}) collective-permute-start(bf16[2,96,384]{2,1,0:T(8,128)(2,1)S(1)} %away_sum.1), channel_id=1, source_target_pairs={{0,2},{2,0},{1,3},{3,1},{4,6},{6,4},{5,7},{7,5},{8,10},{10,8},{9,1... | collective-permute-start | bytes 442376 | tf_op jit(solution)/shard_map/ppermute | solution.py:347
  21.9 3.5 %collective-permute-start.3 = (f32[1,2,128]{2,1,0:T(2,128)S(1)}, f32[1,2,128]{2,1,0:T(2,128)S(1)}, u32[]{:S(2)}, u32[]{:S(2)}) collective-permute-start(f32[1,2,128]{2,1,0:T(2,128)S(1)} %get-tuple-element.34), channel_id=1, source_target_pairs={{0,8},{4,12},{8,0},{12,4},{1,9},{5,13},{9,1},{13,5},{2,10},{6,14},... | collective-permute-start | bytes 3080 | tf_op jit(solution)/shard_map/ppermute | solution.py:347
  25.4 0.0 collective-permute-start.7
  25.4 0.4 %collective-permute-done.4.piece_ref.refs_0_ = bf16[400,384]{1,0:T(8,128)(2,1)S(1)} collective-permute-done((bf16[400,384]{1,0:T(8,128)(2,1)S(1)}, bf16[400,384]{1,0:T(8,128)(2,1)S(1)}, u32[]{:S(2)}, u32[]{:S(2)}) %collective-permute-start.4) | collective-permute-done | bytes 307232 | tf_op jit(solution)/shard_map/ppermute | solution.py:451
  25.8 0.2 collective-permute-start.8
  26.0 0.9 %around.1.around_ref = f32[1,2,128]{2,1,0:T(2,128)S(1)} custom-call(s32[4,8,128]{2,1,0:T(8,128)S(1)} %get-tuple-element.22.sizes_ref, bf16[1,400,384]{2,1,0:T(8,128)(2,1)S(1)} %relay.1.mine_ref, bf16[1,400,384]{2,1,0:T(8,128)(2,1)S(1)} %collective-permute-done.1.other_ref, s32[2,128]{1,0:T(2,128)S(1)} %get-tuple-element.25.here_ref, ...), custom_call_target="tpu_custom_call" | custom-call | bytes 1048576 | tf_op jit(solution)/shard_map/around/pallas_call | solution.py:487
  26.9 0.0 collective-permute-done.3.far_ref
  26.9 0.0 collective-permute-done.6.rest_0_
  27.0 0.0 collective-permute-done.7.too_ref
  27.0 0.3 collective-permute-done.8.recv_ref
  27.2 0.8 %last.1 = (bf16[2,96,384]{2,1,0:T(8,128)(2,1)}, f32[2,128]{1,0:T(2,128)}) custom-call(s32[4,8,128]{2,1,0:T(8,128)S(1)} %get-tuple-element.22.sizes_ref, bf16[2,384,384]{2,1,0:T(8,128)(2,1)S(1)} %get-tuple-element.23.masked_ref, f32[2,96,384]{2,1,0:T(8,128)S(1)} %get-tuple-element.37.own_ref, bf16[2,96,384]{2,1,0:T(8,128)(2,1)S(1)} %collective-permute-done.7.too_ref, ...), custom_call_target="tpu_custom_call" | custom-call | bytes 1048576 | tf_op jit(solution)/shard_map/last/pallas_call | solution.py:501
  (4 shorter events, 0.1 us)
Async XLA Ops:
  1.7 11.6 %collective-permute-start = (bf16[1,400,384]{2,1,0:T(8,128)(2,1)S(1)}, bf16[1,400,384]{2,1,0:T(8,128)(2,1)S(1)}, u32[]{:S(2)}, u32[]{:S(2)}) collective-permute-start(bf16[1,400,384]{2,1,0:T(8,128)(2,1)S(1)} %head.1.payload_ref), channel_id=1, source_target_pairs={{0,12},{4,0},{8,4},{12,8},{1,13},{5,1},{9,5},{13,9},{2,14},{6,2},{... | collective-permute-start | bytes 921608 | tf_op jit(solution)/shard_map/ppermute | solution.py:347
  12.6 1.7 %collective-permute-start.2 = (bf16[2,208,384]{2,1,0:T(8,128)(2,1)S(1)}, bf16[2,208,384]{2,1,0:T(8,128)(2,1)S(1)}, u32[]{:S(2)}, u32[]{:S(2)}) collective-permute-start(bf16[2,208,384]{2,1,0:T(8,128)(2,1)S(1)} %get-tuple-element.29), channel_id=1, source_target_pairs={{0,1},{1,0},{2,3},{3,2},{4,5},{5,4},{6,7},{7,6},{8,9},{9,8},{10,11... | collective-permute-start | bytes 958472 | tf_op jit(solution)/shard_map/ppermute | solution.py:347
  13.3 1.7 %collective-permute-start.1 = (bf16[1,400,384]{2,1,0:T(8,128)(2,1)S(1)}, bf16[1,400,384]{2,1,0:T(8,128)(2,1)S(1)}, u32[]{:S(2)}, u32[]{:S(2)}) collective-permute-start(bf16[1,400,384]{2,1,0:T(8,128)(2,1)S(1)} %relay.1.mine_ref), channel_id=1, source_target_pairs={{0,1},{1,0},{2,3},{3,2},{4,5},{5,4},{6,7},{7,6},{8,9},{9,8},{10,11... | collective-permute-start | bytes 921608 | tf_op jit(solution)/shard_map/ppermute | solution.py:347
  14.4 11.4 %collective-permute-start.4 = (bf16[400,384]{1,0:T(8,128)(2,1)S(1)}, bf16[400,384]{1,0:T(8,128)(2,1)S(1)}, u32[]{:S(2)}, u32[]{:S(2)}) collective-permute-start(bf16[400,384]{1,0:T(8,128)(2,1)S(1)} %get-tuple-element.35), channel_id=1, source_target_pairs={{0,4},{1,6},{2,5},{3,7},{4,8},{5,10},{6,9},{7,11},{8,12},{9,14},{1... | collective-permute-start | bytes 921608 | tf_op jit(solution)/shard_map/ppermute | solution.py:451
  18.9 1.4 %collective-permute-start.5 = (bf16[2,96,384]{2,1,0:T(8,128)(2,1)S(1)}, bf16[2,96,384]{2,1,0:T(8,128)(2,1)S(1)}, u32[]{:S(2)}, u32[]{:S(2)}) collective-permute-start(bf16[2,96,384]{2,1,0:T(8,128)(2,1)S(1)} %get-tuple-element.36), channel_id=1, source_target_pairs={{0,1},{1,0},{2,3},{3,2},{4,5},{5,4},{6,7},{7,6},{8,9},{9,8},{10,11... | collective-permute-start | bytes 442376 | tf_op jit(solution)/shard_map/ppermute | solution.py:347
  20.4 6.6 %collective-permute-start.6 = (bf16[2,96,384]{2,1,0:T(8,128)(2,1)S(1)}, bf16[2,96,384]{2,1,0:T(8,128)(2,1)S(1)}, u32[]{:S(2)}, u32[]{:S(2)}) collective-permute-start(bf16[2,96,384]{2,1,0:T(8,128)(2,1)S(1)} %away_sum.1), channel_id=1, source_target_pairs={{0,2},{2,0},{1,3},{3,1},{4,6},{6,4},{5,7},{7,5},{8,10},{10,8},{9,1... | collective-permute-start | bytes 442376 | tf_op jit(solution)/shard_map/ppermute | solution.py:347
  21.9 5.0 %collective-permute-start.3 = (f32[1,2,128]{2,1,0:T(2,128)S(1)}, f32[1,2,128]{2,1,0:T(2,128)S(1)}, u32[]{:S(2)}, u32[]{:S(2)}) collective-permute-start(f32[1,2,128]{2,1,0:T(2,128)S(1)} %get-tuple-element.34), channel_id=1, source_target_pairs={{0,8},{4,12},{8,0},{12,4},{1,9},{5,13},{9,1},{13,5},{2,10},{6,14},... | collective-permute-start | bytes 3080 | tf_op jit(solution)/shard_map/ppermute | solution.py:347
  25.4 1.6 %collective-permute-start.7 = (bf16[2,96,384]{2,1,0:T(8,128)(2,1)S(1)}, bf16[2,96,384]{2,1,0:T(8,128)(2,1)S(1)}, u32[]{:S(2)}, u32[]{:S(2)}) collective-permute-start(bf16[2,96,384]{2,1,0:T(8,128)(2,1)S(1)} %get-tuple-element.38), channel_id=1, source_target_pairs={{0,1},{1,0},{2,3},{3,2},{4,5},{5,4},{6,7},{7,6},{8,9},{9,8},{10,11... | collective-permute-start | bytes 442376 | tf_op jit(solution)/shard_map/ppermute | solution.py:347
  25.8 1.4 %collective-permute-start.8 = (bf16[2,96,384]{2,1,0:T(8,128)(2,1)S(1)}, bf16[2,96,384]{2,1,0:T(8,128)(2,1)S(1)}, u32[]{:S(2)}, u32[]{:S(2)}) collective-permute-start(bf16[2,96,384]{2,1,0:T(8,128)(2,1)S(1)} %get-tuple-element.40), channel_id=1, source_target_pairs={{0,1},{1,0},{2,3},{3,2},{4,5},{5,4},{6,7},{7,6},{8,9},{9,8},{10,11... | collective-permute-start | bytes 442376 | tf_op jit(solution)/shard_map/ppermute | solution.py:347

commit v8 on v7

--- a/solution.py
+++ b/solution.py
@@ -57,7 +57,7 @@
 def over_lanes(points, block_cols, pts_rows):
     rows = jnp.concatenate(points)
     ones = jnp.ones((16, 128), BF16)
-    total = sum(dot_t(ones, part.astype(BF16)) for part in thirds(rows))
+    total = sum(dot_t(ones, part.astype(BF16)) for part in thirds(rows)[:2])
     size = pts_rows * block_cols
     return [
         [total[0:1, k * size + r * block_cols : k * size + (r + 1) * block_cols] for r in range(pts_rows)]

time: 28.3 us -> 28.3 us (level)
  transfers between devices with their start and end apart: 9 -> 9, of which waited for: 6 -> 7; matrix products, arithmetic and copies ran while one was open for 0% -> 0% of each run, Pallas kernels for 36% -> 36%
where the time goes in v8:
time: 28.3 us; the launch traced here: 28.1 us
  Pallas kernels  12.1 us (43%)
  starting transfers between devices  10.8 us (38%)
  waiting for transfers between devices  3.89 us (14%)
  between operations  1.35 us (5%)
    ppermute x8, starting transfers between devices, turned(): lax.ppermute(value, axis, [(s, (s + steps) % count) for s in range(count)])  10.7 us
    pallas_call x1, Pallas kernels, per_device(): call(right_kernel, 'right', [hbm] * 3 + [smem, vmem] + [hbm] * 4, (halves...  5.33 us
    pallas_call x1, Pallas kernels, per_device(): call(left_kernel, 'left', [vmem] * 8, [shape(by_chip, F32)] + [shape((fra...  3.86 us
    ppermute x8, waiting for transfers between devices, turned(): lax.ppermute(value, axis, [(s, (s + steps) % count) for s in range(count)])  3.5 us
    pallas_call x1, Pallas kernels, per_device(): call(head_kernel, 'head', [hbm] * 2, shape((half, nbasis + EXTRA, nbasis)...  1.04 us
    pallas_call x1, Pallas kernels, per_device(): call(functools.partial(last_kernel, scale), 'last', [vmem] * 7, (shape(mi...  0.81 us
    pallas_call x1, Pallas kernels, per_device(): call(functools.partial(around_kernel, frag_dev), 'around', [vmem] * 6, sl...  0.8 us
  transfers between devices with their start and end apart: 9, of which 7 were waited for; matrix products, arithmetic and copies ran while one was open for 0% of the time, Pallas kernels for 36%

profile of v8, /device:TPU:0, one launch (start us, length us, event | category | flops | bytes accessed | tf_op | source)
XLA Modules:
  0.0 28.1 jit_solution(5261004257788600127)
XLA Ops:
  0.6 1.0 %head.1.payload_ref = bf16[1,400,384]{2,1,0:T(8,128)(2,1)S(1)} custom-call(bf16[2,384,384]{2,1,0:T(8,128)(2,1)} %density_hbm.3, f32[3,2,384]{2,1,0:T(2,128)} %bitcast.1), custom_call_target="tpu_custom_call" | custom-call | bytes 1048576 | tf_op jit(solution)/shard_map/head/pallas_call | solution.py:394
  1.7 5.1 %collective-permute-start = (bf16[1,400,384]{2,1,0:T(8,128)(2,1)S(1)}, bf16[1,400,384]{2,1,0:T(8,128)(2,1)S(1)}, u32[]{:S(2)}, u32[]{:S(2)}) collective-permute-start(bf16[1,400,384]{2,1,0:T(8,128)(2,1)S(1)} %head.1.payload_ref), channel_id=1, source_target_pairs={{0,12},{4,0},{8,4},{12,8},{1,13},{5,1},{9,5},{13,9},{2,14},{6,2},{... | collective-permute-start | bytes 921608 | tf_op jit(solution)/shard_map/ppermute | solution.py:347
  7.4 5.3 %right.1 = (bf16[2,192,384]{2,1,0:T(8,128)(2,1)S(1)}, bf16[2,208,384]{2,1,0:T(8,128)(2,1)S(1)}, f32[2,384,384]{2,1,0:T(8,128)S(1)}, bf16[8,384,384]{2,1,0:T(8,12...) custom-call(s32[8]{0:T(128)} %size_hbm.1, ...), custom_call_target="tpu_custom_call" | custom-call | flops 1811939328 | bytes 1048576 | tf_op jit(solution)/shard_map/right/pallas_call | solution.py:404
  12.8 0.1 collective-permute-start.2
  12.8 0.5 %collective-permute-done.in_ref = bf16[1,400,384]{2,1,0:T(8,128)(2,1)S(1)} collective-permute-done((bf16[1,400,384]{2,1,0:T(8,128)(2,1)S(1)}, bf16[1,400,384]{2,1,0:T(8,128)(2,1)S(1)}, u32[]{:S(2)}, u32[]{:S(2)}) %collective-permute-start) | collective-permute-done | bytes 307232 | tf_op jit(solution)/shard_map/ppermute | solution.py:347
  13.3 0.1 collective-permute-start.1
  13.4 1.0 %collective-permute-done.2.recv_ref = bf16[2,208,384]{2,1,0:T(8,128)(2,1)S(1)} collective-permute-done((bf16[2,208,384]{2,1,0:T(8,128)(2,1)S(1)}, bf16[2,208,384]{2,1,0:T(8,128)(2,1)S(1)}, u32[]{:S(2)}, u32[]{:S(2)}) %collective-permute-start.2) | collective-permute-done | bytes 319520 | tf_op jit(solution)/shard_map/ppermute | solution.py:347
  14.5 0.1 next_sum.1
  14.5 0.1 collective-permute-start.4
  14.6 0.4 %collective-permute-done.1.other_ref = bf16[1,400,384]{2,1,0:T(8,128)(2,1)S(1)} collective-permute-done((bf16[1,400,384]{2,1,0:T(8,128)(2,1)S(1)}, bf16[1,400,384]{2,1,0:T(8,128)(2,1)S(1)}, u32[]{:S(2)}, u32[]{:S(2)}) %collective-permute-start.1) | collective-permute-done | bytes 307232 | tf_op jit(solution)/shard_map/ppermute | solution.py:347
  15.0 3.9 %left.1 = (f32[2,2,96,384]{3,2,1,0:T(8,128)S(1)}, bf16[2,96,384]{2,1,0:T(8,128)(2,1)S(1)}, bf16[2,96,384]{2,1,0:T(8,128)(2,1)S(1)}) custom-call(s32[16,128]{1,0:T(8,128)S(1)} %get-tuple-element.24.slots_ref, s32[4,8,128]{2,1,0:T(8,128)S(1)} %get-tuple-element.22.sizes_ref, bf16[2,384,384]{2,1,0:T(8,128)(2,1)S(1)} %get-tuple-element.23.masked_ref, ...), custom_call_target="tpu_custom_call" | custom-call | flops 1811939328 | bytes 1048576 | tf_op jit(solution)/shard_map/left/pallas_call | solution.py:455
  18.9 0.2 collective-permute-start.5
  19.1 1.2 %collective-permute-done.5.refs_0_ = bf16[2,96,384]{2,1,0:T(8,128)(2,1)S(1)} collective-permute-done((bf16[2,96,384]{2,1,0:T(8,128)(2,1)S(1)}, bf16[2,96,384]{2,1,0:T(8,128)(2,1)S(1)}, u32[]{:S(2)}, u32[]{:S(2)}) %collective-permute-start.5) | collective-permute-done | bytes 147488 | tf_op jit(solution)/shard_map/ppermute | solution.py:347
  20.4 1.6 %collective-permute-start.6 = (bf16[2,96,384]{2,1,0:T(8,128)(2,1)S(1)}, bf16[2,96,384]{2,1,0:T(8,128)(2,1)S(1)}, u32[]{:S(2)}, u32[]{:S(2)}) collective-permute-start(bf16[2,96,384]{2,1,0:T(8,128)(2,1)S(1)} %away_sum.1), channel_id=1, source_target_pairs={{0,2},{2,0},{1,3},{3,1},{4,6},{6,4},{5,7},{7,5},{8,10},{10,8},{9,1... | collective-permute-start | bytes 442376 | tf_op jit(solution)/shard_map/ppermute | solution.py:347
  21.9 3.5 %collective-permute-start.3 = (f32[1,2,128]{2,1,0:T(2,128)S(1)}, f32[1,2,128]{2,1,0:T(2,128)S(1)}, u32[]{:S(2)}, u32[]{:S(2)}) collective-permute-start(f32[1,2,128]{2,1,0:T(2,128)S(1)} %get-tuple-element.34), channel_id=1, source_target_pairs={{0,8},{4,12},{8,0},{12,4},{1,9},{5,13},{9,1},{13,5},{2,10},{6,14},... | collective-permute-start | bytes 3080 | tf_op jit(solution)/shard_map/ppermute | solution.py:347
  25.4 0.0 collective-permute-start.7
  25.4 0.4 %collective-permute-done.4.piece_ref.refs_0_ = bf16[400,384]{1,0:T(8,128)(2,1)S(1)} collective-permute-done((bf16[400,384]{1,0:T(8,128)(2,1)S(1)}, bf16[400,384]{1,0:T(8,128)(2,1)S(1)}, u32[]{:S(2)}, u32[]{:S(2)}) %collective-permute-start.4) | collective-permute-done | bytes 307232 | tf_op jit(solution)/shard_map/ppermute | solution.py:451
  25.8 0.2 collective-permute-start.8
  26.0 0.8 %around.1.around_ref = f32[1,2,128]{2,1,0:T(2,128)S(1)} custom-call(s32[4,8,128]{2,1,0:T(8,128)S(1)} %get-tuple-element.22.sizes_ref, bf16[1,400,384]{2,1,0:T(8,128)(2,1)S(1)} %relay.1.mine_ref, bf16[1,400,384]{2,1,0:T(8,128)(2,1)S(1)} %collective-permute-done.1.other_ref, s32[2,128]{1,0:T(2,128)S(1)} %get-tuple-element.25.here_ref, ...), custom_call_target="tpu_custom_call" | custom-call | bytes 1048576 | tf_op jit(solution)/shard_map/around/pallas_call | solution.py:487
  26.8 0.1 collective-permute-done.3.far_ref
  26.9 0.0 collective-permute-done.6.rest_0_
  27.0 0.0 collective-permute-done.7.too_ref
  27.0 0.3 collective-permute-done.8.recv_ref
  27.2 0.8 %last.1 = (bf16[2,96,384]{2,1,0:T(8,128)(2,1)}, f32[2,128]{1,0:T(2,128)}) custom-call(s32[4,8,128]{2,1,0:T(8,128)S(1)} %get-tuple-element.22.sizes_ref, bf16[2,384,384]{2,1,0:T(8,128)(2,1)S(1)} %get-tuple-element.23.masked_ref, f32[2,96,384]{2,1,0:T(8,128)S(1)} %get-tuple-element.37.own_ref, bf16[2,96,384]{2,1,0:T(8,128)(2,1)S(1)} %collective-permute-done.7.too_ref, ...), custom_call_target="tpu_custom_call" | custom-call | bytes 1048576 | tf_op jit(solution)/shard_map/last/pallas_call | solution.py:501
  (4 shorter events, 0.1 us)
Async XLA Ops:
  1.7 11.6 %collective-permute-start = (bf16[1,400,384]{2,1,0:T(8,128)(2,1)S(1)}, bf16[1,400,384]{2,1,0:T(8,128)(2,1)S(1)}, u32[]{:S(2)}, u32[]{:S(2)}) collective-permute-start(bf16[1,400,384]{2,1,0:T(8,128)(2,1)S(1)} %head.1.payload_ref), channel_id=1, source_target_pairs={{0,12},{4,0},{8,4},{12,8},{1,13},{5,1},{9,5},{13,9},{2,14},{6,2},{... | collective-permute-start | bytes 921608 | tf_op jit(solution)/shard_map/ppermute | solution.py:347
  12.8 1.7 %collective-permute-start.2 = (bf16[2,208,384]{2,1,0:T(8,128)(2,1)S(1)}, bf16[2,208,384]{2,1,0:T(8,128)(2,1)S(1)}, u32[]{:S(2)}, u32[]{:S(2)}) collective-permute-start(bf16[2,208,384]{2,1,0:T(8,128)(2,1)S(1)} %get-tuple-element.29), channel_id=1, source_target_pairs={{0,1},{1,0},{2,3},{3,2},{4,5},{5,4},{6,7},{7,6},{8,9},{9,8},{10,11... | collective-permute-start | bytes 958472 | tf_op jit(solution)/shard_map/ppermute | solution.py:347
  13.3 1.7 %collective-permute-start.1 = (bf16[1,400,384]{2,1,0:T(8,128)(2,1)S(1)}, bf16[1,400,384]{2,1,0:T(8,128)(2,1)S(1)}, u32[]{:S(2)}, u32[]{:S(2)}) collective-permute-start(bf16[1,400,384]{2,1,0:T(8,128)(2,1)S(1)} %relay.1.mine_ref), channel_id=1, source_target_pairs={{0,1},{1,0},{2,3},{3,2},{4,5},{5,4},{6,7},{7,6},{8,9},{9,8},{10,11... | collective-permute-start | bytes 921608 | tf_op jit(solution)/shard_map/ppermute | solution.py:347
  14.5 11.2 %collective-permute-start.4 = (bf16[400,384]{1,0:T(8,128)(2,1)S(1)}, bf16[400,384]{1,0:T(8,128)(2,1)S(1)}, u32[]{:S(2)}, u32[]{:S(2)}) collective-permute-start(bf16[400,384]{1,0:T(8,128)(2,1)S(1)} %get-tuple-element.35), channel_id=1, source_target_pairs={{0,4},{1,6},{2,5},{3,7},{4,8},{5,10},{6,9},{7,11},{8,12},{9,14},{1... | collective-permute-start | bytes 921608 | tf_op jit(solution)/shard_map/ppermute | solution.py:451
  18.9 1.4 %collective-permute-start.5 = (bf16[2,96,384]{2,1,0:T(8,128)(2,1)S(1)}, bf16[2,96,384]{2,1,0:T(8,128)(2,1)S(1)}, u32[]{:S(2)}, u32[]{:S(2)}) collective-permute-start(bf16[2,96,384]{2,1,0:T(8,128)(2,1)S(1)} %get-tuple-element.36), channel_id=1, source_target_pairs={{0,1},{1,0},{2,3},{3,2},{4,5},{5,4},{6,7},{7,6},{8,9},{9,8},{10,11... | collective-permute-start | bytes 442376 | tf_op jit(solution)/shard_map/ppermute | solution.py:347
  20.4 6.6 %collective-permute-start.6 = (bf16[2,96,384]{2,1,0:T(8,128)(2,1)S(1)}, bf16[2,96,384]{2,1,0:T(8,128)(2,1)S(1)}, u32[]{:S(2)}, u32[]{:S(2)}) collective-permute-start(bf16[2,96,384]{2,1,0:T(8,128)(2,1)S(1)} %away_sum.1), channel_id=1, source_target_pairs={{0,2},{2,0},{1,3},{3,1},{4,6},{6,4},{5,7},{7,5},{8,10},{10,8},{9,1... | collective-permute-start | bytes 442376 | tf_op jit(solution)/shard_map/ppermute | solution.py:347
  21.9 5.0 %collective-permute-start.3 = (f32[1,2,128]{2,1,0:T(2,128)S(1)}, f32[1,2,128]{2,1,0:T(2,128)S(1)}, u32[]{:S(2)}, u32[]{:S(2)}) collective-permute-start(f32[1,2,128]{2,1,0:T(2,128)S(1)} %get-tuple-element.34), channel_id=1, source_target_pairs={{0,8},{4,12},{8,0},{12,4},{1,9},{5,13},{9,1},{13,5},{2,10},{6,14},... | collective-permute-start | bytes 3080 | tf_op jit(solution)/shard_map/ppermute | solution.py:347
  25.4 1.6 %collective-permute-start.7 = (bf16[2,96,384]{2,1,0:T(8,128)(2,1)S(1)}, bf16[2,96,384]{2,1,0:T(8,128)(2,1)S(1)}, u32[]{:S(2)}, u32[]{:S(2)}) collective-permute-start(bf16[2,96,384]{2,1,0:T(8,128)(2,1)S(1)} %get-tuple-element.38), channel_id=1, source_target_pairs={{0,1},{1,0},{2,3},{3,2},{4,5},{5,4},{6,7},{7,6},{8,9},{9,8},{10,11... | collective-permute-start | bytes 442376 | tf_op jit(solution)/shard_map/ppermute | solution.py:347
  25.8 1.4 %collective-permute-start.8 = (bf16[2,96,384]{2,1,0:T(8,128)(2,1)S(1)}, bf16[2,96,384]{2,1,0:T(8,128)(2,1)S(1)}, u32[]{:S(2)}, u32[]{:S(2)}) collective-permute-start(bf16[2,96,384]{2,1,0:T(8,128)(2,1)S(1)} %get-tuple-element.40), channel_id=1, source_target_pairs={{0,1},{1,0},{2,3},{3,2},{4,5},{5,4},{6,7},{7,6},{8,9},{9,8},{10,11... | collective-permute-start | bytes 442376 | tf_op jit(solution)/shard_map/ppermute | solution.py:347

commit v9 on v7

--- a/solution.py
+++ b/solution.py
@@ -327,19 +327,26 @@
 
 
 def last_kernel(
-    scale, sizes_ref, masked_ref, own_ref, too_ref, before_ref, recv_ref, pot_ref, out_ref, potential_ref
+    scale, sizes_ref, masked_ref, own_ref, too_ref, before_ref, recv_ref, pot_ref, out_hbm, potential_hbm,
+    out_ref, potential_ref, sems,
 ):
     frag_dev, share, nbasis = out_ref.shape
     member = lax.axis_index("grid") * lax.axis_size("sub") + lax.axis_index("sub")
     row_start = pl.multiple_of(member * share, share)
     rows = row_start + lax.broadcasted_iota(I32, (share, nbasis), 0)
     cols = lax.broadcasted_iota(I32, (share, nbasis), 1)
+    potential_ref[...] = pot_ref[0] * scale
+    copies = fetch([(potential_ref, potential_hbm)], sems)
     for f in range(frag_dev):
         size = sizes_ref[f, 0:1, 0:1]
         correction = own_ref[f] + before_ref[f] + (recv_ref[f].astype(F32) + too_ref[f].astype(F32))
         correction = jnp.where((rows < size) & (cols < size), correction, 0.0)
         out_ref[f] = (masked_ref[f, pl.ds(row_start, share), :].astype(F32) + correction).astype(BF16)
-    potential_ref[...] = pot_ref[0] * scale
+        copy = pltpu.make_async_copy(out_ref.at[f], out_hbm.at[f], sems.at[1 + f])
+        copy.start()
+        copies.append(copy)
+    for copy in copies:
+        copy.wait()
 
 
 def turned(value, axis, steps):
@@ -503,7 +510,11 @@
         "last",
         [vmem] * 7,
         (shape(mine_rows, BF16), shape((pts_rows, block_cols), F32)),
-        (vmem,) * 2,
+        (hbm,) * 2,
+        [
+            pltpu.VMEM(mine_rows, BF16), pltpu.VMEM((pts_rows, block_cols), F32),
+            pltpu.SemaphoreType.DMA((1 + frag_dev,)),
+        ],
     )(sizes, masked, own, own_recv, before, passed, pot)
 
 

time: 28.3 us -> 28.3 us (level)
  no operation moved by 1% of the time
where the time goes in v9:
time: 28.3 us; the launch traced here: 28.1 us
  Pallas kernels  12 us (42%)
  starting transfers between devices  10.7 us (38%)
  waiting for transfers between devices  3.95 us (14%)
  between operations  1.36 us (5%)
    ppermute x8, starting transfers between devices, turned(): lax.ppermute(value, axis, [(s, (s + steps) % count) for s in range(count)])  10.7 us
    pallas_call x1, Pallas kernels, per_device(): call(right_kernel, 'right', [hbm] * 3 + [smem, vmem] + [hbm] * 4, (halves...  5.16 us
    pallas_call x1, Pallas kernels, per_device(): call(left_kernel, 'left', [vmem] * 8, [shape(by_chip, F32)] + [shape((fra...  3.86 us
    ppermute x8, waiting for transfers between devices, turned(): lax.ppermute(value, axis, [(s, (s + steps) % count) for s in range(count)])  3.57 us
    pallas_call x1, Pallas kernels, per_device(): call(head_kernel, 'head', [hbm] * 2, shape((half, nbasis + EXTRA, nbasis)...  1.04 us
    pallas_call x1, Pallas kernels, per_device(): call(functools.partial(around_kernel, frag_dev), 'around', [vmem] * 6, sl...  0.92 us
    pallas_call x1, Pallas kernels, per_device(): call(functools.partial(last_kernel, scale), 'last', [vmem] * 7, (shape(mi...  0.8 us
  transfers between devices with their start and end apart: 9, of which 6 were waited for; matrix products, arithmetic and copies ran while one was open for 0% of the time, Pallas kernels for 36%

profile of v9, /device:TPU:0, one launch (start us, length us, event | category | flops | bytes accessed | tf_op | source)
XLA Modules:
  0.0 28.1 jit_solution(4014070487253278810)
XLA Ops:
  0.6 1.0 %head.1.payload_ref = bf16[1,400,384]{2,1,0:T(8,128)(2,1)S(1)} custom-call(bf16[2,384,384]{2,1,0:T(8,128)(2,1)} %density_hbm.3, f32[3,2,384]{2,1,0:T(2,128)} %bitcast.1), custom_call_target="tpu_custom_call" | custom-call | bytes 1048576 | tf_op jit(solution)/shard_map/head/pallas_call | solution.py:401
  1.7 5.1 %collective-permute-start = (bf16[1,400,384]{2,1,0:T(8,128)(2,1)S(1)}, bf16[1,400,384]{2,1,0:T(8,128)(2,1)S(1)}, u32[]{:S(2)}, u32[]{:S(2)}) collective-permute-start(bf16[1,400,384]{2,1,0:T(8,128)(2,1)S(1)} %head.1.payload_ref), channel_id=1, source_target_pairs={{0,12},{4,0},{8,4},{12,8},{1,13},{5,1},{9,5},{13,9},{2,14},{6,2},{... | collective-permute-start | bytes 921608 | tf_op jit(solution)/shard_map/ppermute | solution.py:354
  7.4 5.2 %right.1 = (bf16[2,192,384]{2,1,0:T(8,128)(2,1)S(1)}, bf16[2,208,384]{2,1,0:T(8,128)(2,1)S(1)}, f32[2,384,384]{2,1,0:T(8,128)S(1)}, bf16[8,384,384]{2,1,0:T(8,12...) custom-call(s32[8]{0:T(128)} %size_hbm.1, ...), custom_call_target="tpu_custom_call" | custom-call | flops 1811939328 | bytes 1048576 | tf_op jit(solution)/shard_map/right/pallas_call | solution.py:411
  12.6 0.1 collective-permute-start.2
  12.7 0.6 %collective-permute-done.in_ref = bf16[1,400,384]{2,1,0:T(8,128)(2,1)S(1)} collective-permute-done((bf16[1,400,384]{2,1,0:T(8,128)(2,1)S(1)}, bf16[1,400,384]{2,1,0:T(8,128)(2,1)S(1)}, u32[]{:S(2)}, u32[]{:S(2)}) %collective-permute-start) | collective-permute-done | bytes 307232 | tf_op jit(solution)/shard_map/ppermute | solution.py:354
  13.3 0.1 collective-permute-start.1
  13.4 0.9 %collective-permute-done.2.recv_ref = bf16[2,208,384]{2,1,0:T(8,128)(2,1)S(1)} collective-permute-done((bf16[2,208,384]{2,1,0:T(8,128)(2,1)S(1)}, bf16[2,208,384]{2,1,0:T(8,128)(2,1)S(1)}, u32[]{:S(2)}, u32[]{:S(2)}) %collective-permute-start.2) | collective-permute-done | bytes 319520 | tf_op jit(solution)/shard_map/ppermute | solution.py:354
  14.3 0.1 next_sum.1
  14.4 0.1 collective-permute-start.4
  14.4 0.6 %collective-permute-done.1.other_ref = bf16[1,400,384]{2,1,0:T(8,128)(2,1)S(1)} collective-permute-done((bf16[1,400,384]{2,1,0:T(8,128)(2,1)S(1)}, bf16[1,400,384]{2,1,0:T(8,128)(2,1)S(1)}, u32[]{:S(2)}, u32[]{:S(2)}) %collective-permute-start.1) | collective-permute-done | bytes 307232 | tf_op jit(solution)/shard_map/ppermute | solution.py:354
  15.0 3.9 %left.1 = (f32[2,2,96,384]{3,2,1,0:T(8,128)S(1)}, bf16[2,96,384]{2,1,0:T(8,128)(2,1)S(1)}, bf16[2,96,384]{2,1,0:T(8,128)(2,1)S(1)}) custom-call(s32[16,128]{1,0:T(8,128)S(1)} %get-tuple-element.24.slots_ref, s32[4,8,128]{2,1,0:T(8,128)S(1)} %get-tuple-element.22.sizes_ref, bf16[2,384,384]{2,1,0:T(8,128)(2,1)S(1)} %get-tuple-element.23.masked_ref, ...), custom_call_target="tpu_custom_call" | custom-call | flops 1811939328 | bytes 1048576 | tf_op jit(solution)/shard_map/left/pallas_call | solution.py:462
  18.9 0.2 collective-permute-start.5
  19.1 1.2 %collective-permute-done.5.refs_0_ = bf16[2,96,384]{2,1,0:T(8,128)(2,1)S(1)} collective-permute-done((bf16[2,96,384]{2,1,0:T(8,128)(2,1)S(1)}, bf16[2,96,384]{2,1,0:T(8,128)(2,1)S(1)}, u32[]{:S(2)}, u32[]{:S(2)}) %collective-permute-start.5) | collective-permute-done | bytes 147488 | tf_op jit(solution)/shard_map/ppermute | solution.py:354
  20.4 1.6 %collective-permute-start.6 = (bf16[2,96,384]{2,1,0:T(8,128)(2,1)S(1)}, bf16[2,96,384]{2,1,0:T(8,128)(2,1)S(1)}, u32[]{:S(2)}, u32[]{:S(2)}) collective-permute-start(bf16[2,96,384]{2,1,0:T(8,128)(2,1)S(1)} %away_sum.1), channel_id=1, source_target_pairs={{0,2},{2,0},{1,3},{3,1},{4,6},{6,4},{5,7},{7,5},{8,10},{10,8},{9,1... | collective-permute-start | bytes 442376 | tf_op jit(solution)/shard_map/ppermute | solution.py:354
  21.9 3.5 %collective-permute-start.3 = (f32[1,2,128]{2,1,0:T(2,128)S(1)}, f32[1,2,128]{2,1,0:T(2,128)S(1)}, u32[]{:S(2)}, u32[]{:S(2)}) collective-permute-start(f32[1,2,128]{2,1,0:T(2,128)S(1)} %get-tuple-element.34), channel_id=1, source_target_pairs={{0,8},{4,12},{8,0},{12,4},{1,9},{5,13},{9,1},{13,5},{2,10},{6,14},... | collective-permute-start | bytes 3080 | tf_op jit(solution)/shard_map/ppermute | solution.py:354
  25.4 0.0 collective-permute-start.7
  25.4 0.4 %collective-permute-done.4.piece_ref.refs_0_ = bf16[400,384]{1,0:T(8,128)(2,1)S(1)} collective-permute-done((bf16[400,384]{1,0:T(8,128)(2,1)S(1)}, bf16[400,384]{1,0:T(8,128)(2,1)S(1)}, u32[]{:S(2)}, u32[]{:S(2)}) %collective-permute-start.4) | collective-permute-done | bytes 307232 | tf_op jit(solution)/shard_map/ppermute | solution.py:458
  25.8 0.2 collective-permute-start.8
  26.0 0.9 %around.1.around_ref = f32[1,2,128]{2,1,0:T(2,128)S(1)} custom-call(s32[4,8,128]{2,1,0:T(8,128)S(1)} %get-tuple-element.22.sizes_ref, bf16[1,400,384]{2,1,0:T(8,128)(2,1)S(1)} %relay.1.mine_ref, bf16[1,400,384]{2,1,0:T(8,128)(2,1)S(1)} %collective-permute-done.1.other_ref, s32[2,128]{1,0:T(2,128)S(1)} %get-tuple-element.25.here_ref, ...), custom_call_target="tpu_custom_call" | custom-call | bytes 1048576 | tf_op jit(solution)/shard_map/around/pallas_call | solution.py:494
  26.9 0.0 collective-permute-done.3.far_ref
  26.9 0.0 collective-permute-done.6.rest_0_
  27.0 0.0 collective-permute-done.7.too_ref
  27.0 0.3 collective-permute-done.8.recv_ref
  27.2 0.8 %last.1 = (bf16[2,96,384]{2,1,0:T(8,128)(2,1)}, f32[2,128]{1,0:T(2,128)}) custom-call(s32[4,8,128]{2,1,0:T(8,128)S(1)} %get-tuple-element.22.sizes_ref, bf16[2,384,384]{2,1,0:T(8,128)(2,1)S(1)} %get-tuple-element.23.masked_ref, f32[2,96,384]{2,1,0:T(8,128)S(1)} %get-tuple-element.37.own_ref, bf16[2,96,384]{2,1,0:T(8,128)(2,1)S(1)} %collective-permute-done.7.too_ref, ...), custom_call_target="tpu_custom_call" | custom-call | bytes 1048576 | tf_op jit(solution)/shard_map/last/pallas_call | solution.py:508
  (4 shorter events, 0.1 us)
Async XLA Ops:
  1.7 11.6 %collective-permute-start = (bf16[1,400,384]{2,1,0:T(8,128)(2,1)S(1)}, bf16[1,400,384]{2,1,0:T(8,128)(2,1)S(1)}, u32[]{:S(2)}, u32[]{:S(2)}) collective-permute-start(bf16[1,400,384]{2,1,0:T(8,128)(2,1)S(1)} %head.1.payload_ref), channel_id=1, source_target_pairs={{0,12},{4,0},{8,4},{12,8},{1,13},{5,1},{9,5},{13,9},{2,14},{6,2},{... | collective-permute-start | bytes 921608 | tf_op jit(solution)/shard_map/ppermute | solution.py:354
  12.6 1.7 %collective-permute-start.2 = (bf16[2,208,384]{2,1,0:T(8,128)(2,1)S(1)}, bf16[2,208,384]{2,1,0:T(8,128)(2,1)S(1)}, u32[]{:S(2)}, u32[]{:S(2)}) collective-permute-start(bf16[2,208,384]{2,1,0:T(8,128)(2,1)S(1)} %get-tuple-element.29), channel_id=1, source_target_pairs={{0,1},{1,0},{2,3},{3,2},{4,5},{5,4},{6,7},{7,6},{8,9},{9,8},{10,11... | collective-permute-start | bytes 958472 | tf_op jit(solution)/shard_map/ppermute | solution.py:354
  13.3 1.7 %collective-permute-start.1 = (bf16[1,400,384]{2,1,0:T(8,128)(2,1)S(1)}, bf16[1,400,384]{2,1,0:T(8,128)(2,1)S(1)}, u32[]{:S(2)}, u32[]{:S(2)}) collective-permute-start(bf16[1,400,384]{2,1,0:T(8,128)(2,1)S(1)} %relay.1.mine_ref), channel_id=1, source_target_pairs={{0,1},{1,0},{2,3},{3,2},{4,5},{5,4},{6,7},{7,6},{8,9},{9,8},{10,11... | collective-permute-start | bytes 921608 | tf_op jit(solution)/shard_map/ppermute | solution.py:354
  14.4 11.4 %collective-permute-start.4 = (bf16[400,384]{1,0:T(8,128)(2,1)S(1)}, bf16[400,384]{1,0:T(8,128)(2,1)S(1)}, u32[]{:S(2)}, u32[]{:S(2)}) collective-permute-start(bf16[400,384]{1,0:T(8,128)(2,1)S(1)} %get-tuple-element.35), channel_id=1, source_target_pairs={{0,4},{1,6},{2,5},{3,7},{4,8},{5,10},{6,9},{7,11},{8,12},{9,14},{1... | collective-permute-start | bytes 921608 | tf_op jit(solution)/shard_map/ppermute | solution.py:458
  18.9 1.4 %collective-permute-start.5 = (bf16[2,96,384]{2,1,0:T(8,128)(2,1)S(1)}, bf16[2,96,384]{2,1,0:T(8,128)(2,1)S(1)}, u32[]{:S(2)}, u32[]{:S(2)}) collective-permute-start(bf16[2,96,384]{2,1,0:T(8,128)(2,1)S(1)} %get-tuple-element.36), channel_id=1, source_target_pairs={{0,1},{1,0},{2,3},{3,2},{4,5},{5,4},{6,7},{7,6},{8,9},{9,8},{10,11... | collective-permute-start | bytes 442376 | tf_op jit(solution)/shard_map/ppermute | solution.py:354
  20.4 6.6 %collective-permute-start.6 = (bf16[2,96,384]{2,1,0:T(8,128)(2,1)S(1)}, bf16[2,96,384]{2,1,0:T(8,128)(2,1)S(1)}, u32[]{:S(2)}, u32[]{:S(2)}) collective-permute-start(bf16[2,96,384]{2,1,0:T(8,128)(2,1)S(1)} %away_sum.1), channel_id=1, source_target_pairs={{0,2},{2,0},{1,3},{3,1},{4,6},{6,4},{5,7},{7,5},{8,10},{10,8},{9,1... | collective-permute-start | bytes 442376 | tf_op jit(solution)/shard_map/ppermute | solution.py:354
  21.9 5.0 %collective-permute-start.3 = (f32[1,2,128]{2,1,0:T(2,128)S(1)}, f32[1,2,128]{2,1,0:T(2,128)S(1)}, u32[]{:S(2)}, u32[]{:S(2)}) collective-permute-start(f32[1,2,128]{2,1,0:T(2,128)S(1)} %get-tuple-element.34), channel_id=1, source_target_pairs={{0,8},{4,12},{8,0},{12,4},{1,9},{5,13},{9,1},{13,5},{2,10},{6,14},... | collective-permute-start | bytes 3080 | tf_op jit(solution)/shard_map/ppermute | solution.py:354
  25.4 1.6 %collective-permute-start.7 = (bf16[2,96,384]{2,1,0:T(8,128)(2,1)S(1)}, bf16[2,96,384]{2,1,0:T(8,128)(2,1)S(1)}, u32[]{:S(2)}, u32[]{:S(2)}) collective-permute-start(bf16[2,96,384]{2,1,0:T(8,128)(2,1)S(1)} %get-tuple-element.38), channel_id=1, source_target_pairs={{0,1},{1,0},{2,3},{3,2},{4,5},{5,4},{6,7},{7,6},{8,9},{9,8},{10,11... | collective-permute-start | bytes 442376 | tf_op jit(solution)/shard_map/ppermute | solution.py:354
  25.8 1.4 %collective-permute-start.8 = (bf16[2,96,384]{2,1,0:T(8,128)(2,1)S(1)}, bf16[2,96,384]{2,1,0:T(8,128)(2,1)S(1)}, u32[]{:S(2)}, u32[]{:S(2)}) collective-permute-start(bf16[2,96,384]{2,1,0:T(8,128)(2,1)S(1)} %get-tuple-element.40), channel_id=1, source_target_pairs={{0,1},{1,0},{2,3},{3,2},{4,5},{5,4},{6,7},{7,6},{8,9},{9,8},{10,11... | collective-permute-start | bytes 442376 | tf_op jit(solution)/shard_map/ppermute | solution.py:354
